TPU v7x, 256 devices: a whole 4x4x8 slice. The times are simulated.
256 devices in a mesh: dp: 4 (over x), ctx: 64 (over z, y, core).
Axes of the slice: x: 4, y: 4, z: 8, core: 2. Of those that a mesh axis runs over, the one named last changes fastest.
Arguments:
- queries: bfloat16 [4, 8192, 1024], P('dp', 'ctx'), may hold values from -240 to 240
- keys: bfloat16 [4, 8192, 128], P('dp', 'ctx'), may hold values from -5 to 5
- values: bfloat16 [4, 8192, 128], P('dp', 'ctx'), may hold values from -6 to 6
- query_map: bfloat16 [8, 128, 64], replicated, may hold values from -0.5 to 0.5
- key_map: bfloat16 [8, 128, 64], replicated, may hold values from -0.5 to 0.5
- documents: int32 [4, 64], P('dp'), may hold values from 0 to 15, never falling along the last dimension, each value on 1 to 16 neighbouring positions
- assignment: int32 [4, 64, 64], P('dp'), may hold values from 0 to 63, each once within a row
Outputs:
- teacher_relaid: bfloat16 [4, 8192, 1024], P('dp', 'ctx')
- difference: float32 [4, 8192, 1024], P('dp', 'ctx')
- feature_grad: float32 [8, 128, 64], replicated
Inputs may be any that keep to these rules, and one draw needn't show every extreme that they name: `documents`: document numbers never fall along a row; each document covers 1 to 16 blocks, and one covers exactly 16. For every row r and shard d, assignment[r, d, :] is a permutation: piece i of shard d goes to context shard assignment[r, d, i], so every shard receives one piece from every shard.
All inputs are finite; a program needn't handle non-finite values.
Results may differ from a plain program's by a relative error of at most 0.015.
Values may be sent and summed in bfloat16 or wider, within the bound.
No kernel may reach another device: no remote copies, remote signals or barrier semaphores. Data moves between devices by JAX's collectives and lax.ppermute only.
A program may use at most 192 MiB of HBM per device.

v0:
```python
import math

import jax
import jax.numpy as jnp
from jax import lax
from jax.sharding import PartitionSpec as P

HEAD_DIM = 128
WINDOW = 64
BLOCK = 128


HIGHEST = lax.Precision.HIGHEST
NEGATIVE = -1e30


def prefix(array, axis, combine, identity):
    peers, position = (lax.axis_size(axis), lax.axis_index(axis))
    everything = jax.tree.map(
        lambda part, kind: lax.all_gather(part.astype(kind), axis),
        array,
        (jnp.bfloat16, jnp.bfloat16, jnp.bfloat16),
    )
    start = jax.tree.map(
        lambda part, zero: jnp.broadcast_to(jnp.asarray(zero, part.dtype), part.shape),
        array,
        identity,
    )

    def lap(k, before):
        reached = k < position
        new = combine(
            before, jax.tree.map(lambda part, own: part[k].astype(own.dtype), everything, array)
        )
        return jax.tree.map(lambda a, b: jnp.where(reached, a, b), new, before)

    return lax.fori_loop(0, peers, lap, start)


def feature_map(logits):
    return jnp.concatenate(
        [jax.nn.softmax(logits, axis=-1), jax.nn.softmax(-logits, axis=-1)], axis=-1
    )


def lookup_documents(positions, doc_row):
    block_ids = jnp.arange(doc_row.shape[0], dtype=jnp.int32)
    match = positions[:, None] // BLOCK == block_ids[None, :]
    return jnp.sum(jnp.where(match, doc_row[None, :], 0), axis=1)


def block_output(query_block, key_block, value_block, phi_block, lin_state, lin_norm):
    scores = jnp.einsum(
        "qhe,ke->hqk", query_block, key_block, preferred_element_type=jnp.float32
    ) / math.sqrt(HEAD_DIM)
    rows_here = key_block.shape[0]
    causal = jnp.arange(rows_here)[:, None] >= jnp.arange(rows_here)[None, :]
    scores = jnp.where(causal[None], scores, -jnp.inf)
    window_max = jnp.max(scores, axis=-1, keepdims=True)
    weights = jnp.exp(scores - window_max)
    near_sum = jnp.einsum("hqk,ke->qhe", weights, value_block, precision=HIGHEST)
    near_total = jnp.transpose(jnp.sum(weights, axis=-1))
    far_sum = jnp.einsum("qhf,hfe->qhe", phi_block, lin_state, precision=HIGHEST)
    far_total = jnp.einsum("qhf,hf->qh", phi_block, lin_norm, precision=HIGHEST)
    return (near_sum + far_sum) / (near_total + far_total)[:, :, None]


def attend(query_rows, query_pos, query_docs, keys, values, doc_row):
    tokens = query_rows.shape[0]
    head_count = query_rows.shape[1]
    running_max = jnp.full((head_count, tokens), NEGATIVE, jnp.float32)
    key_part = lax.all_gather(keys, "ctx", axis=1, tiled=True)[0]
    value_part = lax.all_gather(values, "ctx", axis=1, tiled=True)[0]
    key_count = key_part.shape[0]
    key_pos = jnp.arange(key_count, dtype=jnp.int32)
    key_docs = lookup_documents(key_pos, doc_row)
    scores = jnp.einsum(
        "qhe,ke->hqk", query_rows, key_part, preferred_element_type=jnp.float32
    ) / math.sqrt(HEAD_DIM)
    allowed = (query_docs[:, None] == key_docs[None, :]) & (query_pos[:, None] >= key_pos[None, :])
    scores = jnp.where(allowed[None], scores, -jnp.inf)
    new_max = jnp.maximum(running_max, jnp.max(scores, axis=-1))
    weights = jnp.exp(scores - new_max[:, :, None])
    denominator = jnp.sum(weights, axis=-1)
    weighted = jnp.einsum(
        "hqk,ke->qhe", weights.astype(jnp.bfloat16), value_part, preferred_element_type=jnp.float32
    )
    result = (new_max, denominator, weighted)
    running_max, denominator, weighted = result
    return (
        (weighted / jnp.transpose(denominator)[:, :, None])
        .astype(jnp.bfloat16)
        .reshape(tokens, head_count * HEAD_DIM)
    )


def on_device(queries, keys, values, query_map, key_map, documents, assignment):
    shards = lax.axis_size("ctx")
    device = lax.axis_index("ctx")
    tokens = queries.shape[1]
    columns = queries.shape[2]
    head_count = columns // HEAD_DIM
    piece_len = tokens // shards
    anchor = device * tokens
    doc_row = documents[0]
    local_pos = anchor + jnp.arange(tokens, dtype=jnp.int32)
    local_docs = lookup_documents(local_pos, doc_row)
    slot_ids = jnp.arange(shards, dtype=jnp.int32)
    routes = assignment[0]
    targets = lax.dynamic_index_in_dim(routes, device, 0, keepdims=False)
    placing = (targets[None, :] == slot_ids[:, None]).astype(jnp.bfloat16)
    pieces = queries[0].reshape(shards, piece_len, columns)
    outgoing = jnp.einsum(
        "sj,jpc->spc", placing, pieces, preferred_element_type=jnp.float32
    ).astype(jnp.bfloat16)
    arrived = lax.all_to_all(outgoing, "ctx", split_axis=0, concat_axis=0, tiled=True)
    chosen = jnp.sum(jnp.where(routes == device, slot_ids[None, :], 0), axis=1)
    arrived_pos = (
        (slot_ids * tokens + chosen * piece_len)[:, None]
        + jnp.arange(piece_len, dtype=jnp.int32)[None, :]
    ).reshape(tokens)
    arrived_docs = lookup_documents(arrived_pos, doc_row)
    arrived_query = arrived.reshape(tokens, head_count, HEAD_DIM)
    teacher = attend(arrived_query, arrived_pos, arrived_docs, keys, values, doc_row)
    returned = lax.all_to_all(
        teacher.reshape(shards, piece_len, columns), "ctx", split_axis=0, concat_axis=0, tiled=True
    )
    target = jnp.einsum(
        "sj,spc->jpc", placing, returned, preferred_element_type=jnp.float32
    ).reshape(tokens, columns)
    query_float = queries[0].astype(jnp.float32).reshape(tokens, head_count, HEAD_DIM)
    value_float = values[0].astype(jnp.float32)
    key_features = feature_map(
        jnp.einsum("se,hef->shf", keys[0], key_map, preferred_element_type=jnp.float32)
    )
    doubled = key_features.shape[-1]
    before = jnp.where(device > 0, lookup_documents(jnp.reshape(anchor - 1, (1,)), doc_row)[0], -1)
    last_doc = local_docs[tokens - 1]
    member = (local_docs == last_doc).astype(jnp.float32)
    masked_features = key_features * member[:, None, None]
    summary_state = jnp.einsum("shf,se->hfe", masked_features, value_float, precision=HIGHEST)
    summary_norm = jnp.sum(masked_features, axis=0)
    summary_flag = (last_doc != before).astype(jnp.float32)

    def link_summaries(earlier, later):
        carry_on = 1.0 - later[2]
        return (
            later[0] + carry_on * earlier[0],
            later[1] + carry_on * earlier[1],
            jnp.maximum(earlier[2], later[2]),
        )

    identity = (
        jnp.zeros_like(summary_state),
        jnp.zeros_like(summary_norm),
        jnp.zeros((), jnp.float32),
    )
    incoming = prefix((summary_state, summary_norm, summary_flag), "ctx", link_summaries, identity)
    windows = tokens // WINDOW
    query_blocks = queries[0].reshape(windows, WINDOW, head_count, HEAD_DIM)
    key_blocks = keys[0].reshape(windows, WINDOW, HEAD_DIM)

    def student_of(map_float):
        query_features = feature_map(
            jnp.einsum("she,hef->shf", query_float, map_float, precision=HIGHEST)
        )
        blocks = (
            query_blocks,
            key_blocks,
            value_float.reshape(windows, WINDOW, HEAD_DIM),
            query_features.reshape(windows, WINDOW, head_count, doubled),
            key_features.reshape(windows, WINDOW, head_count, doubled),
            local_docs.reshape(windows, WINDOW)[:, 0],
        )

        def advance(running, inputs):
            lin_state, lin_norm, prior_doc = running
            query_block, key_block, value_block, phi_block, psi_block, doc_now = inputs
            retain = (doc_now == prior_doc).astype(jnp.float32)
            lin_state = lin_state * retain
            lin_norm = lin_norm * retain
            output = block_output(
                query_block, key_block, value_block, phi_block, lin_state, lin_norm
            )
            lin_state = lin_state + jnp.einsum(
                "whf,we->hfe", psi_block, value_block, precision=HIGHEST
            )
            lin_norm = lin_norm + jnp.sum(psi_block, axis=0)
            return ((lin_state, lin_norm, doc_now), output)

        initial = (incoming[0], incoming[1], before)
        unused_state, outputs = lax.scan(advance, initial, blocks)
        return outputs.reshape(tokens, columns)

    loss_scale = HEAD_DIM / math.sqrt(lax.axis_size("dp") * tokens * shards)

    def loss_of(map_float):
        gap = student_of(map_float) - target
        return (jnp.sum(gap * gap) * loss_scale, gap)

    total_loss, pullback, difference = jax.vjp(loss_of, query_map.astype(jnp.float32), has_aux=True)
    local_grad = pullback(jnp.ones((), jnp.float32))[0]
    feature_grad = lax.psum(local_grad, ("dp", "ctx"))
    return (
        teacher.reshape(1, tokens, columns),
        difference.reshape(1, tokens, columns),
        feature_grad,
    )


def solution(mesh):
    return jax.shard_map(
        on_device,
        mesh=mesh,
        in_specs=(
            P("dp", "ctx", None),
            P("dp", "ctx", None),
            P("dp", "ctx", None),
            P(),
            P(),
            P("dp", None),
            P("dp", None, None),
        ),
        out_specs=(P("dp", "ctx", None), P("dp", "ctx", None), P()),
        check_vma=False,
    )
```

profile of v0, /device:TPU:1, one launch (start us, length us, event | category | flops | bytes accessed | tf_op | source)
XLA Modules:
  0.0 868.2 jit_solution(16581985411671954092)
XLA Ops:
  8.0 1.5 copy.75
  14.9 1.8 convolution_convert_fusion
  19.8 13.2 %all-to-all-start = ((bf16[64,2,1024]{2,1,0:T(2,128)(2,1)}), bf16[64,2,1024]{2,1,0:T(2,128)(2,1)S(1)}, u32[]{:S(2)}, u32[]{:S(2)}) async-start(bf16[64,2,1024]{2,1,0:T(2,128)(2,1)} %copy.73), calls=%async_computation | async-start | bytes 524288 | tf_op jit(solution)/shard_map/all_to_all | solution.py:116
  38.6 1.3 fusion.105
  40.8 5.5 all-to-all-done
  46.5 46.8 %all-gather.6.cloned.1.call-done = bf16[1,8192,128]{2,1,0:T(8,128)(2,1)} async-done(((bf16[1,128,128]{2,1,0:T(8,128)(2,1)}), bf16[1,8192,128]{2,1,0:T(8,128)(2,1)}) %all-gather.6.cloned.1.call-update) | async-done | bytes 2097168 | tf_op jit(solution)/shard_map/all_gather | solution.py:72
  93.3 15.4 %bitcast_reduce_fusion = (f32[8,128]{1,0:T(8,128)S(1)}, f32[128,8,8192]{2,0,1:T(8,128)}) fusion(pred[128,8192]{1,0:T(8,128)(4,1)S(1)} %fusion.39, bf16[1,8192,128]{2,1,0:T(8,128)(2,1)} %all-gather.6.cloned.1.call-done, bf16[128,8,128]{2,1,0:T(8,128)(2,1)S(1)} %reshape.367), kind=kOutput, calls=%fused_computation.64 | convolution fusion | flops 2172648448 | bytes 36966400 | tf_op jit(solution)/shard_map/qhe,ke->hqk/dot_general | solution.py:77
  108.7 15.3 %fusion.34 = f32[8,128]{1,0:T(8,128)S(1)} fusion(f32[128,8,8192]{2,0,1:T(8,128)} %get-tuple-element.695, f32[8,128]{1,0:T(8,128)S(1)} %broadcast_maximum_fusion, pred[128,8192]{1,0:T(8,128)(4,1)S(1)} %fusion.39), kind=kLoop, calls=%fused_computation.67 | loop fusion | flops 33553408 | bytes 34611200 | tf_op jit(solution)/shard_map/reduce_sum | solution.py:84
  124.1 42.6 %all-gather.8.cloned.1.call-done = bf16[1,8192,128]{1,2,0:T(8,128)(2,1)} async-done(((bf16[1,128,128]{1,2,0:T(8,128)(2,1)}), bf16[1,8192,128]{1,2,0:T(8,128)(2,1)}) %all-gather.8.cloned.1.call-update) | async-done | bytes 2097168 | tf_op jit(solution)/shard_map/all_gather | solution.py:73
  166.7 15.4 %fusion.61 = bf16[128,8,128]{0,2,1:T(8,128)(2,1)S(1)} fusion(bf16[1,8192,128]{1,2,0:T(8,128)(2,1)} %all-gather.8.cloned.1.call-done, f32[128,8,8192]{2,0,1:T(8,128)} %get-tuple-element.695, f32[8,128]{1,0:T(8,128)S(1)} %broadcast_maximum_fusion, pred[128,8192]{1,0:T(8,128)(4,1)S(1)} %fusion.39, f32[128,8]{0,1:T(8,128)S(1)} %bitcast.278), kind=kOutput, calls=%fused_computation.92 | convolution fusion | flops 2181300224 | bytes 36970496 | tf_op jit(solution)/shard_map/hqk,ke->qhe/dot_general | solution.py:85
  183.0 7.9 all-to-all-start.1
  195.4 125.7 %all-reduce = bf16[64]{0:T(256)(128)(2,1)} all-reduce(bf16[64]{0:T(256)(128)(2,1)S(1)} %dynamic-update-slice), channel_id=1, replica_groups=mesh['dp'=4,'ctx'=64] {'ctx'}, use_global_device_ids=true, to_apply=%add | all-reduce | flops 64 | bytes 256
  321.1 52.1 %all-gather.1 = bf16[512,128]{1,0:T(8,128)(2,1)S(1)} all-gather(bf16[8,128]{1,0:T(8,128)(2,1)} %get-tuple-element.693), channel_id=3, replica_groups=mesh['dp'=4,'ctx'=64] {'ctx'}, dimensions={0}, use_global_device_ids=true | all-gather | bytes 133120 | tf_op jit(solution)/shard_map/all_gather | solution.py:20
  373.2 1.3 multiply_divide_fusion
  377.6 203.8 %while.60 = (s32[]{:T(128)}, f32[8,128,128]{2,1,0:T(8,128)S(1)}, f32[8,128]{1,0:T(8,128)S(1)}, s32[]{:T(128)}, bf16[64,8,128,128]{3,2,1,0:T(8,128)(2,1)}, /*inde...) while((s32[]{:T(128)}, f32[8,128,128]{2,1,0:T(8,128)S(1)}, ...), condition=%wide.region_13.14_spmd.clone, body=%wide.region_12.13_spmd.clone.sunk | while | flops 660485 | bytes 1321125 | solution.py:37
  379.5 1.3 fusion.146
  382.7 1.3 fusion.146
  385.9 1.3 fusion.146
  389.1 1.3 fusion.146
  392.2 1.3 fusion.146
  395.4 1.3 fusion.146
  398.6 1.3 fusion.146
  401.8 1.3 fusion.146
  405.0 1.3 fusion.146
  408.2 1.3 fusion.146
  411.3 1.3 fusion.146
  414.5 1.3 fusion.146
  417.7 1.3 fusion.146
  420.9 1.3 fusion.146
  424.1 1.3 fusion.146
  427.3 1.3 fusion.146
  430.5 1.3 fusion.146
  433.6 1.3 fusion.146
  436.8 1.3 fusion.146
  440.0 1.3 fusion.146
  443.2 1.3 fusion.146
  446.4 1.3 fusion.146
  449.6 1.3 fusion.146
  452.7 1.3 fusion.146
  455.9 1.3 fusion.146
  459.1 1.3 fusion.146
  462.3 1.3 fusion.146
  465.5 1.3 fusion.146
  468.7 1.3 fusion.146
  471.8 1.3 fusion.146
  475.0 1.3 fusion.146
  478.2 1.3 fusion.146
  481.4 1.3 fusion.146
  484.6 1.3 fusion.146
  491.0 1.3 fusion.146
  538.7 1.3 fusion.146
  545.1 1.3 fusion.146
  551.5 1.3 fusion.146
  581.5 20.5 %while.59 = (s32[]{:T(128)}, f32[8,128,128]{2,1,0:T(8,128)S(1)}, f32[8,128]{1,0:T(8,128)S(1)}, s32[]{:T(128)}, f32[2,64,8,128]{3,2,1,0:T(8,128)S(1)}, /*index=5*...) while((s32[]{:T(128)}, f32[8,128,128]{2,1,0:T(8,128)S(1)}, ...), condition=%wide.region_22.23_spmd.clone, body=%wide.region_18.22_spmd.clone.sunk | while | flops 261752320 | bytes 7485703 | solution.py:192
  585.0 1.4 convolution_bitcast_fusion.5
  589.2 1.9 convolution_add_fusion.3
  595.2 1.4 convolution_bitcast_fusion.5
  599.4 1.9 convolution_add_fusion.3
  603.2 8.1 while.58
  604.9 2.2 fusion.138
  609.0 2.2 fusion.138
  613.3 1.8 copy.93
  616.4 243.6 %all-reduce.3.cloned.1.call-done = f32[8,128,64]{1,2,0:T(8,128)} async-done(((f32[8,128,64]{1,2,0:T(8,128)}), f32[8,128,64]{1,2,0:T(8,128)}) %all-reduce.3.cloned.1.call-update) | async-done | bytes 262160 | tf_op jit(solution)/shard_map/psum | solution.py:203
  859.9 1.7 copy.221
  (294 shorter events, 153.4 us)
Async XLA Ops:
  7.2 4.8 copy-start
  7.2 86.1 %all-gather.6.cloned.1.call-start = ((), (), s32[]{:S(2)}) async-start(), calls=%async_computation.2 | async-start | bytes 2129920 | tf_op jit(solution)/shard_map/all_gather | solution.py:72
  7.9 158.7 %all-gather.8.cloned.1.call-start = ((), (), s32[]{:S(2)}) async-start(), calls=%async_computation.3 | async-start | bytes 2129920 | tf_op jit(solution)/shard_map/all_gather | solution.py:73
  9.5 368.2 %all-gather.10.cloned.1.call-start = ((), (), s32[]{:S(2)}) async-start(), calls=%async_computation.5 | async-start | bytes 17039360 | tf_op jit(solution)/shard_map/all_gather | solution.py:20
  18.5 14.5 %copy-start.12 = (s32[64]{0:T(128)}, s32[64]{0:T(128)S(1)}, u32[]{:S(2)}) copy-start(s32[64]{0:T(128)S(1)} %dynamic-slice_bitcast_fusion.3) | copy-start | bytes 772
  19.8 26.5 %all-to-all-start = ((bf16[64,2,1024]{2,1,0:T(2,128)(2,1)}), bf16[64,2,1024]{2,1,0:T(2,128)(2,1)S(1)}, u32[]{:S(2)}, u32[]{:S(2)}) async-start(bf16[64,2,1024]{2,1,0:T(2,128)(2,1)} %copy.73), calls=%async_computation | async-start | bytes 524288 | tf_op jit(solution)/shard_map/all_to_all | solution.py:116
  36.6 0.7 copy-start.2
  37.0 0.7 copy-start.4
  37.0 71.7 %copy-start.8 = (f32[128,8]{0,1:T(8,128)}, f32[128,8]{0,1:T(8,128)S(1)}, u32[]{:S(2)}) copy-start(f32[128,8]{0,1:T(8,128)S(1)} %get-tuple-element.702) | copy-start | bytes 12292
  166.7 26.5 %copy-start.7 = (bf16[1,128,128]{2,1,0:T(8,128)(2,1)S(1)}, bf16[1,128,128]{2,1,0:T(8,128)(2,1)}, u32[]{:S(2)}) copy-start(bf16[1,128,128]{2,1,0:T(8,128)(2,1)} %param.15) | copy-start | bytes 98308
  166.7 27.4 %copy-start.13 = (u32[256]{0:T(256)S(1)}, u32[256]{0:T(256)}, u32[]{:S(2)}) copy-start(u32[256]{0:T(256)} %constant.224) | copy-start | bytes 3076
  182.0 193.1 %copy-start.6 = (bf16[128,8,128]{0,2,1:T(8,128)(2,1)}, bf16[128,8,128]{0,2,1:T(8,128)(2,1)S(1)}, u32[]{:S(2)}) copy-start(bf16[128,8,128]{0,2,1:T(8,128)(2,1)S(1)} %fusion.61) | copy-start | bytes 786436
  183.0 192.1 %all-to-all-start.1 = ((bf16[64,2,1024]{2,1,0:T(2,128)(2,1)}), bf16[64,2,1024]{2,1,0:T(2,128)(2,1)S(1)}, u32[]{:S(2)}, u32[]{:S(2)}) async-start(bf16[64,2,1024]{2,1,0:T(2,128)(2,1)} %reshape_reshape.7), calls=%async_computation.1 | async-start | bytes 524288 | tf_op jit(solution)/shard_map/all_to_all | solution.py:125
  190.9 669.0 %all-reduce.3.cloned.1.call-start = ((), (), s32[]{:S(2)}) async-start(), calls=%async_computation.4 | async-start | bytes 524288 | tf_op jit(solution)/shard_map/psum | solution.py:203
  601.9 10.1 %copy-start.5 = (f32[128,8,64]{0,2,1:T(8,128)S(1)}, f32[128,8,64]{0,2,1:T(8,128)}, u32[]{:S(2)}) copy-start(f32[128,8,64]{0,2,1:T(8,128)} %copy-done.4) | copy-start | bytes 786436
  601.9 10.1 %copy-start.11 = (f32[128,8]{0,1:T(8,128)S(1)}, f32[128,8]{0,1:T(8,128)}, u32[]{:S(2)}) copy-start(f32[128,8]{0,1:T(8,128)} %multiply_divide_fusion) | copy-start | bytes 12292
  602.0 10.1 %copy-start.3 = (f32[128,8,64]{0,2,1:T(8,128)S(1)}, f32[128,8,64]{0,2,1:T(8,128)}, u32[]{:S(2)}) copy-start(f32[128,8,64]{0,2,1:T(8,128)} %copy-done.2) | copy-start | bytes 786436
  602.0 10.1 %copy-start.10 = (f32[128,8]{0,1:T(8,128)S(1)}, f32[128,8]{0,1:T(8,128)}, u32[]{:S(2)}) copy-start(f32[128,8]{0,1:T(8,128)} %multiply_divide_fusion.1) | copy-start | bytes 12292
  602.0 10.2 %copy-start.9 = (f32[128,8]{0,1:T(8,128)S(1)}, f32[128,8]{0,1:T(8,128)}, u32[]{:S(2)}) copy-start(f32[128,8]{0,1:T(8,128)} %copy-done.8) | copy-start | bytes 12292
  602.0 259.6 %copy-start.1 = (bf16[8,128,64]{1,2,0:T(8,128)(2,1)S(1)}, bf16[8,128,64]{1,2,0:T(8,128)(2,1)}, u32[]{:S(2)}) copy-start(bf16[8,128,64]{1,2,0:T(8,128)(2,1)} %param.17) | copy-start | bytes 393220
Sparse Core Ops, SparseCore 0:
  10.8 82.4 all-gather.5
  96.5 70.1 all-gather.7
  170.0 101.2 all-gather.9
  613.4 246.4 all-reduce.2
where the time goes:
time: 874 us; the launch traced here: 868 us
  waiting for transfers between devices  339 us (39%)
  blocking collectives  178 us (20%)
  other arithmetic  116 us (13%)
  local copies, waits for them, and re-layouts  98.4 us (11%)
  matrix products  53.3 us (6%)
  loops' own time  46.7 us (5%)
  starting transfers between devices  21.4 us (2%)
  between operations  15.4 us (2%)
    psum x1, waiting for transfers between devices, on_device(): feature_grad = lax.psum(local_grad, ('dp', 'ctx'))  244 us
    unnamed x1, blocking collectives  126 us
    select_n x128, other arithmetic, lap(): return jax.tree.map(lambda a, b: jnp.where(reached, a, b), new, before)  83.1 us
    dynamic_slice x64, local copies, waits for them, and re-layouts, lap(): part[k].astype(own.dtype)  76.5 us
    all_gather x1, blocking collectives, prefix(): lax.all_gather(part.astype(kind), axis)  52.1 us
    all_gather x1, waiting for transfers between devices, attend(): key_part = lax.all_gather(keys, 'ctx', axis=1, tiled=True)[0]  46.8 us
    another operation x1, loops' own time, prefix(): return lax.fori_loop(0, peers, lap, start)  44.2 us
    all_gather x1, waiting for transfers between devices, attend(): value_part = lax.all_gather(values, 'ctx', axis=1, tiled=True)[0]  42.6 us
  transfers between devices with their start and end apart: 6, of which 4 were waited for; matrix products, arithmetic and copies ran while one was open for 9% of the time, Pallas kernels for 0%

commit v1 on v0

v1 whole, which is shorter than its diff:
```python
import functools
import math

import jax
import jax.numpy as jnp
import numpy as np
from jax import lax
from jax.experimental import pallas as pl
from jax.experimental.pallas import tpu as pltpu
from jax.sharding import Mesh, PartitionSpec as P

HEAD_DIM = 128
WINDOW = 64
BLOCK = 128
HEADS = 8
FEATURES = 64
ROWS = HEADS * BLOCK
CHUNK = 2 * BLOCK
CHUNKS = 8
FAR = CHUNK * CHUNKS
SCALE = math.log2(math.e) / math.sqrt(HEAD_DIM)
NEGATIVE = -1e30
NT = (((1,), (1,)), ((), ()))
NN = (((1,), (0,)), ((), ()))
F32 = jnp.float32
BF16 = jnp.bfloat16
LOG2E = math.log2(math.e)


def dot(a, b, dims=NN):
    return lax.dot_general(a, b, dims, preferred_element_type=F32)


def two_softmax(u):
    u = u * LOG2E
    top = jnp.max(u, axis=1, keepdims=True)
    low = jnp.min(u, axis=1, keepdims=True)
    up = jnp.exp2(u - top)
    down = jnp.exp2(low - u)
    up = up * (1.0 / jnp.sum(up, axis=1, keepdims=True))
    down = down * (1.0 / jnp.sum(down, axis=1, keepdims=True))
    return jnp.concatenate([up, down], axis=1)


def main_kernel(
    loss_scale,
    pos_ref,
    doc_ref,
    q_ref,
    k_ref,
    v_ref,
    a_ref,
    b_ref,
    qm_ref,
    km_ref,
    row_ref,
    diff_ref,
    buf_ref,
    qs,
    s_scr,
    p_scr,
    w_scr,
    psi_scr,
    vp_scr,
    phi_scr,
):
    here = pos_ref[0]
    z = lax.shift_right_logical(here, 3)
    y = lax.shift_right_logical(here, 1) & 3
    c = here & 1
    doc = doc_ref[here]

    def valid(chunk, k):
        yy = chunk % 4
        cc = c if chunk < 4 else 1 - c
        if k == 0:
            back = jnp.where(yy < y, 0, jnp.where(yy > y, 1, 2 * cc))
        else:
            back = jnp.where(yy > y, 2, 1)
        g = (z - back) * 8 + yy * 2 + cc
        inside = (g >= 0) & (g < here) & (g > here - 16)
        return inside & (doc_ref[jnp.maximum(g, 0)] == doc)

    for h in range(HEADS):
        qs[h * BLOCK : (h + 1) * BLOCK, :] = q_ref[:, h * BLOCK : (h + 1) * BLOCK]

    key_own = k_ref[...]
    tile = 256
    lane = lax.broadcasted_iota(jnp.int32, (1, CHUNK), 1)
    col = lax.broadcasted_iota(jnp.int32, (tile, BLOCK), 1)
    row = lax.broadcasted_iota(jnp.int32, (tile, BLOCK), 0) % BLOCK
    causal = col <= row
    near = causal & ((col < WINDOW) == (row < WINDOW))
    biases = []
    key_chunks = []
    for i in range(CHUNKS):
        src = a_ref if i < 4 else b_ref
        ok = [valid(i, 0), valid(i, 1)]
        biases.append(
            jnp.where(
                lane < BLOCK,
                jnp.where(ok[0], 0.0, NEGATIVE),
                jnp.where(ok[1], 0.0, NEGATIVE),
            )
        )
        for k in range(2):
            at = i * CHUNK + k * BLOCK
            value = src[i % 4, k, BLOCK:, :]
            one = jnp.where(ok[k], 1.0, 0.0).astype(BF16)
            vp_scr[at : at + BLOCK, :BLOCK] = value * one
            vp_scr[at : at + BLOCK, BLOCK:] = jnp.ones((BLOCK, BLOCK), BF16) * one
    vp_scr[FAR:, :BLOCK] = v_ref[...]
    vp_scr[FAR:, BLOCK:] = jnp.ones((BLOCK, BLOCK), BF16)
    for r in range(ROWS // tile):
        at = r * tile
        query = qs[at : at + tile, :]
        diag = dot(query, key_own, NT) * SCALE
        own = jnp.where(causal, diag, NEGATIVE)
        top = own
        for i in range(CHUNKS):
            src = a_ref if i < 4 else b_ref
            keys = jnp.concatenate([src[i % 4, 0, :BLOCK, :], src[i % 4, 1, :BLOCK, :]], axis=0)
            s = dot(query, keys, NT) * SCALE + biases[i]
            s_scr[at : at + tile, i * CHUNK : (i + 1) * CHUNK] = s
            top = jnp.maximum(top, jnp.maximum(s[:, :BLOCK], s[:, BLOCK:]))
        top = jnp.max(top, axis=1, keepdims=True)
        p_scr[at : at + tile, FAR:] = jnp.exp2(own - top).astype(BF16)
        for i in range(CHUNKS):
            s = s_scr[at : at + tile, i * CHUNK : (i + 1) * CHUNK]
            p_scr[at : at + tile, i * CHUNK : (i + 1) * CHUNK] = jnp.exp2(s - top).astype(BF16)
        window = jnp.where(near, diag, NEGATIVE)
        window_top = jnp.max(window, axis=1, keepdims=True)
        w_scr[at : at + tile, :] = jnp.exp2(window - window_top).astype(BF16)

    for i in range(CHUNKS):
        src = a_ref if i < 4 else b_ref
        keys = jnp.concatenate([src[i % 4, 0, :BLOCK, :], src[i % 4, 1, :BLOCK, :]], axis=0)
        u = dot(km_ref[...], keys, NT).reshape(HEADS, FEATURES, CHUNK)
        psi_scr[:, i * CHUNK : (i + 1) * CHUNK] = (
            two_softmax(u).reshape(ROWS, CHUNK).astype(BF16)
        )
    u = dot(km_ref[...], key_own, NT).reshape(HEADS, FEATURES, BLOCK)
    psi_own = two_softmax(u).reshape(ROWS, BLOCK).astype(BF16)

    value_own = vp_scr[FAR:, :]
    early = lax.broadcasted_iota(jnp.int32, (BLOCK, CHUNK), 0) < WINDOW
    value_early = jnp.where(early, value_own.astype(F32), 0.0).astype(BF16)

    mixed = dot(p_scr[...], vp_scr[...])
    state = dot(psi_scr[...], vp_scr[:FAR, :])
    state_late = state + dot(psi_own, value_early)
    local = dot(w_scr[...], value_own)
    state = state.astype(BF16)
    state_late = state_late.astype(BF16)

    first_half = lax.broadcasted_iota(jnp.int32, (BLOCK, BLOCK), 1) < WINDOW
    dest = (lax.broadcasted_iota(jnp.int32, (BLOCK, BLOCK), 0) == row_ref[...]).astype(BF16)
    for h in range(HEADS):
        at = h * BLOCK
        query = qs[at : at + BLOCK, :]
        u = dot(qm_ref[h * FEATURES : (h + 1) * FEATURES, :], query, NT)
        phi = two_softmax(u[None])[0]
        phi_both = jnp.concatenate(
            [jnp.where(first_half, phi, 0.0), jnp.where(first_half, 0.0, phi)], axis=0
        )
        states = jnp.concatenate([state[at : at + BLOCK], state_late[at : at + BLOCK]], axis=0)
        far = dot(phi_both.T.astype(BF16), states)
        total = far + local[at : at + BLOCK]
        inverse = 1.0 / total[:, BLOCK:]
        student = total[:, :BLOCK] * inverse
        teacher = (mixed[at : at + BLOCK, :BLOCK] / mixed[at : at + BLOCK, BLOCK:]).astype(BF16)
        gap = student - teacher.astype(F32)
        diff_ref[:, at : at + BLOCK] = gap
        moved = dot(dest, teacher).astype(BF16)
        for s in range(8):
            buf_ref[s, :, at : at + BLOCK] = moved[s * 16 : (s + 1) * 16, :]
        grad_out = gap * inverse * (2.0 * loss_scale)
        grad_both = jnp.concatenate([grad_out, -grad_out * student], axis=1).astype(BF16)
        dphi = dot(states, grad_both, NT)
        dphi = jnp.where(first_half, dphi[:BLOCK], dphi[BLOCK:])
        part = phi * dphi
        up, down = phi[:FEATURES], phi[FEATURES:]
        du = (
            part[:FEATURES]
            - part[FEATURES:]
            - up * jnp.sum(part[:FEATURES], axis=0, keepdims=True)
            + down * jnp.sum(part[FEATURES:], axis=0, keepdims=True)
        )
        grad = dot(du.astype(BF16), query).astype(BF16)
        for s in range(4):
            lanes = 1024 + s * BLOCK
            buf_ref[h, :, lanes : lanes + BLOCK] = grad[s * 16 : (s + 1) * 16, :]


def main_call(loss_scale, pos, doc, q, k, v, a, b, qm, km, row):
    vmem = pl.BlockSpec(memory_space=pltpu.VMEM)
    smem = pl.BlockSpec(memory_space=pltpu.SMEM)
    return pl.pallas_call(
        functools.partial(main_kernel, loss_scale),
        out_shape=(
            jax.ShapeDtypeStruct((BLOCK, HEADS * HEAD_DIM), F32),
            jax.ShapeDtypeStruct((8, 16, 1536), BF16),
        ),
        in_specs=[smem, smem] + [vmem] * 8,
        out_specs=(vmem, vmem),
        scratch_shapes=[
            pltpu.VMEM((ROWS, BLOCK), BF16),
            pltpu.VMEM((ROWS, FAR), F32),
            pltpu.VMEM((ROWS, FAR + BLOCK), BF16),
            pltpu.VMEM((ROWS, BLOCK), BF16),
            pltpu.VMEM((ROWS, FAR), BF16),
            pltpu.VMEM((FAR + BLOCK, CHUNK), BF16),
            pltpu.VMEM((BLOCK, BLOCK), F32),
        ],
        compiler_params=pltpu.CompilerParams(vmem_limit_bytes=48 * 1024 * 1024),
        cost_estimate=pl.CostEstimate(
            flops=3_000_000_000, bytes_accessed=3_000_000, transcendentals=4_000_000
        ),
        name="transfer",
    )(pos, doc, q, k, v, a, b, qm, km, row)


def on_device(queries, keys, values, query_map, key_map, documents, assignment):
    z, y, c = lax.axis_index("z"), lax.axis_index("y"), lax.axis_index("c")
    device = (z * 4 + y) * 2 + c
    kv = jnp.concatenate([keys[0], values[0]], axis=0)
    plane1 = lax.ppermute(kv, "z", [(i, (i + 1) % 8) for i in range(8)])
    plane2 = lax.ppermute(kv, "z", [(i, (i + 2) % 8) for i in range(8)])
    own = jnp.where(c == 1, plane2, kv)
    slots = jnp.stack(
        [
            jnp.stack(
                [
                    jnp.where(d > y, kv, jnp.where(d < y, plane1, own)),
                    jnp.where(d < y, plane2, plane1),
                ]
            )
            for d in range(4)
        ]
    )
    mine = lax.all_to_all(slots, "y", 0, 0, tiled=True)
    other = lax.ppermute(mine, "c", [(0, 1), (1, 0)])

    targets = lax.dynamic_index_in_dim(assignment[0], device, 0, keepdims=False)
    order = (targets % 8) * 8 + targets // 8
    row = (order[:, None] * 2 + jnp.arange(2, dtype=jnp.int32)[None, :]).reshape(1, BLOCK)
    query_rows = jnp.swapaxes(query_map, 1, 2).reshape(HEADS * FEATURES, HEAD_DIM)
    key_rows = jnp.swapaxes(key_map, 1, 2).reshape(HEADS * FEATURES, HEAD_DIM)
    loss_scale = HEAD_DIM / math.sqrt(4 * 64 * BLOCK)
    difference, outgoing = main_call(
        loss_scale,
        jnp.reshape(device, (1,)).astype(jnp.int32),
        documents[0],
        queries[0],
        keys[0],
        values[0],
        mine,
        other,
        query_rows,
        key_rows,
        row,
    )
    got = lax.all_to_all(outgoing, ("y", "c"), 0, 0, tiled=True)
    relay = got[:, :, :1024].reshape(8, 8, 2, 1024).transpose(1, 0, 2, 3).reshape(8, 16, 1024)
    part = jnp.sum(got[:, :, 1024:].astype(F32), axis=0).astype(BF16)
    part = jnp.broadcast_to(part[None], (8, 16, 512))
    got = lax.all_to_all(jnp.concatenate([relay, part], axis=2), "z", 0, 0, tiled=True)
    relaid = got[:, :, :1024].reshape(1, BLOCK, 1024)
    part = jnp.sum(got[:, :, 1024:].astype(F32), axis=0).astype(BF16)
    part = jnp.broadcast_to(part[None], (32, 16, 512))
    got = lax.all_to_all(part, ("x", "y", "c"), 0, 0, tiled=True)
    grad = jnp.sum(got.reshape(4, 8, 16, 512).astype(F32), axis=0)
    grad = grad.reshape(HEADS, 16, 4, HEAD_DIM).transpose(0, 2, 1, 3).reshape(HEADS, FEATURES, HEAD_DIM)
    return relaid, difference[None], jnp.swapaxes(grad, 1, 2)


def solution(mesh):
    split = Mesh(np.array(mesh.devices).reshape(4, 8, 4, 2), ("x", "z", "y", "c"))
    ctx = ("z", "y", "c")
    return jax.shard_map(
        on_device,
        mesh=split,
        in_specs=(
            P("x", ctx, None),
            P("x", ctx, None),
            P("x", ctx, None),
            P(),
            P(),
            P("x", None),
            P("x", None, None),
        ),
        out_specs=(P("x", ctx, None), P("x", ctx, None), P()),
        check_vma=False,
    )
```

time: 874 us -> 92.2 us (0.11)
  waiting for transfers between devices: 339 us -> 17.4 us
  blocking collectives: 178 us -> 41.5 us
  other arithmetic: 116 us -> 1.99 us
  local copies, waits for them, and re-layouts: 98.4 us -> 3.52 us
  matrix products: 53.3 us -> 0 us
  loops' own time: 46.7 us -> 0 us
  between operations: 15.4 us -> 0.79 us
  Pallas kernels: 0 us -> 11.8 us
    psum x1 -> x0, waiting for transfers between devices: 244 us -> none  [on_device(): feature_grad = lax.psum(local_grad, ('dp', 'ctx'))]
    unnamed x1 -> x0, blocking collectives: 126 us -> none
    all_gather x3 -> x0, waiting for transfers between devices: 89.3 us -> none  [the longest x1 46.8 us: attend(): key_part = lax.all_gather(keys, 'ctx', axis=1, tiled=True)[0]]
    select_n x130 -> x0, other arithmetic: 83.1 us -> none  [the longest x128 83.1 us: lap(): return jax.tree.map(lambda a, b: jnp.where(reached, a, b), new, before)]
    dynamic_slice x72 -> x0, local copies, waits for them, and re-layouts: 78.9 us -> none  [the longest x64 76.5 us: lap(): part[k].astype(own.dtype)]
    all_gather x1 -> x0, blocking collectives: 52.1 us -> none  [prefix(): lax.all_gather(part.astype(kind), axis)]
    dot_general x19 -> x0, matrix products: 51.4 us -> none  [the longest x1 15.4 us: attend(): jnp.einsum('qhe,ke->hqk', query_rows, key_part, preferred_element_type=jn...]
    another operation x3 -> x0, loops' own time: 46.7 us -> none  [the longest x1 44.2 us: prefix(): return lax.fori_loop(0, peers, lap, start)]
  transfers between devices with their start and end apart: 6 -> 4, of which waited for: 4 -> 4; matrix products, arithmetic and copies ran while one was open for 9% -> 2% of each run, Pallas kernels for 0% -> 0%
where the time goes in v1:
time: 92.2 us; the launch traced here: 91.8 us
  blocking collectives  41.5 us (45%)
  waiting for transfers between devices  17.4 us (19%)
  starting transfers between devices  14.9 us (16%)
  Pallas kernels  11.8 us (13%)
  local copies, waits for them, and re-layouts  3.52 us (4%)
  other arithmetic  1.99 us (2%)
    all_to_all x1, blocking collectives, on_device(): lax.all_to_all(jnp.concatenate([relay, part], axis=2), 'z', 0, 0, tiled=T...  18.3 us
    all_to_all x1, blocking collectives, on_device(): mine = lax.all_to_all(slots, 'y', 0, 0, tiled=True)  12.4 us
    pallas_call x1, Pallas kernels, main_call(): pl.pallas_call(functools.partial(main_kernel, loss_scale), out_shape=(jax...  11.8 us
    all_to_all x1, waiting for transfers between devices, on_device(): got = lax.all_to_all(part, ('x', 'y', 'c'), 0, 0, tiled=True)  10.9 us
    all_to_all x1, blocking collectives, on_device(): got = lax.all_to_all(outgoing, ('y', 'c'), 0, 0, tiled=True)  10.8 us
    all_to_all x1, starting transfers between devices, on_device(): got = lax.all_to_all(part, ('x', 'y', 'c'), 0, 0, tiled=True)  7.28 us
    ppermute x1, starting transfers between devices, on_device(): plane2 = lax.ppermute(kv, 'z', [(i, (i + 2) % 8) for i in range(8)])  3.82 us
    ppermute x1, waiting for transfers between devices, on_device(): plane2 = lax.ppermute(kv, 'z', [(i, (i + 2) % 8) for i in range(8)])  3.14 us
  transfers between devices with their start and end apart: 4, of which 4 were waited for; matrix products, arithmetic and copies ran while one was open for 2% of the time, Pallas kernels for 0%

profile of v1, /device:TPU:1, one launch (start us, length us, event | category | flops | bytes accessed | tf_op | source)
XLA Modules:
  0.0 91.8 jit_solution(17189508350491250208)
XLA Ops:
  0.6 0.0 copy-start
  0.6 0.0 copy-start.1
  0.7 0.8 pad_maximum_fusion.2
  1.5 3.8 %collective-permute-start.1 = (bf16[256,128]{1,0:T(8,128)(2,1)S(1)}, bf16[256,128]{1,0:T(8,128)(2,1)S(1)}, u32[]{:S(2)}, u32[]{:S(2)}) collective-permute-start(bf16[256,128]{1,0:T(8,128)(2,1)S(1)} %pad_maximum_fusion.2), channel_id=1, source_target_pairs={{0,16},{8,24},{16,32},{24,40},{32,48},{40,56},{48,0},{56,8},{1,17}... | collective-permute-start | bytes 196616 | tf_op jit(solution)/shard_map/ppermute | solution.py:228
  5.3 1.6 %collective-permute-start = (bf16[256,128]{1,0:T(8,128)(2,1)S(1)}, bf16[256,128]{1,0:T(8,128)(2,1)S(1)}, u32[]{:S(2)}, u32[]{:S(2)}) collective-permute-start(bf16[256,128]{1,0:T(8,128)(2,1)S(1)} %pad_maximum_fusion.2), channel_id=1, source_target_pairs={{0,8},{8,16},{16,24},{24,32},{32,40},{40,48},{48,56},{56,0},{1,9},... | collective-permute-start | bytes 196616 | tf_op jit(solution)/shard_map/ppermute | solution.py:227
  6.9 3.1 %collective-permute-done.1 = bf16[256,128]{1,0:T(8,128)(2,1)S(1)} collective-permute-done((bf16[256,128]{1,0:T(8,128)(2,1)S(1)}, bf16[256,128]{1,0:T(8,128)(2,1)S(1)}, u32[]{:S(2)}, u32[]{:S(2)}) %collective-permute-start.1) | collective-permute-done | bytes 65568 | tf_op jit(solution)/shard_map/ppermute | solution.py:228
  10.1 2.7 %collective-permute-done = bf16[256,128]{1,0:T(8,128)(2,1)S(1)} collective-permute-done((bf16[256,128]{1,0:T(8,128)(2,1)S(1)}, bf16[256,128]{1,0:T(8,128)(2,1)S(1)}, u32[]{:S(2)}, u32[]{:S(2)}) %collective-permute-start) | collective-permute-done | bytes 65568 | tf_op jit(solution)/shard_map/ppermute | solution.py:227
  12.8 0.0 copy-done
  12.8 0.0 copy-done.1
  12.8 0.1 select_bitcast_fusion.7
  13.0 0.1 pad_maximum_fusion
  13.1 0.0 copy-start.2
  13.1 0.0 copy-start.3
  13.1 0.0 copy-start.4
  13.1 12.4 %all_to_all.20.a_ref = bf16[4,2,256,128]{3,2,1,0:T(8,128)(2,1)S(1)} all-to-all(bf16[4,2,256,128]{3,2,1,0:T(8,128)(2,1)S(1)} %pad_maximum_fusion), channel_id=1, replica_groups=mesh['x'=4,'z'=8,'y'=4,'c'=2] {'y'}, dimensions={0} | all-to-all | bytes 1048576 | tf_op jit(solution)/shard_map/all_to_all | solution.py:241
  25.6 2.1 %collective-permute-start.2 = (bf16[4,2,256,128]{3,2,1,0:T(8,128)(2,1)S(1)}, bf16[4,2,256,128]{3,2,1,0:T(8,128)(2,1)S(1)}, u32[]{:S(2)}, u32[]{:S(2)}) collective-permute-start(bf16[4,2,256,128]{3,2,1,0:T(8,128)(2,1)S(1)} %all_to_all.20.a_ref), channel_id=1, source_target_pairs={{0,1},{1,0},{2,3},{3,2},{4,5},{5,4},{6,7},{7,6},{8,9},{9,8},{10,11... | collective-permute-start | bytes 1572872 | tf_op jit(solution)/shard_map/ppermute | solution.py:242
  27.7 0.7 fusion.2
  28.4 0.1 iota_add_fusion
  28.5 0.1 add.63.row_ref
  28.6 0.6 collective-permute-done.2.b_ref
  29.2 0.0 copy-start.5
  29.2 0.0 copy-done.2
  29.2 0.0 copy-done.3
  29.2 0.0 copy-done.4
  29.2 0.6 copy-done.5
  29.9 11.8 %transfer.1 = (f32[128,1024]{1,0:T(8,128)}, bf16[8,16,1536]{2,1,0:T(8,128)(2,1)S(1)}) custom-call(s32[1]{0:T(128)} %bitcast.pos_ref, s32[64]{0:T(128)S(1)} %bitcast.70, bf16[128,1024]{1,0:T(8,128)(2,1)S(1)} %bitcast.67, bf16[128,128]{1,0:T(8,128)(2,1)S(1)} %bitcast.63, bf16[128,128]{1,0:T(8,128)(2,1)S(1)} %bitcast.66, ...), custom_call_target="tpu_custom_call" | custom-call | flops 3000000000 | bytes 3000000 | tf_op jit(solution)/shard_map/transfer/pallas_call | solution.py:198
  41.7 10.8 %all_to_all.21 = bf16[8,16,1536]{2,1,0:T(8,128)(2,1)S(1)} all-to-all(bf16[8,16,1536]{2,1,0:T(8,128)(2,1)S(1)} %get-tuple-element.5), channel_id=1, replica_groups=mesh['x'=4,'z'=8,'y'=4,'c'=2] {'y','c'}, dimensions={0} | all-to-all | bytes 786432 | tf_op jit(solution)/shard_map/all_to_all | solution.py:263
  52.5 0.1 reshape.115
  52.6 0.1 copy.17
  52.8 0.1 copy.18
  52.9 18.3 %all_to_all.22 = bf16[8,16,1536]{2,1,0:T(8,128)(2,1)S(1)} all-to-all(bf16[8,16,1536]{2,1,0:T(8,128)(2,1)S(1)} %copy.18), channel_id=1, replica_groups=mesh['x'=4,'z'=8,'y'=4,'c'=2] {'z'}, dimensions={0} | all-to-all | bytes 786432 | tf_op jit(solution)/shard_map/all_to_all | solution.py:267
  71.2 0.9 broadcast_in_dim.8
  72.0 7.3 %all-to-all-start.3 = ((bf16[32,16,512]{2,1,0:T(8,128)(2,1)}), bf16[32,16,512]{2,1,0:T(8,128)(2,1)S(1)}, u32[]{:S(2)}, u32[]{:S(2)}) async-start(bf16[32,16,512]{2,1,0:T(8,128)(2,1)} %broadcast_in_dim.8), calls=%async_computation.3 | async-start | bytes 1048576 | tf_op jit(solution)/shard_map/all_to_all | solution.py:271
  79.3 0.7 slice.18
  80.1 10.9 %all-to-all-done.3 = bf16[32,16,512]{2,1,0:T(8,128)(2,1)S(1)} async-done(((bf16[32,16,512]{2,1,0:T(8,128)(2,1)}), bf16[32,16,512]{2,1,0:T(8,128)(2,1)S(1)}, u32[]{:S(2)}, u32[]{:S(2)}) %all-to-all-start.3) | async-done | bytes 524320 | tf_op jit(solution)/shard_map/all_to_all | solution.py:271
  90.9 0.1 convert_reduce_fusion
  91.0 0.1 reshape.118
  91.1 0.7 copy.19
  (7 shorter events, 0.2 us)
Async XLA Ops:
  0.6 12.2 %copy-start = (bf16[1,128,128]{2,1,0:T(8,128)(2,1)S(1)}, bf16[1,128,128]{2,1,0:T(8,128)(2,1)}, u32[]{:S(2)}) copy-start(bf16[1,128,128]{2,1,0:T(8,128)(2,1)} %param.8) | copy-start | bytes 98308
  0.6 12.2 %copy-start.1 = (bf16[1,128,128]{2,1,0:T(8,128)(2,1)S(1)}, bf16[1,128,128]{2,1,0:T(8,128)(2,1)}, u32[]{:S(2)}) copy-start(bf16[1,128,128]{2,1,0:T(8,128)(2,1)} %param.9) | copy-start | bytes 98308
  1.5 8.6 %collective-permute-start.1 = (bf16[256,128]{1,0:T(8,128)(2,1)S(1)}, bf16[256,128]{1,0:T(8,128)(2,1)S(1)}, u32[]{:S(2)}, u32[]{:S(2)}) collective-permute-start(bf16[256,128]{1,0:T(8,128)(2,1)S(1)} %pad_maximum_fusion.2), channel_id=1, source_target_pairs={{0,16},{8,24},{16,32},{24,40},{32,48},{40,56},{48,0},{56,8},{1,17}... | collective-permute-start | bytes 196616 | tf_op jit(solution)/shard_map/ppermute | solution.py:228
  5.3 7.5 %collective-permute-start = (bf16[256,128]{1,0:T(8,128)(2,1)S(1)}, bf16[256,128]{1,0:T(8,128)(2,1)S(1)}, u32[]{:S(2)}, u32[]{:S(2)}) collective-permute-start(bf16[256,128]{1,0:T(8,128)(2,1)S(1)} %pad_maximum_fusion.2), channel_id=1, source_target_pairs={{0,8},{8,16},{16,24},{24,32},{32,40},{40,48},{48,56},{56,0},{1,9},... | collective-permute-start | bytes 196616 | tf_op jit(solution)/shard_map/ppermute | solution.py:227
  13.1 16.1 %copy-start.2 = (bf16[1,128,1024]{2,1,0:T(8,128)(2,1)S(1)}, bf16[1,128,1024]{2,1,0:T(8,128)(2,1)}, u32[]{:S(2)}) copy-start(bf16[1,128,1024]{2,1,0:T(8,128)(2,1)} %param.7) | copy-start | bytes 786436
  13.1 16.1 %copy-start.3 = (bf16[8,128,64]{1,2,0:T(8,128)(2,1)S(1)}, bf16[8,128,64]{1,2,0:T(8,128)(2,1)}, u32[]{:S(2)}) copy-start(bf16[8,128,64]{1,2,0:T(8,128)(2,1)} %param.10) | copy-start | bytes 393220
  13.1 16.1 %copy-start.4 = (bf16[8,128,64]{1,2,0:T(8,128)(2,1)S(1)}, bf16[8,128,64]{1,2,0:T(8,128)(2,1)}, u32[]{:S(2)}) copy-start(bf16[8,128,64]{1,2,0:T(8,128)(2,1)} %param.11) | copy-start | bytes 393220
  25.6 3.7 %collective-permute-start.2 = (bf16[4,2,256,128]{3,2,1,0:T(8,128)(2,1)S(1)}, bf16[4,2,256,128]{3,2,1,0:T(8,128)(2,1)S(1)}, u32[]{:S(2)}, u32[]{:S(2)}) collective-permute-start(bf16[4,2,256,128]{3,2,1,0:T(8,128)(2,1)S(1)} %all_to_all.20.a_ref), channel_id=1, source_target_pairs={{0,1},{1,0},{2,3},{3,2},{4,5},{5,4},{6,7},{7,6},{8,9},{9,8},{10,11... | collective-permute-start | bytes 1572872 | tf_op jit(solution)/shard_map/ppermute | solution.py:242
  29.2 0.7 copy-start.5
  72.0 18.9 %all-to-all-start.3 = ((bf16[32,16,512]{2,1,0:T(8,128)(2,1)}), bf16[32,16,512]{2,1,0:T(8,128)(2,1)S(1)}, u32[]{:S(2)}, u32[]{:S(2)}) async-start(bf16[32,16,512]{2,1,0:T(8,128)(2,1)} %broadcast_in_dim.8), calls=%async_computation.3 | async-start | bytes 1048576 | tf_op jit(solution)/shard_map/all_to_all | solution.py:271

commit v2 on v1

v2 whole, which is shorter than its diff:
```python
import functools
import math

import jax
import jax.numpy as jnp
import numpy as np
from jax import lax
from jax.experimental import pallas as pl
from jax.experimental.pallas import tpu as pltpu
from jax.sharding import Mesh, PartitionSpec as P

HEAD_DIM = 128
WINDOW = 64
BLOCK = 128
HEADS = 8
FEATURES = 64
ROWS = HEADS * BLOCK
CHUNK = 2 * BLOCK
CHUNKS = 8
FAR = CHUNK * CHUNKS
SCALE = math.log2(math.e) / math.sqrt(HEAD_DIM)
NEGATIVE = -1e30
NT = (((1,), (1,)), ((), ()))
NN = (((1,), (0,)), ((), ()))
TN = (((0,), (0,)), ((), ()))
TALL = HEAD_DIM + 16
F32 = jnp.float32
BF16 = jnp.bfloat16
LOG2E = math.log2(math.e)


def dot(a, b, dims=NN):
    return lax.dot_general(a, b, dims, preferred_element_type=F32)


def two_softmax(u):
    u = u * LOG2E
    top = jnp.max(u, axis=1, keepdims=True)
    low = jnp.min(u, axis=1, keepdims=True)
    up = jnp.exp2(u - top)
    down = jnp.exp2(low - u)
    up = up * (1.0 / jnp.sum(up, axis=1, keepdims=True))
    down = down * (1.0 / jnp.sum(down, axis=1, keepdims=True))
    return jnp.concatenate([up, down], axis=1)


def pack_kernel(k_ref, v_ref, out_ref):
    out_ref[:BLOCK, :] = k_ref[...]
    out_ref[BLOCK:, :] = v_ref[...].T


def pack_call(k, v):
    vmem = pl.BlockSpec(memory_space=pltpu.VMEM)
    return pl.pallas_call(
        pack_kernel,
        out_shape=jax.ShapeDtypeStruct((2 * BLOCK, HEAD_DIM), BF16),
        in_specs=[vmem] * 2,
        out_specs=vmem,
        compiler_params=pltpu.CompilerParams(vmem_limit_bytes=4 * 1024 * 1024),
        name="pack_block",
    )(k, v)


def with_ones(values):
    return jnp.concatenate([values, jnp.ones((TALL - HEAD_DIM, values.shape[1]), BF16)], axis=0)


def shard_index():
    return (lax.axis_index("z") * 4 + lax.axis_index("y")) * 2 + lax.axis_index("c")


def iota(shape, axis):
    return lax.broadcasted_iota(jnp.int32, shape, axis)


def local_kernel(
    q_ref,
    kv_ref,
    qm_ref,
    km_ref,
    route_ref,
    doc_ref,
    own_ref,
    near_ref,
    phi_ref,
    both_ref,
    psi_ref,
    dest_ref,
    ok_ref,
):
    keys = kv_ref[:BLOCK, :]
    values = with_ones(kv_ref[BLOCK:, :])
    col = lax.broadcasted_iota(jnp.int32, (BLOCK, BLOCK), 1)
    row = lax.broadcasted_iota(jnp.int32, (BLOCK, BLOCK), 0)
    causal = row <= col
    near = causal & ((col < WINDOW) == (row < WINDOW))
    first_half = col < WINDOW
    psi = two_softmax(dot(km_ref[...], keys, NT).reshape(HEADS, FEATURES, BLOCK))
    psi_ref[...] = psi.reshape(ROWS, BLOCK).astype(BF16)
    z, y, c = lax.axis_index("z"), lax.axis_index("y"), lax.axis_index("c")
    here = shard_index()
    place = iota((2 * CHUNKS, 64), 0)
    block = iota((2 * CHUNKS, 64), 1)
    from_y = lax.shift_right_logical(place, 1) & 3
    from_c = jnp.where(place < CHUNKS, c, 1 - c)
    first = jnp.where(from_y < y, 0, jnp.where(from_y > y, 1, 2 * from_c))
    second = jnp.where(from_y > y, 2, 1)
    source = (z - jnp.where((place & 1) == 0, first, second)) * 8 + from_y * 2 + from_c
    documents = doc_ref[...]
    own_document = jnp.sum(jnp.where(iota((1, 64), 1) == here, documents, 0), axis=1, keepdims=True)
    same = (documents == own_document) & (iota((1, 64), 1) < here) & (iota((1, 64), 1) > here - 16)
    found = jnp.where((source == block) & same, 1.0, 0.0)
    ok_ref[...] = jnp.broadcast_to(jnp.max(found, axis=1, keepdims=True), ok_ref.shape)
    shard = route_ref[pl.ds(here, 1), :]
    order = (shard & 7) * 8 + lax.shift_right_logical(shard, 3)
    pieces = (iota((64, 64), 0) == order).astype(BF16)
    rows = (lax.shift_right_logical(iota((BLOCK, 64), 0), 1) == iota((BLOCK, 64), 1)).astype(BF16)
    tokens = (iota((64, BLOCK), 0) == lax.shift_right_logical(iota((64, BLOCK), 1), 1)).astype(BF16)
    placed = dot(dot(rows, pieces).astype(BF16), tokens)
    dest_ref[...] = jnp.where((row & 1) == (col & 1), placed, 0.0).astype(BF16)
    for h in range(HEADS):
        at = h * BLOCK
        query = q_ref[:, at : at + BLOCK]
        scores = dot(keys, query, NT)
        own_ref[:, at : at + BLOCK] = jnp.where(causal, scores, NEGATIVE)
        window = jnp.where(near, scores * SCALE, NEGATIVE)
        weights = jnp.exp2(window - jnp.max(window, axis=0, keepdims=True))
        near_ref[:, at : at + BLOCK] = dot(values, weights.astype(BF16))
        u = dot(qm_ref[h * FEATURES : (h + 1) * FEATURES, :], query, NT)
        phi = two_softmax(u[None])[0]
        phi_ref[at : at + BLOCK, :] = phi
        both = jnp.concatenate(
            [jnp.where(first_half, phi, 0.0), jnp.where(first_half, 0.0, phi)], axis=0
        )
        both_ref[h * CHUNK : (h + 1) * CHUNK, :] = both.astype(BF16)


def local_call(q, kv, qm, km, routes, documents):
    vmem = pl.BlockSpec(memory_space=pltpu.VMEM)
    return pl.pallas_call(
        local_kernel,
        out_shape=(
            jax.ShapeDtypeStruct((BLOCK, ROWS), F32),
            jax.ShapeDtypeStruct((TALL, ROWS), F32),
            jax.ShapeDtypeStruct((ROWS, BLOCK), F32),
            jax.ShapeDtypeStruct((2 * ROWS, BLOCK), BF16),
            jax.ShapeDtypeStruct((ROWS, BLOCK), BF16),
            jax.ShapeDtypeStruct((BLOCK, BLOCK), BF16),
            jax.ShapeDtypeStruct((2 * CHUNKS, BLOCK), F32),
        ),
        in_specs=[vmem] * 6,
        out_specs=(vmem,) * 7,
        compiler_params=pltpu.CompilerParams(vmem_limit_bytes=16 * 1024 * 1024),
        cost_estimate=pl.CostEstimate(
            flops=400_000_000, bytes_accessed=4_000_000, transcendentals=500_000
        ),
        name="local_block",
    )(q, kv, qm, km, routes, documents)


def main_kernel(
    loss_scale,
    q_ref,
    kv_ref,
    a_ref,
    b_ref,
    km_ref,
    own_ref,
    near_ref,
    phi_ref,
    both_ref,
    psi_own_ref,
    dest_ref,
    ok_ref,
    diff_ref,
    buf_ref,
    s_scr,
    p_scr,
    psi_scr,
    key_scr,
    vp_scr,
):
    first_key = kv_ref[0:1, :]
    ones = jnp.ones((TALL - HEAD_DIM, BLOCK), BF16)
    for i in range(CHUNKS):
        src = a_ref if i < 4 else b_ref
        for k in range(2):
            at = i * CHUNK + k * BLOCK
            one = ok_ref[2 * i + k : 2 * i + k + 1, :]
            other = (1.0 - one).astype(BF16)
            one = one.astype(BF16)
            key_scr[at : at + BLOCK, :] = src[i % 4, k, :BLOCK, :] * one + first_key * other
            vp_scr[:HEAD_DIM, at : at + BLOCK] = src[i % 4, k, BLOCK:, :] * one
            vp_scr[HEAD_DIM:, at : at + BLOCK] = ones * one
    value_own = with_ones(kv_ref[BLOCK:, :])
    vp_scr[:, FAR:] = value_own
    early = lax.broadcasted_iota(jnp.int32, (TALL, BLOCK), 1) < WINDOW
    value_early = jnp.where(early, value_own.astype(F32), 0.0).astype(BF16)
    first_half = lax.broadcasted_iota(jnp.int32, (BLOCK, BLOCK), 1) < WINDOW
    first_row = lax.broadcasted_iota(jnp.int32, (TALL - HEAD_DIM, CHUNK), 0) == 0
    dest = dest_ref[...]

    groups = HEADS // 2
    tops, sums = [None] * groups, [None] * groups

    def scores(g):
        query = jnp.concatenate(
            [q_ref[:, (2 * g + k) * BLOCK : (2 * g + k + 1) * BLOCK] for k in range(2)], axis=0
        )
        top = jnp.max(
            own_ref[:, g * CHUNK : (g + 1) * CHUNK].reshape(BLOCK // 8, 8, CHUNK), axis=0
        )
        for i in range(CHUNKS):
            s = dot(key_scr[i * CHUNK : (i + 1) * CHUNK, :], query, NT)
            s_scr[g % 2, i * CHUNK : (i + 1) * CHUNK, :] = s
            top = jnp.maximum(top, jnp.max(s.reshape(CHUNK // 8, 8, CHUNK), axis=0))
            yield
        tops[g] = jnp.max(top, axis=0, keepdims=True) * SCALE

    def features(g):
        for i in range(CHUNKS):
            keys = key_scr[i * CHUNK : (i + 1) * CHUNK, :]
            u = dot(km_ref[g * BLOCK : (g + 1) * BLOCK, :], keys, NT)
            psi = two_softmax(u.reshape(2, FEATURES, CHUNK)).reshape(CHUNK, CHUNK)
            psi_scr[g % 3, :, i * CHUNK : (i + 1) * CHUNK] = psi.astype(BF16)
            yield

    def weights(g):
        for i in range(CHUNKS):
            s = s_scr[g % 2, i * CHUNK : (i + 1) * CHUNK, :]
            w = jnp.exp2(s * SCALE - tops[g])
            p_scr[g % 2, i * CHUNK : (i + 1) * CHUNK, :] = w.astype(BF16)
            yield
        s = own_ref[:, g * CHUNK : (g + 1) * CHUNK]
        p_scr[g % 2, FAR:, :] = jnp.exp2(s * SCALE - tops[g]).astype(BF16)
        yield

    def mixes(g):
        mixed = dot(vp_scr[...], p_scr[g % 2])
        yield
        state = dot(vp_scr[:, :FAR], psi_scr[g % 3], NT)
        yield
        late = state + dot(value_early, psi_own_ref[g * CHUNK : (g + 1) * CHUNK, :], NT)
        sums[g] = (mixed, state.astype(BF16), late.astype(BF16))
        yield

    def outputs(g):
        mixed, state, late = sums[g]
        heads = [2 * g, 2 * g + 1]
        parts = [slice(0, BLOCK), slice(BLOCK, CHUNK)]
        wide = slice(g * CHUNK, (g + 1) * CHUNK)
        states = [jnp.concatenate([state[:, p], late[:, p]], axis=1) for p in parts]
        far = [dot(states[k], both_ref[heads[k] * CHUNK : (heads[k] + 1) * CHUNK, :]) for k in range(2)]
        yield
        total = jnp.concatenate(far, axis=1) + near_ref[:, wide]
        share = 1.0 / mixed[HEAD_DIM : HEAD_DIM + 1]
        teacher = (mixed[:HEAD_DIM] * share).astype(BF16)
        yield
        moved = [dot(dest, teacher[:, p], NT) for p in parts]
        inverse = 1.0 / total[HEAD_DIM : HEAD_DIM + 1]
        student = total[:HEAD_DIM] * inverse
        gap = student - teacher.astype(F32)
        yield
        grad_out = gap * (inverse * (2.0 * loss_scale))
        drop = jnp.sum(grad_out * student, axis=0, keepdims=True)
        drop = jnp.where(first_row, -drop, 0.0).astype(BF16)
        grad_both = jnp.concatenate([grad_out.astype(BF16), drop], axis=0)
        yield
        dphi = [dot(states[k], grad_both[:, parts[k]], TN) for k in range(2)]
        yield
        for k in range(2):
            diff_ref[:, heads[k] * BLOCK : (heads[k] + 1) * BLOCK] = gap[:, parts[k]].T
            for shard in range(8):
                buf_ref[shard, :, heads[k] * BLOCK : (heads[k] + 1) * BLOCK] = moved[k][
                    shard * 16 : (shard + 1) * 16
                ].astype(BF16)
        yield
        du = []
        for k in range(2):
            phi = phi_ref[heads[k] * BLOCK : (heads[k] + 1) * BLOCK, :]
            terms = phi * jnp.where(first_half, dphi[k][:BLOCK], dphi[k][BLOCK:])
            up, down = phi[:FEATURES], phi[FEATURES:]
            du.append(
                terms[:FEATURES]
                - terms[FEATURES:]
                - up * jnp.sum(terms[:FEATURES], axis=0, keepdims=True)
                + down * jnp.sum(terms[FEATURES:], axis=0, keepdims=True)
            )
        yield
        for k in range(2):
            h = heads[k]
            grad = dot(du[k].astype(BF16), q_ref[:, h * BLOCK : (h + 1) * BLOCK]).astype(BF16)
            for i in range(4):
                at = (HEADS + i) * BLOCK
                buf_ref[h, :, at : at + BLOCK] = grad[i * 16 : (i + 1) * 16]
        yield

    for step in range(groups + 3):
        running = []
        for stage, length, late_by in (
            (scores, 9, 0),
            (features, 8, 0),
            (weights, 9, 1),
            (mixes, 3, 2),
            (outputs, 8, 3),
        ):
            if 0 <= step - late_by < groups:
                running.append((stage(step - late_by), length))
        marks = sorted(
            ((n + 0.5) / length, at) for at, (_, length) in enumerate(running) for n in range(length)
        )
        for _, at in marks:
            next(running[at][0], None)
        for stage, _ in running:
            for _ in stage:
                pass


def main_call(loss_scale, q, kv, a, b, km, local):
    vmem = pl.BlockSpec(memory_space=pltpu.VMEM)
    return pl.pallas_call(
        functools.partial(main_kernel, loss_scale),
        out_shape=(
            jax.ShapeDtypeStruct((BLOCK, HEADS * HEAD_DIM), F32),
            jax.ShapeDtypeStruct((8, 16, 1536), BF16),
        ),
        in_specs=[vmem] * 12,
        out_specs=(vmem, vmem),
        scratch_shapes=[
            pltpu.VMEM((2, FAR, CHUNK), F32),
            pltpu.VMEM((2, FAR + BLOCK, CHUNK), BF16),
            pltpu.VMEM((3, CHUNK, FAR), BF16),
            pltpu.VMEM((FAR, BLOCK), BF16),
            pltpu.VMEM((TALL, FAR + BLOCK), BF16),
        ],
        compiler_params=pltpu.CompilerParams(vmem_limit_bytes=32 * 1024 * 1024),
        cost_estimate=pl.CostEstimate(
            flops=3_000_000_000, bytes_accessed=3_000_000, transcendentals=4_000_000
        ),
        name="transfer",
    )(q, kv, a, b, km, *local)


def on_device(queries, keys, values, query_map, key_map, documents, assignment):
    y, c = lax.axis_index("y"), lax.axis_index("c")
    query_rows = jnp.swapaxes(query_map, 1, 2).reshape(HEADS * FEATURES, HEAD_DIM)
    key_rows = jnp.swapaxes(key_map, 1, 2).reshape(HEADS * FEATURES, HEAD_DIM)
    kv = pack_call(keys[0], values[0])
    plane1 = lax.ppermute(kv, "z", [(i, (i + 1) % 8) for i in range(8)])
    plane2 = lax.ppermute(kv, "z", [(i, (i + 2) % 8) for i in range(8)])
    local = local_call(queries[0], kv, query_rows, key_rows, assignment[0], documents)
    plane1, plane2, local = lax.optimization_barrier((plane1, plane2, local))
    own = jnp.where(c == 1, plane2, kv)
    slots = jnp.stack(
        [
            jnp.stack(
                [
                    jnp.where(d > y, kv, jnp.where(d < y, plane1, own)),
                    jnp.where(d < y, plane2, plane1),
                ]
            )
            for d in range(4)
        ]
    )
    mine = lax.all_to_all(slots, "y", 0, 0, tiled=True)
    other = lax.ppermute(mine, "c", [(0, 1), (1, 0)])
    loss_scale = HEAD_DIM / math.sqrt(4 * 64 * BLOCK)
    difference, outgoing = main_call(
        loss_scale, queries[0], kv, mine, other, key_rows, local
    )
    got = lax.all_to_all(outgoing, ("y", "c"), 0, 0, tiled=True)
    relay = got[:, :, :1024].reshape(8, 8, 2, 1024).transpose(1, 0, 2, 3).reshape(8, 16, 1024)
    part = jnp.sum(got[:, :, 1024:].astype(F32), axis=0).astype(BF16)
    part = jnp.broadcast_to(part[None], (8, 16, 512))
    got = lax.all_to_all(jnp.concatenate([relay, part], axis=2), "z", 0, 0, tiled=True)
    relaid = got[:, :, :1024].reshape(1, BLOCK, 1024)
    part = jnp.sum(got[:, :, 1024:].astype(F32), axis=0).astype(BF16)
    part = part.reshape(16, 4, HEAD_DIM).transpose(1, 0, 2).reshape(FEATURES, HEAD_DIM)
    part = jnp.broadcast_to(part[None], (32, FEATURES, HEAD_DIM))
    got = lax.all_to_all(part, ("x", "y", "c"), 0, 0, tiled=True)
    grad = jnp.sum(got.reshape(4, HEADS, FEATURES, HEAD_DIM).astype(F32), axis=0)
    return relaid, difference[None], jnp.swapaxes(grad, 1, 2)


def solution(mesh):
    split = Mesh(np.array(mesh.devices).reshape(4, 8, 4, 2), ("x", "z", "y", "c"))
    ctx = ("z", "y", "c")
    return jax.shard_map(
        on_device,
        mesh=split,
        in_specs=(
            P("x", ctx, None),
            P("x", ctx, None),
            P("x", ctx, None),
            P(),
            P(),
            P("x", None),
            P("x", None, None),
        ),
        out_specs=(P("x", ctx, None), P("x", ctx, None), P()),
        check_vma=False,
    )
```

time: 92.2 us -> 88 us (0.954)
  waiting for transfers between devices: 17.4 us -> 13.8 us
  local copies, waits for them, and re-layouts: 3.52 us -> 6 us
  Pallas kernels: 11.8 us -> 9.42 us
  other arithmetic: 1.99 us -> 1.02 us
    pallas_call x1, Pallas kernels: 11.8 us -> 7.41 us  [main_call(): pl.pallas_call(functools.partial(main_kernel, loss_scale), out_shape=(jax...]
    unnamed x12 -> x18, local copies, waits for them, and re-layouts: 0.67 us -> 4.03 us
    ppermute x1, waiting for transfers between devices: 3.14 us -> 0.01 us  [on_device(): plane2 = lax.ppermute(kv, 'z', [(i, (i + 2) % 8) for i in range(8)])]
    pallas_call x0 -> x2, Pallas kernels: none -> 2.01 us  [the longest x1 1.94 us: local_call(): pl.pallas_call(local_kernel, out_shape=(jax.ShapeDtypeStruct((BLOCK, ROWS...]
    ppermute x1, waiting for transfers between devices: 2.74 us -> 1.42 us  [on_device(): plane1 = lax.ppermute(kv, 'z', [(i, (i + 1) % 8) for i in range(8)])]
    ppermute x1, waiting for transfers between devices: 0.61 us -> 1.54 us  [on_device(): other = lax.ppermute(mine, 'c', [(0, 1), (1, 0)])]
  transfers between devices with their start and end apart: 4 -> 4, of which waited for: 4 -> 3; matrix products, arithmetic and copies ran while one was open for 2% -> 1% of each run, Pallas kernels for 0% -> 2%
where the time goes in v2:
time: 88 us; the launch traced here: 87.5 us
  blocking collectives  41.5 us (47%)
  starting transfers between devices  14.9 us (17%)
  waiting for transfers between devices  13.8 us (16%)
  Pallas kernels  9.42 us (11%)
  local copies, waits for them, and re-layouts  6 us (7%)
  other arithmetic  1.02 us (1%)
    all_to_all x1, blocking collectives, on_device(): lax.all_to_all(jnp.concatenate([relay, part], axis=2), 'z', 0, 0, tiled=T...  18.3 us
    all_to_all x1, blocking collectives, on_device(): mine = lax.all_to_all(slots, 'y', 0, 0, tiled=True)  12.4 us
    all_to_all x1, waiting for transfers between devices, on_device(): got = lax.all_to_all(part, ('x', 'y', 'c'), 0, 0, tiled=True)  10.9 us
    all_to_all x1, blocking collectives, on_device(): got = lax.all_to_all(outgoing, ('y', 'c'), 0, 0, tiled=True)  10.8 us
    pallas_call x1, Pallas kernels, main_call(): pl.pallas_call(functools.partial(main_kernel, loss_scale), out_shape=(jax...  7.41 us
    all_to_all x1, starting transfers between devices, on_device(): got = lax.all_to_all(part, ('x', 'y', 'c'), 0, 0, tiled=True)  7.28 us
    unnamed x18, local copies, waits for them, and re-layouts  4.03 us
    ppermute x1, starting transfers between devices, on_device(): plane2 = lax.ppermute(kv, 'z', [(i, (i + 2) % 8) for i in range(8)])  3.9 us
  transfers between devices with their start and end apart: 4, of which 3 were waited for; matrix products, arithmetic and copies ran while one was open for 1% of the time, Pallas kernels for 2%

profile of v2, /device:TPU:1, one launch (start us, length us, event | category | flops | bytes accessed | tf_op | source)
XLA Modules:
  0.0 87.5 jit_solution(13515299630544532101)
XLA Ops:
  0.6 0.0 copy-start
  0.6 0.7 copy-done
  1.4 0.0 copy-start.1
  1.4 0.8 copy-done.1
  2.1 0.0 copy-start.4
  2.2 0.1 pack_block.1.kv_ref
  2.2 0.0 copy-start.7
  2.2 3.9 %collective-permute-start.1 = (bf16[256,128]{1,0:T(8,128)(2,1)S(1)}, bf16[256,128]{1,0:T(8,128)(2,1)S(1)}, u32[]{:S(2)}, u32[]{:S(2)}) collective-permute-start(bf16[256,128]{1,0:T(8,128)(2,1)S(1)} %pack_block.1.kv_ref), channel_id=1, source_target_pairs={{0,16},{8,24},{16,32},{24,40},{32,48},{40,56},{48,0},{56,8},{1,17}... | collective-permute-start | bytes 196616 | tf_op jit(solution)/shard_map/ppermute | solution.py:350
  6.1 1.6 %collective-permute-start = (bf16[256,128]{1,0:T(8,128)(2,1)S(1)}, bf16[256,128]{1,0:T(8,128)(2,1)S(1)}, u32[]{:S(2)}, u32[]{:S(2)}) collective-permute-start(bf16[256,128]{1,0:T(8,128)(2,1)S(1)} %pack_block.1.kv_ref), channel_id=1, source_target_pairs={{0,8},{8,16},{16,24},{24,32},{32,40},{40,48},{48,56},{56,0},{1,9},... | collective-permute-start | bytes 196616 | tf_op jit(solution)/shard_map/ppermute | solution.py:349
  7.8 0.0 copy-start.8
  7.8 0.0 copy-done.4
  7.8 0.0 copy-done.7
  7.8 0.6 copy-done.8
  8.4 0.0 copy-start.2
  8.4 0.9 %copy-done.2 = bf16[1,128,1024]{2,1,0:T(8,128)(2,1)S(1)} copy-done((bf16[1,128,1024]{2,1,0:T(8,128)(2,1)S(1)}, bf16[1,128,1024]{2,1,0:T(8,128)(2,1)}, u32[]{:S(2)}) %copy-start.2) | copy-done | bytes 262168
  9.4 0.0 copy-start.5
  9.4 0.9 %copy-done.5 = bf16[8,128,64]{1,2,0:T(8,128)(2,1)S(1)} copy-done((bf16[8,128,64]{1,2,0:T(8,128)(2,1)S(1)}, bf16[8,128,64]{1,2,0:T(8,128)(2,1)}, u32[]{:S(2)}) %copy-start.5) | copy-done | bytes 131096
  10.3 1.9 %local_block.1 = (f32[128,1024]{1,0:T(8,128)S(1)}, f32[144,1024]{1,0:T(8,128)S(1)}, f32[1024,128]{1,0:T(8,128)S(1)}, bf16[2048,128]{1,0:T(8,128)(2,1)S(1)}, bf16...) custom-call(bf16[128,1024]{1,0:T(8,128)(2,1)S(1)} %bitcast.46, ...), custom_call_target="tpu_custom_call" | custom-call | flops 400000000 | bytes 4000000 | tf_op jit(solution)/shard_map/local_block/pallas_call | solution.py:140
  12.2 0.0 collective-permute-done.1
  12.2 1.4 %collective-permute-done = bf16[256,128]{1,0:T(8,128)(2,1)S(1)} collective-permute-done((bf16[256,128]{1,0:T(8,128)(2,1)S(1)}, bf16[256,128]{1,0:T(8,128)(2,1)S(1)}, u32[]{:S(2)}, u32[]{:S(2)}) %collective-permute-start) | collective-permute-done | bytes 65568 | tf_op jit(solution)/shard_map/ppermute | solution.py:349
  13.8 0.1 pad_maximum_fusion
  13.9 0.0 copy-start.3
  13.9 0.0 copy-start.6
  13.9 12.4 %all_to_all.20.a_ref = bf16[4,2,256,128]{3,2,1,0:T(8,128)(2,1)S(1)} all-to-all(bf16[4,2,256,128]{3,2,1,0:T(8,128)(2,1)S(1)} %pad_maximum_fusion), channel_id=1, replica_groups=mesh['x'=4,'z'=8,'y'=4,'c'=2] {'y'}, dimensions={0} | all-to-all | bytes 1048576 | tf_op jit(solution)/shard_map/all_to_all | solution.py:365
  26.3 2.1 %collective-permute-start.2 = (bf16[4,2,256,128]{3,2,1,0:T(8,128)(2,1)S(1)}, bf16[4,2,256,128]{3,2,1,0:T(8,128)(2,1)S(1)}, u32[]{:S(2)}, u32[]{:S(2)}) collective-permute-start(bf16[4,2,256,128]{3,2,1,0:T(8,128)(2,1)S(1)} %all_to_all.20.a_ref), channel_id=1, source_target_pairs={{0,1},{1,0},{2,3},{3,2},{4,5},{5,4},{6,7},{7,6},{8,9},{9,8},{10,11... | collective-permute-start | bytes 1572872 | tf_op jit(solution)/shard_map/ppermute | solution.py:366
  28.4 1.5 %collective-permute-done.2.b_ref = bf16[4,2,256,128]{3,2,1,0:T(8,128)(2,1)S(1)} collective-permute-done((bf16[4,2,256,128]{3,2,1,0:T(8,128)(2,1)S(1)}, bf16[4,2,256,128]{3,2,1,0:T(8,128)(2,1)S(1)}, u32[]{:S(2)}, u32[]{:S(2)}) %collective-permute-start.2) | collective-permute-done | bytes 524320 | tf_op jit(solution)/shard_map/ppermute | solution.py:366
  30.0 0.0 copy-done.3
  30.0 0.0 copy-done.6
  30.0 7.4 %transfer.1 = (f32[128,1024]{1,0:T(8,128)}, bf16[8,16,1536]{2,1,0:T(8,128)(2,1)S(1)}) custom-call(bf16[128,1024]{1,0:T(8,128)(2,1)S(1)} %bitcast.47, bf16[256,128]{1,0:T(8,128)(2,1)S(1)} %pack_block.1.kv_ref, bf16[4,2,256,128]{3,2,1,0:T(8,128)(2,1)S(1)} %all_to_all.20.a_ref, bf16[4,2,256,128]{3,2,1,0:T(8,128)(2,1)S(1)} %collective-permute-done.2.b_ref, ...), custom_call_target="tpu_custom_call" | custom-call | flops 3000000000 | bytes 3000000 | tf_op jit(solution)/shard_map/transfer/pallas_call | solution.py:321
  37.4 10.8 %all_to_all.21 = bf16[8,16,1536]{2,1,0:T(8,128)(2,1)S(1)} all-to-all(bf16[8,16,1536]{2,1,0:T(8,128)(2,1)S(1)} %get-tuple-element.37), channel_id=1, replica_groups=mesh['x'=4,'z'=8,'y'=4,'c'=2] {'y','c'}, dimensions={0} | all-to-all | bytes 786432 | tf_op jit(solution)/shard_map/all_to_all | solution.py:371
  48.2 0.1 reshape.31
  48.3 0.1 copy.17
  48.5 0.1 copy.18
  48.6 18.3 %all_to_all.22 = bf16[8,16,1536]{2,1,0:T(8,128)(2,1)S(1)} all-to-all(bf16[8,16,1536]{2,1,0:T(8,128)(2,1)S(1)} %copy.18), channel_id=1, replica_groups=mesh['x'=4,'z'=8,'y'=4,'c'=2] {'z'}, dimensions={0} | all-to-all | bytes 786432 | tf_op jit(solution)/shard_map/all_to_all | solution.py:375
  66.9 0.9 %broadcast_in_dim.19 = bf16[32,64,128]{2,1,0:T(8,128)(2,1)} broadcast(bf16[64,128]{1,0:T(8,128)(2,1)S(1)} %bitcast.56), dimensions={1,2} | broadcast | bytes 540672 | tf_op jit(solution)/shard_map/broadcast_in_dim | solution.py:379
  67.8 7.3 %all-to-all-start.3 = ((bf16[32,64,128]{2,1,0:T(8,128)(2,1)}), bf16[32,64,128]{2,1,0:T(8,128)(2,1)S(1)}, u32[]{:S(2)}, u32[]{:S(2)}) async-start(bf16[32,64,128]{2,1,0:T(8,128)(2,1)} %broadcast_in_dim.19), calls=%async_computation.3 | async-start | bytes 1048576 | tf_op jit(solution)/shard_map/all_to_all | solution.py:380
  75.1 0.7 slice.18
  75.9 10.9 %all-to-all-done.3 = bf16[32,64,128]{2,1,0:T(8,128)(2,1)S(1)} async-done(((bf16[32,64,128]{2,1,0:T(8,128)(2,1)}), bf16[32,64,128]{2,1,0:T(8,128)(2,1)S(1)}, u32[]{:S(2)}, u32[]{:S(2)}) %all-to-all-start.3) | async-done | bytes 524320 | tf_op jit(solution)/shard_map/all_to_all | solution.py:380
  86.7 0.8 convert_reduce_fusion
  (10 shorter events, 0.2 us)
Async XLA Ops:
  0.6 0.8 copy-start
  1.4 0.8 copy-start.1
  2.1 5.6 %copy-start.4 = (bf16[8,128,64]{1,2,0:T(8,128)(2,1)S(1)}, bf16[8,128,64]{1,2,0:T(8,128)(2,1)}, u32[]{:S(2)}) copy-start(bf16[8,128,64]{1,2,0:T(8,128)(2,1)} %param.10) | copy-start | bytes 393220
  2.2 5.6 %copy-start.7 = (s32[1,64,64]{2,1,0:T(8,128)S(1)}, s32[1,64,64]{2,1,0:T(8,128)}, u32[]{:S(2)}) copy-start(s32[1,64,64]{2,1,0:T(8,128)} %param.13) | copy-start | bytes 49156
  2.2 10.0 %collective-permute-start.1 = (bf16[256,128]{1,0:T(8,128)(2,1)S(1)}, bf16[256,128]{1,0:T(8,128)(2,1)S(1)}, u32[]{:S(2)}, u32[]{:S(2)}) collective-permute-start(bf16[256,128]{1,0:T(8,128)(2,1)S(1)} %pack_block.1.kv_ref), channel_id=1, source_target_pairs={{0,16},{8,24},{16,32},{24,40},{32,48},{40,56},{48,0},{56,8},{1,17}... | collective-permute-start | bytes 196616 | tf_op jit(solution)/shard_map/ppermute | solution.py:350
  6.1 7.5 %collective-permute-start = (bf16[256,128]{1,0:T(8,128)(2,1)S(1)}, bf16[256,128]{1,0:T(8,128)(2,1)S(1)}, u32[]{:S(2)}, u32[]{:S(2)}) collective-permute-start(bf16[256,128]{1,0:T(8,128)(2,1)S(1)} %pack_block.1.kv_ref), channel_id=1, source_target_pairs={{0,8},{8,16},{16,24},{24,32},{32,40},{40,48},{48,56},{56,0},{1,9},... | collective-permute-start | bytes 196616 | tf_op jit(solution)/shard_map/ppermute | solution.py:349
  7.8 0.7 copy-start.8
  8.4 0.9 %copy-start.2 = (bf16[1,128,1024]{2,1,0:T(8,128)(2,1)S(1)}, bf16[1,128,1024]{2,1,0:T(8,128)(2,1)}, u32[]{:S(2)}) copy-start(bf16[1,128,1024]{2,1,0:T(8,128)(2,1)} %param.7) | copy-start | bytes 786436
  9.4 0.9 %copy-start.5 = (bf16[8,128,64]{1,2,0:T(8,128)(2,1)S(1)}, bf16[8,128,64]{1,2,0:T(8,128)(2,1)}, u32[]{:S(2)}) copy-start(bf16[8,128,64]{1,2,0:T(8,128)(2,1)} %param.11) | copy-start | bytes 393220
  13.9 16.1 %copy-start.3 = (bf16[1,128,1024]{2,1,0:T(8,128)(2,1)S(1)}, bf16[1,128,1024]{2,1,0:T(8,128)(2,1)}, u32[]{:S(2)}) copy-start(bf16[1,128,1024]{2,1,0:T(8,128)(2,1)} %param.7) | copy-start | bytes 786436
  13.9 16.1 %copy-start.6 = (bf16[8,128,64]{1,2,0:T(8,128)(2,1)S(1)}, bf16[8,128,64]{1,2,0:T(8,128)(2,1)}, u32[]{:S(2)}) copy-start(bf16[8,128,64]{1,2,0:T(8,128)(2,1)} %param.11) | copy-start | bytes 393220
  26.3 3.7 %collective-permute-start.2 = (bf16[4,2,256,128]{3,2,1,0:T(8,128)(2,1)S(1)}, bf16[4,2,256,128]{3,2,1,0:T(8,128)(2,1)S(1)}, u32[]{:S(2)}, u32[]{:S(2)}) collective-permute-start(bf16[4,2,256,128]{3,2,1,0:T(8,128)(2,1)S(1)} %all_to_all.20.a_ref), channel_id=1, source_target_pairs={{0,1},{1,0},{2,3},{3,2},{4,5},{5,4},{6,7},{7,6},{8,9},{9,8},{10,11... | collective-permute-start | bytes 1572872 | tf_op jit(solution)/shard_map/ppermute | solution.py:366
  67.8 18.9 %all-to-all-start.3 = ((bf16[32,64,128]{2,1,0:T(8,128)(2,1)}), bf16[32,64,128]{2,1,0:T(8,128)(2,1)S(1)}, u32[]{:S(2)}, u32[]{:S(2)}) async-start(bf16[32,64,128]{2,1,0:T(8,128)(2,1)} %broadcast_in_dim.19), calls=%async_computation.3 | async-start | bytes 1048576 | tf_op jit(solution)/shard_map/all_to_all | solution.py:380

commit v3 on v2

--- a/solution.py
+++ b/solution.py
@@ -44,19 +44,30 @@
     return jnp.concatenate([up, down], axis=1)
 
 
-def pack_kernel(k_ref, v_ref, out_ref):
-    out_ref[:BLOCK, :] = k_ref[...]
-    out_ref[BLOCK:, :] = v_ref[...].T
+def pack_kernel(k_ref, v_ref, out_ref, key_scr, value_scr, sems):
+    key_copy = pltpu.make_async_copy(k_ref, key_scr, sems.at[0])
+    value_copy = pltpu.make_async_copy(v_ref, value_scr, sems.at[1])
+    value_copy.start()
+    key_copy.start()
+    value_copy.wait()
+    out_ref[BLOCK:, :] = value_scr[...].T
+    key_copy.wait()
+    out_ref[:BLOCK, :] = key_scr[...]
 
 
 def pack_call(k, v):
-    vmem = pl.BlockSpec(memory_space=pltpu.VMEM)
+    hbm = pl.BlockSpec(memory_space=pltpu.HBM)
     return pl.pallas_call(
         pack_kernel,
         out_shape=jax.ShapeDtypeStruct((2 * BLOCK, HEAD_DIM), BF16),
-        in_specs=[vmem] * 2,
-        out_specs=vmem,
-        compiler_params=pltpu.CompilerParams(vmem_limit_bytes=4 * 1024 * 1024),
+        in_specs=[hbm] * 2,
+        out_specs=pl.BlockSpec(memory_space=pltpu.VMEM),
+        scratch_shapes=[
+            pltpu.VMEM((BLOCK, HEAD_DIM), BF16),
+            pltpu.VMEM((BLOCK, HEAD_DIM), BF16),
+            pltpu.SemaphoreType.DMA((2,)),
+        ],
+        compiler_params=pltpu.CompilerParams(vmem_limit_bytes=56 * 1024 * 1024),
         name="pack_block",
     )(k, v)
 
@@ -74,12 +85,12 @@
 
 
 def local_kernel(
-    q_ref,
+    q_hbm,
+    qm_hbm,
+    km_hbm,
+    route_hbm,
+    doc_hbm,
     kv_ref,
-    qm_ref,
-    km_ref,
-    route_ref,
-    doc_ref,
     own_ref,
     near_ref,
     phi_ref,
@@ -87,7 +98,25 @@
     psi_ref,
     dest_ref,
     ok_ref,
+    q_ref,
+    qm_ref,
+    km_ref,
+    route_ref,
+    doc_ref,
+    sems,
 ):
+    pairs = (
+        (route_hbm, route_ref),
+        (doc_hbm, doc_ref),
+        (km_hbm, km_ref),
+        (qm_hbm, qm_ref),
+        (q_hbm, q_ref),
+    )
+    copies = [pltpu.make_async_copy(a, b, sems.at[n]) for n, (a, b) in enumerate(pairs)]
+    for copy in copies:
+        copy.start()
+    copies[0].wait()
+    copies[1].wait()
     keys = kv_ref[:BLOCK, :]
     values = with_ones(kv_ref[BLOCK:, :])
     col = lax.broadcasted_iota(jnp.int32, (BLOCK, BLOCK), 1)
@@ -95,8 +124,6 @@
     causal = row <= col
     near = causal & ((col < WINDOW) == (row < WINDOW))
     first_half = col < WINDOW
-    psi = two_softmax(dot(km_ref[...], keys, NT).reshape(HEADS, FEATURES, BLOCK))
-    psi_ref[...] = psi.reshape(ROWS, BLOCK).astype(BF16)
     z, y, c = lax.axis_index("z"), lax.axis_index("y"), lax.axis_index("c")
     here = shard_index()
     place = iota((2 * CHUNKS, 64), 0)
@@ -118,6 +145,11 @@
     tokens = (iota((64, BLOCK), 0) == lax.shift_right_logical(iota((64, BLOCK), 1), 1)).astype(BF16)
     placed = dot(dot(rows, pieces).astype(BF16), tokens)
     dest_ref[...] = jnp.where((row & 1) == (col & 1), placed, 0.0).astype(BF16)
+    copies[2].wait()
+    psi = two_softmax(dot(km_ref[...], keys, NT).reshape(HEADS, FEATURES, BLOCK))
+    psi_ref[...] = psi.reshape(ROWS, BLOCK).astype(BF16)
+    copies[3].wait()
+    copies[4].wait()
     for h in range(HEADS):
         at = h * BLOCK
         query = q_ref[:, at : at + BLOCK]
@@ -148,14 +180,22 @@
             jax.ShapeDtypeStruct((BLOCK, BLOCK), BF16),
             jax.ShapeDtypeStruct((2 * CHUNKS, BLOCK), F32),
         ),
-        in_specs=[vmem] * 6,
+        in_specs=[pl.BlockSpec(memory_space=pltpu.HBM)] * 5 + [vmem],
         out_specs=(vmem,) * 7,
-        compiler_params=pltpu.CompilerParams(vmem_limit_bytes=16 * 1024 * 1024),
+        scratch_shapes=[
+            pltpu.VMEM((BLOCK, ROWS), BF16),
+            pltpu.VMEM((HEADS * FEATURES, HEAD_DIM), BF16),
+            pltpu.VMEM((HEADS * FEATURES, HEAD_DIM), BF16),
+            pltpu.VMEM((64, 64), jnp.int32),
+            pltpu.VMEM((1, 64), jnp.int32),
+            pltpu.SemaphoreType.DMA((5,)),
+        ],
+        compiler_params=pltpu.CompilerParams(vmem_limit_bytes=56 * 1024 * 1024),
         cost_estimate=pl.CostEstimate(
             flops=400_000_000, bytes_accessed=4_000_000, transcendentals=500_000
         ),
         name="local_block",
-    )(q, kv, qm, km, routes, documents)
+    )(q, qm, km, routes, documents, kv)
 
 
 def main_kernel(
@@ -376,9 +416,13 @@
     relaid = got[:, :, :1024].reshape(1, BLOCK, 1024)
     part = jnp.sum(got[:, :, 1024:].astype(F32), axis=0).astype(BF16)
     part = part.reshape(16, 4, HEAD_DIM).transpose(1, 0, 2).reshape(FEATURES, HEAD_DIM)
-    part = jnp.broadcast_to(part[None], (32, FEATURES, HEAD_DIM))
-    got = lax.all_to_all(part, ("x", "y", "c"), 0, 0, tiled=True)
-    grad = jnp.sum(got.reshape(4, HEADS, FEATURES, HEAD_DIM).astype(F32), axis=0)
+    part = jnp.broadcast_to(part[None], (16, FEATURES, HEAD_DIM))
+    got = lax.all_to_all(part, ("x", "y"), 0, 0, tiled=True)
+    part = jnp.sum(got.reshape(4, 4, FEATURES, HEAD_DIM).astype(F32), axis=0).astype(BF16)
+    far = lax.ppermute(part, "c", [(0, 1), (1, 0)])
+    mine_first = lax.broadcasted_iota(jnp.int32, (4, 2, FEATURES, HEAD_DIM), 1) == c
+    grad = jnp.where(mine_first, part[:, None], far[:, None]).astype(F32)
+    grad = grad.reshape(HEADS, FEATURES, HEAD_DIM)
     return relaid, difference[None], jnp.swapaxes(grad, 1, 2)
 
 

time: 88 us -> 84.8 us (0.964)
  blocking collectives: 41.5 us -> 53.5 us
  waiting for transfers between devices: 13.8 us -> 2.47 us
  local copies, waits for them, and re-layouts: 6 us -> 1.25 us
  Pallas kernels: 9.42 us -> 14 us
  starting transfers between devices: 14.9 us -> 11.2 us
    all_to_all x0 -> x1, blocking collectives: none -> 12 us  [on_device(): got = lax.all_to_all(part, ('x', 'y'), 0, 0, tiled=True)]
    all_to_all x1 -> x0, waiting for transfers between devices: 10.9 us -> none  [on_device(): got = lax.all_to_all(part, ('x', 'y', 'c'), 0, 0, tiled=True)]
    all_to_all x1 -> x0, starting transfers between devices: 7.28 us -> none  [on_device(): got = lax.all_to_all(part, ('x', 'y', 'c'), 0, 0, tiled=True)]
    unnamed x18 -> x20, local copies, waits for them, and re-layouts: 4.03 us -> 0.05 us
    ppermute x0 -> x1, starting transfers between devices: none -> 3.59 us  [on_device(): far = lax.ppermute(part, 'c', [(0, 1), (1, 0)])]
    pallas_call x1, Pallas kernels: 1.94 us -> 5.21 us  [local_call(): pl.pallas_call(local_kernel, out_shape=(jax.ShapeDtypeStruct((BLOCK, ROWS...]
    pallas_call x1, Pallas kernels: 0.06 us -> 1.48 us  [pack_call(): pl.pallas_call(pack_kernel, out_shape=jax.ShapeDtypeStruct((2 * BLOCK, HE...]
  transfers between devices with their start and end apart: 4 -> 4, of which waited for: 3 -> 3; matrix products, arithmetic and copies ran while one was open for 1% -> 1% of each run, Pallas kernels for 2% -> 6%
where the time goes in v3:
time: 84.8 us; the launch traced here: 84.5 us
  blocking collectives  53.5 us (63%)
  Pallas kernels  14 us (17%)
  starting transfers between devices  11.2 us (13%)
  waiting for transfers between devices  2.47 us (3%)
  local copies, waits for them, and re-layouts  1.25 us (1%)
  other arithmetic  1.08 us (1%)
  between operations  0.89 us (1%)
    all_to_all x1, blocking collectives, on_device(): lax.all_to_all(jnp.concatenate([relay, part], axis=2), 'z', 0, 0, tiled=T...  18.3 us
    all_to_all x1, blocking collectives, on_device(): mine = lax.all_to_all(slots, 'y', 0, 0, tiled=True)  12.4 us
    all_to_all x1, blocking collectives, on_device(): got = lax.all_to_all(part, ('x', 'y'), 0, 0, tiled=True)  12 us
    all_to_all x1, blocking collectives, on_device(): got = lax.all_to_all(outgoing, ('y', 'c'), 0, 0, tiled=True)  10.8 us
    pallas_call x1, Pallas kernels, main_call(): pl.pallas_call(functools.partial(main_kernel, loss_scale), out_shape=(jax...  7.35 us
    pallas_call x1, Pallas kernels, local_call(): pl.pallas_call(local_kernel, out_shape=(jax.ShapeDtypeStruct((BLOCK, ROWS...  5.21 us
    ppermute x1, starting transfers between devices, on_device(): plane2 = lax.ppermute(kv, 'z', [(i, (i + 2) % 8) for i in range(8)])  3.9 us
    ppermute x1, starting transfers between devices, on_device(): far = lax.ppermute(part, 'c', [(0, 1), (1, 0)])  3.59 us
  transfers between devices with their start and end apart: 4, of which 3 were waited for; matrix products, arithmetic and copies ran while one was open for 1% of the time, Pallas kernels for 6%

profile of v3, /device:TPU:1, one launch (start us, length us, event | category | flops | bytes accessed | tf_op | source)
XLA Modules:
  0.0 84.5 jit_solution(17063279969875185576)
XLA Ops:
  0.6 1.5 %pack_block.1.kv_ref = bf16[256,128]{1,0:T(8,128)(2,1)} custom-call(bf16[128,128]{1,0:T(8,128)(2,1)} %bitcast.59, bf16[128,128]{1,0:T(8,128)(2,1)} %bitcast.60), custom_call_target="tpu_custom_call" | custom-call | tf_op jit(solution)/shard_map/pack_block/pallas_call | solution.py:60
  2.1 3.9 %collective-permute-start.1 = (bf16[256,128]{1,0:T(8,128)(2,1)}, bf16[256,128]{1,0:T(8,128)(2,1)S(1)}, u32[]{:S(2)}, u32[]{:S(2)}) collective-permute-start(bf16[256,128]{1,0:T(8,128)(2,1)} %pack_block.1.kv_ref), channel_id=1, source_target_pairs={{0,16},{8,24},{16,32},{24,40},{32,48},{40,56},{48,0},{56,8},{1,17}... | collective-permute-start | bytes 196616 | tf_op jit(solution)/shard_map/ppermute | solution.py:390
  6.0 1.6 %collective-permute-start = (bf16[256,128]{1,0:T(8,128)(2,1)}, bf16[256,128]{1,0:T(8,128)(2,1)S(1)}, u32[]{:S(2)}, u32[]{:S(2)}) collective-permute-start(bf16[256,128]{1,0:T(8,128)(2,1)} %pack_block.1.kv_ref), channel_id=1, source_target_pairs={{0,8},{8,16},{16,24},{24,32},{32,40},{40,48},{48,56},{56,0},{1,9},... | collective-permute-start | bytes 196616 | tf_op jit(solution)/shard_map/ppermute | solution.py:389
  7.7 0.0 copy-start
  7.7 5.2 %local_block.1 = (f32[128,1024]{1,0:T(8,128)}, f32[144,1024]{1,0:T(8,128)}, f32[1024,128]{1,0:T(8,128)}, bf16[2048,128]{1,0:T(8,128)(2,1)}, bf16[1024,128]{1,0:T...) custom-call(bf16[128,1024]{1,0:T(8,128)(2,1)} %bitcast.50, bf16[512,128]{1,0:T(8,128)(2,1)} %bitcast.61, ...), custom_call_target="tpu_custom_call" | custom-call | flops 400000000 | bytes 4000000 | tf_op jit(solution)/shard_map/local_block/pallas_call | solution.py:172
  12.9 0.0 collective-permute-done.1
  12.9 0.9 %collective-permute-done = bf16[256,128]{1,0:T(8,128)(2,1)S(1)} collective-permute-done((bf16[256,128]{1,0:T(8,128)(2,1)}, bf16[256,128]{1,0:T(8,128)(2,1)S(1)}, u32[]{:S(2)}, u32[]{:S(2)}) %collective-permute-start) | collective-permute-done | bytes 65568 | tf_op jit(solution)/shard_map/ppermute | solution.py:389
  13.7 0.0 copy-done
  13.8 0.0 copy-start.7
  13.8 0.0 copy-start.6
  13.9 0.0 copy-start.4
  13.9 0.0 copy-start.5
  13.9 0.1 pad_maximum_fusion
  14.0 0.0 copy-start.1
  14.0 0.0 copy-start.2
  14.0 0.0 copy-start.3
  14.0 0.0 copy-start.8
  14.0 0.0 copy-start.9
  14.0 12.4 %all_to_all.20.a_ref = bf16[4,2,256,128]{3,2,1,0:T(8,128)(2,1)S(1)} all-to-all(bf16[4,2,256,128]{3,2,1,0:T(8,128)(2,1)S(1)} %pad_maximum_fusion), channel_id=1, replica_groups=mesh['x'=4,'z'=8,'y'=4,'c'=2] {'y'}, dimensions={0} | all-to-all | bytes 1048576 | tf_op jit(solution)/shard_map/all_to_all | solution.py:405
  26.5 2.1 %collective-permute-start.2 = (bf16[4,2,256,128]{3,2,1,0:T(8,128)(2,1)S(1)}, bf16[4,2,256,128]{3,2,1,0:T(8,128)(2,1)S(1)}, u32[]{:S(2)}, u32[]{:S(2)}) collective-permute-start(bf16[4,2,256,128]{3,2,1,0:T(8,128)(2,1)S(1)} %all_to_all.20.a_ref), channel_id=1, source_target_pairs={{0,1},{1,0},{2,3},{3,2},{4,5},{5,4},{6,7},{7,6},{8,9},{9,8},{10,11... | collective-permute-start | bytes 1572872 | tf_op jit(solution)/shard_map/ppermute | solution.py:406
  28.6 1.5 %collective-permute-done.2.b_ref = bf16[4,2,256,128]{3,2,1,0:T(8,128)(2,1)S(1)} collective-permute-done((bf16[4,2,256,128]{3,2,1,0:T(8,128)(2,1)S(1)}, bf16[4,2,256,128]{3,2,1,0:T(8,128)(2,1)S(1)}, u32[]{:S(2)}, u32[]{:S(2)}) %collective-permute-start.2) | collective-permute-done | bytes 524320 | tf_op jit(solution)/shard_map/ppermute | solution.py:406
  30.1 0.0 copy-done.7
  30.1 0.0 copy-done.6
  30.1 0.0 copy-done.4
  30.1 0.0 copy-done.5
  30.1 0.0 copy-done.1
  30.2 0.0 copy-done.2
  30.2 0.0 copy-done.3
  30.2 0.0 copy-done.8
  30.2 0.0 copy-done.9
  30.2 7.3 %transfer.1 = (f32[128,1024]{1,0:T(8,128)}, bf16[8,16,1536]{2,1,0:T(8,128)(2,1)S(1)}) custom-call(bf16[128,1024]{1,0:T(8,128)(2,1)S(1)} %bitcast.51, bf16[256,128]{1,0:T(8,128)(2,1)S(1)} %copy-done, bf16[4,2,256,128]{3,2,1,0:T(8,128)(2,1)S(1)} %all_to_all.20.a_ref, bf16[4,2,256,128]{3,2,1,0:T(8,128)(2,1)S(1)} %collective-permute-done.2.b_ref, ...), custom_call_target="tpu_custom_call" | custom-call | flops 3000000000 | bytes 3000000 | tf_op jit(solution)/shard_map/transfer/pallas_call | solution.py:361
  37.5 10.8 %all_to_all.21 = bf16[8,16,1536]{2,1,0:T(8,128)(2,1)S(1)} all-to-all(bf16[8,16,1536]{2,1,0:T(8,128)(2,1)S(1)} %get-tuple-element.37), channel_id=1, replica_groups=mesh['x'=4,'z'=8,'y'=4,'c'=2] {'y','c'}, dimensions={0} | all-to-all | bytes 786432 | tf_op jit(solution)/shard_map/all_to_all | solution.py:411
  48.4 0.1 reshape.37
  48.5 0.1 copy.17
  48.7 0.1 copy.18
  48.8 18.3 %all_to_all.22 = bf16[8,16,1536]{2,1,0:T(8,128)(2,1)S(1)} all-to-all(bf16[8,16,1536]{2,1,0:T(8,128)(2,1)S(1)} %copy.18), channel_id=1, replica_groups=mesh['x'=4,'z'=8,'y'=4,'c'=2] {'z'}, dimensions={0} | all-to-all | bytes 786432 | tf_op jit(solution)/shard_map/all_to_all | solution.py:415
  67.2 12.0 %all_to_all.23 = bf16[16,64,128]{2,1,0:T(8,128)(2,1)S(1)} all-to-all(bf16[16,64,128]{2,1,0:T(8,128)(2,1)S(1)} %broadcast_in_dim.41), channel_id=1, replica_groups=mesh['x'=4,'z'=8,'y'=4,'c'=2] {'x','y'}, dimensions={0} | all-to-all | bytes 524288 | tf_op jit(solution)/shard_map/all_to_all | solution.py:420
  79.2 3.6 %collective-permute-start.3 = (bf16[4,64,128]{2,1,0:T(8,128)(2,1)S(1)}, bf16[4,64,128]{2,1,0:T(8,128)(2,1)S(1)}, u32[]{:S(2)}, u32[]{:S(2)}) collective-permute-start(bf16[4,64,128]{2,1,0:T(8,128)(2,1)S(1)} %reduce_sum.38), channel_id=1, source_target_pairs={{0,1},{1,0},{2,3},{3,2},{4,5},{5,4},{6,7},{7,6},{8,9},{9,8},{10,11... | collective-permute-start | bytes 196616 | tf_op jit(solution)/shard_map/ppermute | solution.py:422
  82.8 0.1 iota.12
  82.9 0.7 slice.18
  83.6 0.1 collective-permute-done.3
  83.7 0.8 convert_bitcast_fusion
  (14 shorter events, 0.3 us)
Async XLA Ops:
  2.1 10.8 %collective-permute-start.1 = (bf16[256,128]{1,0:T(8,128)(2,1)}, bf16[256,128]{1,0:T(8,128)(2,1)S(1)}, u32[]{:S(2)}, u32[]{:S(2)}) collective-permute-start(bf16[256,128]{1,0:T(8,128)(2,1)} %pack_block.1.kv_ref), channel_id=1, source_target_pairs={{0,16},{8,24},{16,32},{24,40},{32,48},{40,56},{48,0},{56,8},{1,17}... | collective-permute-start | bytes 196616 | tf_op jit(solution)/shard_map/ppermute | solution.py:390
  6.0 7.7 %collective-permute-start = (bf16[256,128]{1,0:T(8,128)(2,1)}, bf16[256,128]{1,0:T(8,128)(2,1)S(1)}, u32[]{:S(2)}, u32[]{:S(2)}) collective-permute-start(bf16[256,128]{1,0:T(8,128)(2,1)} %pack_block.1.kv_ref), channel_id=1, source_target_pairs={{0,8},{8,16},{16,24},{24,32},{32,40},{40,48},{48,56},{56,0},{1,9},... | collective-permute-start | bytes 196616 | tf_op jit(solution)/shard_map/ppermute | solution.py:389
  7.7 6.1 %copy-start = (bf16[256,128]{1,0:T(8,128)(2,1)S(1)}, bf16[256,128]{1,0:T(8,128)(2,1)}, u32[]{:S(2)}) copy-start(bf16[256,128]{1,0:T(8,128)(2,1)} %pack_block.1.kv_ref) | copy-start | bytes 196612
  13.8 16.3 %copy-start.7 = (bf16[1024,128]{1,0:T(8,128)(2,1)S(1)}, bf16[1024,128]{1,0:T(8,128)(2,1)}, u32[]{:S(2)}) copy-start(bf16[1024,128]{1,0:T(8,128)(2,1)} %get-tuple-element.34.psi_own_ref) | copy-start | bytes 786436
  13.8 16.3 %copy-start.6 = (bf16[2048,128]{1,0:T(8,128)(2,1)S(1)}, bf16[2048,128]{1,0:T(8,128)(2,1)}, u32[]{:S(2)}) copy-start(bf16[2048,128]{1,0:T(8,128)(2,1)} %get-tuple-element.33.both_ref) | copy-start | bytes 1572868
  13.9 16.2 %copy-start.4 = (f32[128,1024]{1,0:T(8,128)S(1)}, f32[128,1024]{1,0:T(8,128)}, u32[]{:S(2)}) copy-start(f32[128,1024]{1,0:T(8,128)} %get-tuple-element.30.own_ref) | copy-start | bytes 1572868
  13.9 16.2 %copy-start.5 = (f32[1024,128]{1,0:T(8,128)S(1)}, f32[1024,128]{1,0:T(8,128)}, u32[]{:S(2)}) copy-start(f32[1024,128]{1,0:T(8,128)} %get-tuple-element.32.phi_ref) | copy-start | bytes 1572868
  14.0 16.1 %copy-start.1 = (bf16[1,128,1024]{2,1,0:T(8,128)(2,1)S(1)}, bf16[1,128,1024]{2,1,0:T(8,128)(2,1)}, u32[]{:S(2)}) copy-start(bf16[1,128,1024]{2,1,0:T(8,128)(2,1)} %param.7) | copy-start | bytes 786436
  14.0 16.1 %copy-start.2 = (bf16[8,128,64]{1,2,0:T(8,128)(2,1)S(1)}, bf16[8,128,64]{1,2,0:T(8,128)(2,1)}, u32[]{:S(2)}) copy-start(bf16[8,128,64]{1,2,0:T(8,128)(2,1)} %param.11) | copy-start | bytes 393220
  14.0 16.1 %copy-start.3 = (f32[144,1024]{1,0:T(8,128)S(1)}, f32[144,1024]{1,0:T(8,128)}, u32[]{:S(2)}) copy-start(f32[144,1024]{1,0:T(8,128)} %get-tuple-element.31.near_ref) | copy-start | bytes 1769476
  14.0 16.1 %copy-start.8 = (bf16[128,128]{1,0:T(8,128)(2,1)S(1)}, bf16[128,128]{1,0:T(8,128)(2,1)}, u32[]{:S(2)}) copy-start(bf16[128,128]{1,0:T(8,128)(2,1)} %get-tuple-element.35.dest_ref) | copy-start | bytes 98308
  14.0 16.1 %copy-start.9 = (f32[16,128]{1,0:T(8,128)S(1)}, f32[16,128]{1,0:T(8,128)}, u32[]{:S(2)}) copy-start(f32[16,128]{1,0:T(8,128)} %get-tuple-element.36.ok_ref) | copy-start | bytes 24580
  26.5 3.7 %collective-permute-start.2 = (bf16[4,2,256,128]{3,2,1,0:T(8,128)(2,1)S(1)}, bf16[4,2,256,128]{3,2,1,0:T(8,128)(2,1)S(1)}, u32[]{:S(2)}, u32[]{:S(2)}) collective-permute-start(bf16[4,2,256,128]{3,2,1,0:T(8,128)(2,1)S(1)} %all_to_all.20.a_ref), channel_id=1, source_target_pairs={{0,1},{1,0},{2,3},{3,2},{4,5},{5,4},{6,7},{7,6},{8,9},{9,8},{10,11... | collective-permute-start | bytes 1572872 | tf_op jit(solution)/shard_map/ppermute | solution.py:406
  79.2 4.5 %collective-permute-start.3 = (bf16[4,64,128]{2,1,0:T(8,128)(2,1)S(1)}, bf16[4,64,128]{2,1,0:T(8,128)(2,1)S(1)}, u32[]{:S(2)}, u32[]{:S(2)}) collective-permute-start(bf16[4,64,128]{2,1,0:T(8,128)(2,1)S(1)} %reduce_sum.38), channel_id=1, source_target_pairs={{0,1},{1,0},{2,3},{3,2},{4,5},{5,4},{6,7},{7,6},{8,9},{9,8},{10,11... | collective-permute-start | bytes 196616 | tf_op jit(solution)/shard_map/ppermute | solution.py:422

commit v4 on v3

--- a/solution.py
+++ b/solution.py
@@ -44,36 +44,8 @@
     return jnp.concatenate([up, down], axis=1)
 
 
-def pack_kernel(k_ref, v_ref, out_ref, key_scr, value_scr, sems):
-    key_copy = pltpu.make_async_copy(k_ref, key_scr, sems.at[0])
-    value_copy = pltpu.make_async_copy(v_ref, value_scr, sems.at[1])
-    value_copy.start()
-    key_copy.start()
-    value_copy.wait()
-    out_ref[BLOCK:, :] = value_scr[...].T
-    key_copy.wait()
-    out_ref[:BLOCK, :] = key_scr[...]
-
-
-def pack_call(k, v):
-    hbm = pl.BlockSpec(memory_space=pltpu.HBM)
-    return pl.pallas_call(
-        pack_kernel,
-        out_shape=jax.ShapeDtypeStruct((2 * BLOCK, HEAD_DIM), BF16),
-        in_specs=[hbm] * 2,
-        out_specs=pl.BlockSpec(memory_space=pltpu.VMEM),
-        scratch_shapes=[
-            pltpu.VMEM((BLOCK, HEAD_DIM), BF16),
-            pltpu.VMEM((BLOCK, HEAD_DIM), BF16),
-            pltpu.SemaphoreType.DMA((2,)),
-        ],
-        compiler_params=pltpu.CompilerParams(vmem_limit_bytes=56 * 1024 * 1024),
-        name="pack_block",
-    )(k, v)
-
-
-def with_ones(values):
-    return jnp.concatenate([values, jnp.ones((TALL - HEAD_DIM, values.shape[1]), BF16)], axis=0)
+def in_hbm(x):
+    return pltpu.with_memory_space_constraint(x, pltpu.HBM)
 
 
 def shard_index():
@@ -90,7 +62,8 @@
     km_hbm,
     route_hbm,
     doc_hbm,
-    kv_ref,
+    k_hbm,
+    v_hbm,
     own_ref,
     near_ref,
     phi_ref,
@@ -103,11 +76,15 @@
     km_ref,
     route_ref,
     doc_ref,
+    k_ref,
+    v_ref,
     sems,
 ):
     pairs = (
         (route_hbm, route_ref),
         (doc_hbm, doc_ref),
+        (k_hbm, k_ref),
+        (v_hbm, v_ref),
         (km_hbm, km_ref),
         (qm_hbm, qm_ref),
         (q_hbm, q_ref),
@@ -117,8 +94,6 @@
         copy.start()
     copies[0].wait()
     copies[1].wait()
-    keys = kv_ref[:BLOCK, :]
-    values = with_ones(kv_ref[BLOCK:, :])
     col = lax.broadcasted_iota(jnp.int32, (BLOCK, BLOCK), 1)
     row = lax.broadcasted_iota(jnp.int32, (BLOCK, BLOCK), 0)
     causal = row <= col
@@ -145,11 +120,14 @@
     tokens = (iota((64, BLOCK), 0) == lax.shift_right_logical(iota((64, BLOCK), 1), 1)).astype(BF16)
     placed = dot(dot(rows, pieces).astype(BF16), tokens)
     dest_ref[...] = jnp.where((row & 1) == (col & 1), placed, 0.0).astype(BF16)
-    copies[2].wait()
+    for copy in copies[2:5]:
+        copy.wait()
+    keys = k_ref[...]
+    values = jnp.concatenate([v_ref[...], jnp.ones((BLOCK, BLOCK), BF16)], axis=1)
     psi = two_softmax(dot(km_ref[...], keys, NT).reshape(HEADS, FEATURES, BLOCK))
     psi_ref[...] = psi.reshape(ROWS, BLOCK).astype(BF16)
-    copies[3].wait()
-    copies[4].wait()
+    copies[5].wait()
+    copies[6].wait()
     for h in range(HEADS):
         at = h * BLOCK
         query = q_ref[:, at : at + BLOCK]
@@ -157,30 +135,30 @@
         own_ref[:, at : at + BLOCK] = jnp.where(causal, scores, NEGATIVE)
         window = jnp.where(near, scores * SCALE, NEGATIVE)
         weights = jnp.exp2(window - jnp.max(window, axis=0, keepdims=True))
-        near_ref[:, at : at + BLOCK] = dot(values, weights.astype(BF16))
+        near_ref[at : at + BLOCK, :] = dot(weights.T.astype(BF16), values)
         u = dot(qm_ref[h * FEATURES : (h + 1) * FEATURES, :], query, NT)
         phi = two_softmax(u[None])[0]
         phi_ref[at : at + BLOCK, :] = phi
         both = jnp.concatenate(
             [jnp.where(first_half, phi, 0.0), jnp.where(first_half, 0.0, phi)], axis=0
         )
-        both_ref[h * CHUNK : (h + 1) * CHUNK, :] = both.astype(BF16)
-
-
-def local_call(q, kv, qm, km, routes, documents):
+        both_ref[at : at + BLOCK, :] = both.T.astype(BF16)
+
+
+def local_call(q, k, v, qm, km, routes, documents):
     vmem = pl.BlockSpec(memory_space=pltpu.VMEM)
     return pl.pallas_call(
         local_kernel,
         out_shape=(
             jax.ShapeDtypeStruct((BLOCK, ROWS), F32),
-            jax.ShapeDtypeStruct((TALL, ROWS), F32),
+            jax.ShapeDtypeStruct((ROWS, CHUNK), F32),
             jax.ShapeDtypeStruct((ROWS, BLOCK), F32),
-            jax.ShapeDtypeStruct((2 * ROWS, BLOCK), BF16),
+            jax.ShapeDtypeStruct((ROWS, CHUNK), BF16),
             jax.ShapeDtypeStruct((ROWS, BLOCK), BF16),
             jax.ShapeDtypeStruct((BLOCK, BLOCK), BF16),
             jax.ShapeDtypeStruct((2 * CHUNKS, BLOCK), F32),
         ),
-        in_specs=[pl.BlockSpec(memory_space=pltpu.HBM)] * 5 + [vmem],
+        in_specs=[pl.BlockSpec(memory_space=pltpu.HBM)] * 7,
         out_specs=(vmem,) * 7,
         scratch_shapes=[
             pltpu.VMEM((BLOCK, ROWS), BF16),
@@ -188,20 +166,66 @@
             pltpu.VMEM((HEADS * FEATURES, HEAD_DIM), BF16),
             pltpu.VMEM((64, 64), jnp.int32),
             pltpu.VMEM((1, 64), jnp.int32),
-            pltpu.SemaphoreType.DMA((5,)),
+            pltpu.VMEM((BLOCK, HEAD_DIM), BF16),
+            pltpu.VMEM((BLOCK, HEAD_DIM), BF16),
+            pltpu.SemaphoreType.DMA((7,)),
         ],
-        compiler_params=pltpu.CompilerParams(vmem_limit_bytes=56 * 1024 * 1024),
+        compiler_params=pltpu.CompilerParams(vmem_limit_bytes=16 * 1024 * 1024),
         cost_estimate=pl.CostEstimate(
             flops=400_000_000, bytes_accessed=4_000_000, transcendentals=500_000
         ),
         name="local_block",
-    )(q, qm, km, routes, documents, kv)
+    )(*[in_hbm(each) for each in (q, qm, km, routes, documents, k, v)])
+
+
+def slot_kernel(k0_ref, v0_ref, k1_ref, v1_ref, k2_ref, v2_ref, out_ref):
+    y, c = lax.axis_index("y"), lax.axis_index("c")
+    planes = ((k0_ref, v0_ref), (k1_ref, v1_ref), (k2_ref, v2_ref))
+
+    def put(d, k, plane):
+        for n in range(2):
+            out_ref[d, k, n] = planes[plane][n][...]
+
+    for d in range(4):
+
+        @pl.when(d > y)
+        def _():
+            put(d, 0, 0)
+            put(d, 1, 1)
+
+        @pl.when(d < y)
+        def _():
+            put(d, 0, 1)
+            put(d, 1, 2)
+
+        @pl.when((d == y) & (c == 0))
+        def _():
+            put(d, 0, 0)
+            put(d, 1, 1)
+
+        @pl.when((d == y) & (c == 1))
+        def _():
+            put(d, 0, 2)
+            put(d, 1, 1)
+
+
+def slot_call(*blocks):
+    vmem = pl.BlockSpec(memory_space=pltpu.VMEM)
+    return pl.pallas_call(
+        slot_kernel,
+        out_shape=jax.ShapeDtypeStruct((4, 2, 2, BLOCK, HEAD_DIM), BF16),
+        in_specs=[vmem] * 6,
+        out_specs=vmem,
+        compiler_params=pltpu.CompilerParams(vmem_limit_bytes=8 * 1024 * 1024),
+        name="fill_slots",
+    )(*blocks)
 
 
 def main_kernel(
     loss_scale,
     q_ref,
-    kv_ref,
+    k_ref,
+    v_ref,
     a_ref,
     b_ref,
     km_ref,
@@ -219,8 +243,10 @@
     psi_scr,
     key_scr,
     vp_scr,
+    wide_scr,
 ):
-    first_key = kv_ref[0:1, :]
+    first_key = k_ref[0:1, :]
+    all_ones = jnp.ones((BLOCK, BLOCK), BF16)
     ones = jnp.ones((TALL - HEAD_DIM, BLOCK), BF16)
     for i in range(CHUNKS):
         src = a_ref if i < 4 else b_ref
@@ -229,15 +255,18 @@
             one = ok_ref[2 * i + k : 2 * i + k + 1, :]
             other = (1.0 - one).astype(BF16)
             one = one.astype(BF16)
-            key_scr[at : at + BLOCK, :] = src[i % 4, k, :BLOCK, :] * one + first_key * other
-            vp_scr[:HEAD_DIM, at : at + BLOCK] = src[i % 4, k, BLOCK:, :] * one
+            value = src[i % 4, k, 1] * one
+            key_scr[at : at + BLOCK, :] = src[i % 4, k, 0] * one + first_key * other
+            vp_scr[:HEAD_DIM, at : at + BLOCK] = value.T
             vp_scr[HEAD_DIM:, at : at + BLOCK] = ones * one
-    value_own = with_ones(kv_ref[BLOCK:, :])
-    vp_scr[:, FAR:] = value_own
-    early = lax.broadcasted_iota(jnp.int32, (TALL, BLOCK), 1) < WINDOW
-    value_early = jnp.where(early, value_own.astype(F32), 0.0).astype(BF16)
+            wide_scr[at : at + BLOCK, :BLOCK] = value
+            wide_scr[at : at + BLOCK, BLOCK:] = all_ones * one
+    vp_scr[:HEAD_DIM, FAR:] = v_ref[...].T
+    vp_scr[HEAD_DIM:, FAR:] = ones
+    early = lax.broadcasted_iota(jnp.int32, (BLOCK, CHUNK), 0) < WINDOW
+    value_early = jnp.concatenate([v_ref[...], all_ones], axis=1)
+    value_early = jnp.where(early, value_early.astype(F32), 0.0).astype(BF16)
     first_half = lax.broadcasted_iota(jnp.int32, (BLOCK, BLOCK), 1) < WINDOW
-    first_row = lax.broadcasted_iota(jnp.int32, (TALL - HEAD_DIM, CHUNK), 0) == 0
     dest = dest_ref[...]
 
     groups = HEADS // 2
@@ -278,9 +307,9 @@
     def mixes(g):
         mixed = dot(vp_scr[...], p_scr[g % 2])
         yield
-        state = dot(vp_scr[:, :FAR], psi_scr[g % 3], NT)
-        yield
-        late = state + dot(value_early, psi_own_ref[g * CHUNK : (g + 1) * CHUNK, :], NT)
+        state = dot(psi_scr[g % 3], wide_scr[...])
+        yield
+        late = state + dot(psi_own_ref[g * CHUNK : (g + 1) * CHUNK, :], value_early)
         sums[g] = (mixed, state.astype(BF16), late.astype(BF16))
         yield
 
@@ -288,28 +317,27 @@
         mixed, state, late = sums[g]
         heads = [2 * g, 2 * g + 1]
         parts = [slice(0, BLOCK), slice(BLOCK, CHUNK)]
-        wide = slice(g * CHUNK, (g + 1) * CHUNK)
-        states = [jnp.concatenate([state[:, p], late[:, p]], axis=1) for p in parts]
-        far = [dot(states[k], both_ref[heads[k] * CHUNK : (heads[k] + 1) * CHUNK, :]) for k in range(2)]
-        yield
-        total = jnp.concatenate(far, axis=1) + near_ref[:, wide]
+        states = [jnp.concatenate([state[p], late[p]], axis=0) for p in parts]
+        far = [dot(both_ref[h * BLOCK : (h + 1) * BLOCK, :], states[k]) for k, h in enumerate(heads)]
+        yield
+        total = jnp.concatenate(far, axis=0) + near_ref[g * CHUNK : (g + 1) * CHUNK, :]
         share = 1.0 / mixed[HEAD_DIM : HEAD_DIM + 1]
-        teacher = (mixed[:HEAD_DIM] * share).astype(BF16)
-        yield
-        moved = [dot(dest, teacher[:, p], NT) for p in parts]
-        inverse = 1.0 / total[HEAD_DIM : HEAD_DIM + 1]
-        student = total[:HEAD_DIM] * inverse
+        teacher = mixed[:HEAD_DIM] * share
+        teacher = jnp.concatenate([teacher[:, p].T for p in parts], axis=0).astype(BF16)
+        yield
+        moved = [dot(dest, teacher[p]) for p in parts]
+        inverse = 1.0 / total[:, HEAD_DIM:]
+        student = total[:, :HEAD_DIM] * inverse
         gap = student - teacher.astype(F32)
+        for k in range(2):
+            diff_ref[:, heads[k] * BLOCK : (heads[k] + 1) * BLOCK] = gap[parts[k]]
         yield
         grad_out = gap * (inverse * (2.0 * loss_scale))
-        drop = jnp.sum(grad_out * student, axis=0, keepdims=True)
-        drop = jnp.where(first_row, -drop, 0.0).astype(BF16)
-        grad_both = jnp.concatenate([grad_out.astype(BF16), drop], axis=0)
-        yield
-        dphi = [dot(states[k], grad_both[:, parts[k]], TN) for k in range(2)]
+        grad_both = jnp.concatenate([grad_out, -grad_out * student], axis=1).astype(BF16)
+        yield
+        dphi = [dot(states[k], grad_both[parts[k]], NT) for k in range(2)]
         yield
         for k in range(2):
-            diff_ref[:, heads[k] * BLOCK : (heads[k] + 1) * BLOCK] = gap[:, parts[k]].T
             for shard in range(8):
                 buf_ref[shard, :, heads[k] * BLOCK : (heads[k] + 1) * BLOCK] = moved[k][
                     shard * 16 : (shard + 1) * 16
@@ -356,7 +384,7 @@
                 pass
 
 
-def main_call(loss_scale, q, kv, a, b, km, local):
+def main_call(loss_scale, q, k, v, a, b, km, local):
     vmem = pl.BlockSpec(memory_space=pltpu.VMEM)
     return pl.pallas_call(
         functools.partial(main_kernel, loss_scale),
@@ -364,7 +392,7 @@
             jax.ShapeDtypeStruct((BLOCK, HEADS * HEAD_DIM), F32),
             jax.ShapeDtypeStruct((8, 16, 1536), BF16),
         ),
-        in_specs=[vmem] * 12,
+        in_specs=[vmem] * 13,
         out_specs=(vmem, vmem),
         scratch_shapes=[
             pltpu.VMEM((2, FAR, CHUNK), F32),
@@ -372,41 +400,36 @@
             pltpu.VMEM((3, CHUNK, FAR), BF16),
             pltpu.VMEM((FAR, BLOCK), BF16),
             pltpu.VMEM((TALL, FAR + BLOCK), BF16),
+            pltpu.VMEM((FAR, CHUNK), BF16),
         ],
         compiler_params=pltpu.CompilerParams(vmem_limit_bytes=32 * 1024 * 1024),
         cost_estimate=pl.CostEstimate(
             flops=3_000_000_000, bytes_accessed=3_000_000, transcendentals=4_000_000
         ),
         name="transfer",
-    )(q, kv, a, b, km, *local)
+    )(q, k, v, a, b, km, *local)
 
 
 def on_device(queries, keys, values, query_map, key_map, documents, assignment):
-    y, c = lax.axis_index("y"), lax.axis_index("c")
+    c = lax.axis_index("c")
     query_rows = jnp.swapaxes(query_map, 1, 2).reshape(HEADS * FEATURES, HEAD_DIM)
     key_rows = jnp.swapaxes(key_map, 1, 2).reshape(HEADS * FEATURES, HEAD_DIM)
-    kv = pack_call(keys[0], values[0])
-    plane1 = lax.ppermute(kv, "z", [(i, (i + 1) % 8) for i in range(8)])
-    plane2 = lax.ppermute(kv, "z", [(i, (i + 2) % 8) for i in range(8)])
-    local = local_call(queries[0], kv, query_rows, key_rows, assignment[0], documents)
+    shift1 = [(i, (i + 1) % 8) for i in range(8)]
+    shift2 = [(i, (i + 2) % 8) for i in range(8)]
+    plane0 = (keys[0], values[0])
+    plane2 = tuple(lax.ppermute(each, "z", shift2) for each in plane0)
+    plane1 = tuple(lax.ppermute(each, "z", shift1) for each in plane0)
+    local = local_call(
+        queries[0], keys[0], values[0], query_rows, key_rows, assignment[0], documents
+    )
     plane1, plane2, local = lax.optimization_barrier((plane1, plane2, local))
-    own = jnp.where(c == 1, plane2, kv)
-    slots = jnp.stack(
-        [
-            jnp.stack(
-                [
-                    jnp.where(d > y, kv, jnp.where(d < y, plane1, own)),
-                    jnp.where(d < y, plane2, plane1),
-                ]
-            )
-            for d in range(4)
-        ]
-    )
+
+    slots = slot_call(*plane0, *plane1, *plane2)
     mine = lax.all_to_all(slots, "y", 0, 0, tiled=True)
     other = lax.ppermute(mine, "c", [(0, 1), (1, 0)])
     loss_scale = HEAD_DIM / math.sqrt(4 * 64 * BLOCK)
     difference, outgoing = main_call(
-        loss_scale, queries[0], kv, mine, other, key_rows, local
+        loss_scale, queries[0], keys[0], values[0], mine, other, key_rows, local
     )
     got = lax.all_to_all(outgoing, ("y", "c"), 0, 0, tiled=True)
     relay = got[:, :, :1024].reshape(8, 8, 2, 1024).transpose(1, 0, 2, 3).reshape(8, 16, 1024)

time: 84.8 us -> 84.4 us (level)
  blocking collectives: 53.5 us -> 38 us
  starting transfers between devices: 11.2 us -> 22 us
  waiting for transfers between devices: 2.47 us -> 9.36 us
  Pallas kernels: 14 us -> 11.1 us
    all_to_all x1 -> x0, blocking collectives: 12 us -> none  [on_device(): got = lax.all_to_all(part, ('x', 'y'), 0, 0, tiled=True)]
    all_to_all x0 -> x1, waiting for transfers between devices: none -> 7.47 us  [on_device(): got = lax.all_to_all(part, ('x', 'y'), 0, 0, tiled=True)]
    all_to_all x0 -> x1, starting transfers between devices: none -> 4.73 us  [on_device(): got = lax.all_to_all(part, ('x', 'y'), 0, 0, tiled=True)]
    ppermute x2 -> x4, starting transfers between devices: 5.53 us -> 9.58 us  [the longest x2 5.39 us: on_device(): plane1 = tuple((lax.ppermute(each, 'z', shift1) for each in plane0))]
    all_to_all x1, blocking collectives: 18.3 us -> 16.2 us  [on_device(): lax.all_to_all(jnp.concatenate([relay, part], axis=2), 'z', 0, 0, tiled=T...]
    ppermute x1, starting transfers between devices: 2.12 us -> 4.09 us  [on_device(): other = lax.ppermute(mine, 'c', [(0, 1), (1, 0)])]
    pallas_call x1, Pallas kernels: 5.21 us -> 3.57 us  [local_call(): pl.pallas_call(local_kernel, out_shape=(jax.ShapeDtypeStruct((BLOCK, ROWS...]
    pallas_call x1, Pallas kernels: 1.48 us -> 0.07 us  [slot_call(): pl.pallas_call(slot_kernel, out_shape=jax.ShapeDtypeStruct((4, 2, 2, BLOC...]
  transfers between devices with their start and end apart: 4 -> 7, of which waited for: 3 -> 4; matrix products, arithmetic and copies ran while one was open for 1% -> 1% of each run, Pallas kernels for 6% -> 4%
where the time goes in v4:
time: 84.4 us; the launch traced here: 84.1 us
  blocking collectives  38 us (45%)
  starting transfers between devices  22 us (26%)
  Pallas kernels  11.1 us (13%)
  waiting for transfers between devices  9.36 us (11%)
  local copies, waits for them, and re-layouts  1.93 us (2%)
  other arithmetic  0.91 us (1%)
    all_to_all x1, blocking collectives, on_device(): lax.all_to_all(jnp.concatenate([relay, part], axis=2), 'z', 0, 0, tiled=T...  16.2 us
    all_to_all x1, blocking collectives, on_device(): mine = lax.all_to_all(slots, 'y', 0, 0, tiled=True)  11.1 us
    all_to_all x1, blocking collectives, on_device(): got = lax.all_to_all(outgoing, ('y', 'c'), 0, 0, tiled=True)  10.8 us
    all_to_all x1, waiting for transfers between devices, on_device(): got = lax.all_to_all(part, ('x', 'y'), 0, 0, tiled=True)  7.47 us
    pallas_call x1, Pallas kernels, main_call(): pl.pallas_call(functools.partial(main_kernel, loss_scale), out_shape=(jax...  7.43 us
    ppermute x2, starting transfers between devices, on_device(): plane1 = tuple((lax.ppermute(each, 'z', shift1) for each in plane0))  5.39 us
    all_to_all x1, starting transfers between devices, on_device(): got = lax.all_to_all(part, ('x', 'y'), 0, 0, tiled=True)  4.73 us
    ppermute x2, starting transfers between devices, on_device(): plane2 = tuple((lax.ppermute(each, 'z', shift2) for each in plane0))  4.18 us
  transfers between devices with their start and end apart: 7, of which 4 were waited for; matrix products, arithmetic and copies ran while one was open for 1% of the time, Pallas kernels for 4%

profile of v4, /device:TPU:1, one launch (start us, length us, event | category | flops | bytes accessed | tf_op | source)
XLA Modules:
  0.0 84.1 jit_solution(12380599668316914255)
XLA Ops:
  0.6 2.5 %collective-permute-start = (bf16[128,128]{1,0:T(8,128)(2,1)}, bf16[128,128]{1,0:T(8,128)(2,1)S(1)}, u32[]{:S(2)}, u32[]{:S(2)}) collective-permute-start(bf16[128,128]{1,0:T(8,128)(2,1)} %bitcast.26), channel_id=1, source_target_pairs={{0,8},{8,16},{16,24},{24,32},{32,40},{40,48},{48,56},{56,0},{1,9},... | collective-permute-start | bytes 98312 | tf_op jit(solution)/shard_map/ppermute | solution.py:421
  3.2 3.0 %collective-permute-start.2 = (bf16[128,128]{1,0:T(8,128)(2,1)}, bf16[128,128]{1,0:T(8,128)(2,1)S(1)}, u32[]{:S(2)}, u32[]{:S(2)}) collective-permute-start(bf16[128,128]{1,0:T(8,128)(2,1)} %bitcast.27), channel_id=1, source_target_pairs={{0,16},{8,24},{16,32},{24,40},{32,48},{40,56},{48,0},{56,8},{1,17}... | collective-permute-start | bytes 98312 | tf_op jit(solution)/shard_map/ppermute | solution.py:420
  6.2 2.8 %collective-permute-start.1 = (bf16[128,128]{1,0:T(8,128)(2,1)}, bf16[128,128]{1,0:T(8,128)(2,1)S(1)}, u32[]{:S(2)}, u32[]{:S(2)}) collective-permute-start(bf16[128,128]{1,0:T(8,128)(2,1)} %bitcast.31), channel_id=1, source_target_pairs={{0,8},{8,16},{16,24},{24,32},{32,40},{40,48},{48,56},{56,0},{1,9},... | collective-permute-start | bytes 98312 | tf_op jit(solution)/shard_map/ppermute | solution.py:421
  9.0 1.2 %collective-permute-start.3 = (bf16[128,128]{1,0:T(8,128)(2,1)}, bf16[128,128]{1,0:T(8,128)(2,1)S(1)}, u32[]{:S(2)}, u32[]{:S(2)}) collective-permute-start(bf16[128,128]{1,0:T(8,128)(2,1)} %bitcast.32), channel_id=1, source_target_pairs={{0,16},{8,24},{16,32},{24,40},{32,48},{40,56},{48,0},{56,8},{1,17}... | collective-permute-start | bytes 98312 | tf_op jit(solution)/shard_map/ppermute | solution.py:420
  10.2 0.0 copy-start
  10.2 0.0 copy-start.1
  10.2 3.6 %local_block.1 = (f32[128,1024]{1,0:T(8,128)S(1)}, f32[1024,256]{1,0:T(8,128)S(1)}, f32[1024,128]{1,0:T(8,128)S(1)}, bf16[1024,256]{1,0:T(8,128)(2,1)S(1)}, bf16...) custom-call(bf16[128,1024]{1,0:T(8,128)(2,1)} %bitcast.36, ...), custom_call_target="tpu_custom_call" | custom-call | flops 400000000 | bytes 4000000 | tf_op jit(solution)/shard_map/local_block/pallas_call | solution.py:150
  13.8 0.0 collective-permute-done.k1_ref
  13.8 0.0 collective-permute-done.1.v1_ref
  13.8 0.0 collective-permute-done.2.k2_ref
  13.8 0.3 collective-permute-done.3.v2_ref
  14.1 0.0 copy-done
  14.1 0.0 copy-done.1
  14.1 0.1 fill_slots.1
  14.2 0.0 copy-start.2
  14.2 0.0 copy-start.3
  14.2 11.1 %all_to_all.20.a_ref = bf16[4,2,2,128,128]{4,3,2,1,0:T(8,128)(2,1)S(1)} all-to-all(bf16[4,2,2,128,128]{4,3,2,1,0:T(8,128)(2,1)S(1)} %fill_slots.1), channel_id=1, replica_groups=mesh['x'=4,'z'=8,'y'=4,'c'=2] {'y'}, dimensions={0} | all-to-all | bytes 1048576 | tf_op jit(solution)/shard_map/all_to_all | solution.py:428
  25.3 4.1 %collective-permute-start.4 = (bf16[4,2,2,128,128]{4,3,2,1,0:T(8,128)(2,1)S(1)}, bf16[4,2,2,128,128]{4,3,2,1,0:T(8,128)(2,1)S(1)}, u32[]{:S(2)}, u32[]{:S(2)}) collective-permute-start(bf16[4,2,2,128,128]{4,3,2,1,0:T(8,128)(2,1)S(1)} %all_to_all.20.a_ref), channel_id=1, source_target_pairs={{0,1},{1,0},{2,3},{3,2},{4,5},{5,4},{6,7},{7,6},{8,9},{9,8},{10,11... | collective-permute-start | bytes 1572872 | tf_op jit(solution)/shard_map/ppermute | solution.py:429
  29.4 1.5 %collective-permute-done.4.b_ref = bf16[4,2,2,128,128]{4,3,2,1,0:T(8,128)(2,1)S(1)} collective-permute-done((bf16[4,2,2,128,128]{4,3,2,1,0:T(8,128)(2,1)S(1)}, bf16[4,2,2,128,128]{4,3,2,1,0:T(8,128)(2,1)S(1)}, u32[]{:S(2)}, u32[]{:S(2)}) %collective-permute-start.4) | collective-permute-done | bytes 524320 | tf_op jit(solution)/shard_map/ppermute | solution.py:429
  30.9 0.0 copy-done.2
  30.9 0.0 copy-done.3
  30.9 7.4 %transfer.1 = (f32[128,1024]{1,0:T(8,128)}, bf16[8,16,1536]{2,1,0:T(8,128)(2,1)S(1)}) custom-call(bf16[128,1024]{1,0:T(8,128)(2,1)S(1)} %bitcast.37, bf16[128,128]{1,0:T(8,128)(2,1)S(1)} %bitcast.30, bf16[128,128]{1,0:T(8,128)(2,1)S(1)} %bitcast.35, bf16[4,2,2,128,128]{4,3,2,1,0:T(8,128)(2,1)S(1)} %all_to_all.20.a_ref, ...), custom_call_target="tpu_custom_call" | custom-call | flops 3000000000 | bytes 3000000 | tf_op jit(solution)/shard_map/transfer/pallas_call | solution.py:389
  38.3 10.8 %all_to_all.21 = bf16[8,16,1536]{2,1,0:T(8,128)(2,1)S(1)} all-to-all(bf16[8,16,1536]{2,1,0:T(8,128)(2,1)S(1)} %get-tuple-element.41), channel_id=1, replica_groups=mesh['x'=4,'z'=8,'y'=4,'c'=2] {'y','c'}, dimensions={0} | all-to-all | bytes 786432 | tf_op jit(solution)/shard_map/all_to_all | solution.py:434
  49.2 0.1 reshape.37
  49.3 0.1 copy.17
  49.5 0.1 copy.18
  49.6 16.2 %all_to_all.22 = bf16[8,16,1536]{2,1,0:T(8,128)(2,1)S(1)} all-to-all(bf16[8,16,1536]{2,1,0:T(8,128)(2,1)S(1)} %copy.18), channel_id=1, replica_groups=mesh['x'=4,'z'=8,'y'=4,'c'=2] {'z'}, dimensions={0} | all-to-all | bytes 786432 | tf_op jit(solution)/shard_map/all_to_all | solution.py:438
  65.8 0.8 broadcast_in_dim.41
  66.6 4.7 %all-to-all-start.3 = ((bf16[16,64,128]{2,1,0:T(8,128)(2,1)}), bf16[16,64,128]{2,1,0:T(8,128)(2,1)S(1)}, u32[]{:S(2)}, u32[]{:S(2)}) async-start(bf16[16,64,128]{2,1,0:T(8,128)(2,1)} %broadcast_in_dim.41), calls=%async_computation.3 | async-start | bytes 524288 | tf_op jit(solution)/shard_map/all_to_all | solution.py:443
  71.3 7.5 %all-to-all-done.3 = bf16[16,64,128]{2,1,0:T(8,128)(2,1)S(1)} async-done(((bf16[16,64,128]{2,1,0:T(8,128)(2,1)}), bf16[16,64,128]{2,1,0:T(8,128)(2,1)S(1)}, u32[]{:S(2)}, u32[]{:S(2)}) %all-to-all-start.3) | async-done | bytes 262176 | tf_op jit(solution)/shard_map/all_to_all | solution.py:443
  78.8 3.6 %collective-permute-start.5 = (bf16[4,64,128]{2,1,0:T(8,128)(2,1)S(1)}, bf16[4,64,128]{2,1,0:T(8,128)(2,1)S(1)}, u32[]{:S(2)}, u32[]{:S(2)}) collective-permute-start(bf16[4,64,128]{2,1,0:T(8,128)(2,1)S(1)} %reduce_sum.38), channel_id=1, source_target_pairs={{0,1},{1,0},{2,3},{3,2},{4,5},{5,4},{6,7},{7,6},{8,9},{9,8},{10,11... | collective-permute-start | bytes 196616 | tf_op jit(solution)/shard_map/ppermute | solution.py:445
  82.4 0.1 iota.12
  82.5 0.7 slice.18
  83.2 0.1 collective-permute-done.5
  83.3 0.8 convert_bitcast_fusion
  (10 shorter events, 0.2 us)
Async XLA Ops:
  0.6 13.2 %collective-permute-start = (bf16[128,128]{1,0:T(8,128)(2,1)}, bf16[128,128]{1,0:T(8,128)(2,1)S(1)}, u32[]{:S(2)}, u32[]{:S(2)}) collective-permute-start(bf16[128,128]{1,0:T(8,128)(2,1)} %bitcast.26), channel_id=1, source_target_pairs={{0,8},{8,16},{16,24},{24,32},{32,40},{40,48},{48,56},{56,0},{1,9},... | collective-permute-start | bytes 98312 | tf_op jit(solution)/shard_map/ppermute | solution.py:421
  3.2 10.6 %collective-permute-start.2 = (bf16[128,128]{1,0:T(8,128)(2,1)}, bf16[128,128]{1,0:T(8,128)(2,1)S(1)}, u32[]{:S(2)}, u32[]{:S(2)}) collective-permute-start(bf16[128,128]{1,0:T(8,128)(2,1)} %bitcast.27), channel_id=1, source_target_pairs={{0,16},{8,24},{16,32},{24,40},{32,48},{40,56},{48,0},{56,8},{1,17}... | collective-permute-start | bytes 98312 | tf_op jit(solution)/shard_map/ppermute | solution.py:420
  6.2 7.6 %collective-permute-start.1 = (bf16[128,128]{1,0:T(8,128)(2,1)}, bf16[128,128]{1,0:T(8,128)(2,1)S(1)}, u32[]{:S(2)}, u32[]{:S(2)}) collective-permute-start(bf16[128,128]{1,0:T(8,128)(2,1)} %bitcast.31), channel_id=1, source_target_pairs={{0,8},{8,16},{16,24},{24,32},{32,40},{40,48},{48,56},{56,0},{1,9},... | collective-permute-start | bytes 98312 | tf_op jit(solution)/shard_map/ppermute | solution.py:421
  9.0 5.1 %collective-permute-start.3 = (bf16[128,128]{1,0:T(8,128)(2,1)}, bf16[128,128]{1,0:T(8,128)(2,1)S(1)}, u32[]{:S(2)}, u32[]{:S(2)}) collective-permute-start(bf16[128,128]{1,0:T(8,128)(2,1)} %bitcast.32), channel_id=1, source_target_pairs={{0,16},{8,24},{16,32},{24,40},{32,48},{40,56},{48,0},{56,8},{1,17}... | collective-permute-start | bytes 98312 | tf_op jit(solution)/shard_map/ppermute | solution.py:420
  10.2 3.9 %copy-start = (bf16[1,128,128]{2,1,0:T(8,128)(2,1)S(1)}, bf16[1,128,128]{2,1,0:T(8,128)(2,1)}, u32[]{:S(2)}) copy-start(bf16[1,128,128]{2,1,0:T(8,128)(2,1)} %param.8) | copy-start | bytes 98308
  10.2 3.9 %copy-start.1 = (bf16[1,128,128]{2,1,0:T(8,128)(2,1)S(1)}, bf16[1,128,128]{2,1,0:T(8,128)(2,1)}, u32[]{:S(2)}) copy-start(bf16[1,128,128]{2,1,0:T(8,128)(2,1)} %param.9) | copy-start | bytes 98308
  14.2 16.7 %copy-start.2 = (bf16[1,128,1024]{2,1,0:T(8,128)(2,1)S(1)}, bf16[1,128,1024]{2,1,0:T(8,128)(2,1)}, u32[]{:S(2)}) copy-start(bf16[1,128,1024]{2,1,0:T(8,128)(2,1)} %param.7) | copy-start | bytes 786436
  14.2 16.7 %copy-start.3 = (bf16[8,128,64]{1,2,0:T(8,128)(2,1)S(1)}, bf16[8,128,64]{1,2,0:T(8,128)(2,1)}, u32[]{:S(2)}) copy-start(bf16[8,128,64]{1,2,0:T(8,128)(2,1)} %param.11) | copy-start | bytes 393220
  25.3 5.6 %collective-permute-start.4 = (bf16[4,2,2,128,128]{4,3,2,1,0:T(8,128)(2,1)S(1)}, bf16[4,2,2,128,128]{4,3,2,1,0:T(8,128)(2,1)S(1)}, u32[]{:S(2)}, u32[]{:S(2)}) collective-permute-start(bf16[4,2,2,128,128]{4,3,2,1,0:T(8,128)(2,1)S(1)} %all_to_all.20.a_ref), channel_id=1, source_target_pairs={{0,1},{1,0},{2,3},{3,2},{4,5},{5,4},{6,7},{7,6},{8,9},{9,8},{10,11... | collective-permute-start | bytes 1572872 | tf_op jit(solution)/shard_map/ppermute | solution.py:429
  66.6 12.2 %all-to-all-start.3 = ((bf16[16,64,128]{2,1,0:T(8,128)(2,1)}), bf16[16,64,128]{2,1,0:T(8,128)(2,1)S(1)}, u32[]{:S(2)}, u32[]{:S(2)}) async-start(bf16[16,64,128]{2,1,0:T(8,128)(2,1)} %broadcast_in_dim.41), calls=%async_computation.3 | async-start | bytes 524288 | tf_op jit(solution)/shard_map/all_to_all | solution.py:443
  78.8 4.5 %collective-permute-start.5 = (bf16[4,64,128]{2,1,0:T(8,128)(2,1)S(1)}, bf16[4,64,128]{2,1,0:T(8,128)(2,1)S(1)}, u32[]{:S(2)}, u32[]{:S(2)}) collective-permute-start(bf16[4,64,128]{2,1,0:T(8,128)(2,1)S(1)} %reduce_sum.38), channel_id=1, source_target_pairs={{0,1},{1,0},{2,3},{3,2},{4,5},{5,4},{6,7},{7,6},{8,9},{9,8},{10,11... | collective-permute-start | bytes 196616 | tf_op jit(solution)/shard_map/ppermute | solution.py:445

commit v5 on v4

--- a/solution.py
+++ b/solution.py
@@ -48,59 +48,21 @@
     return pltpu.with_memory_space_constraint(x, pltpu.HBM)
 
 
-def shard_index():
-    return (lax.axis_index("z") * 4 + lax.axis_index("y")) * 2 + lax.axis_index("c")
-
-
 def iota(shape, axis):
     return lax.broadcasted_iota(jnp.int32, shape, axis)
 
 
-def local_kernel(
-    q_hbm,
-    qm_hbm,
-    km_hbm,
-    route_hbm,
-    doc_hbm,
-    k_hbm,
-    v_hbm,
-    own_ref,
-    near_ref,
-    phi_ref,
-    both_ref,
-    psi_ref,
-    dest_ref,
-    ok_ref,
-    q_ref,
-    qm_ref,
-    km_ref,
-    route_ref,
-    doc_ref,
-    k_ref,
-    v_ref,
-    sems,
+def place_kernel(
+    km_hbm, route_hbm, doc_hbm, k_hbm, psi_ref, dest_ref, ok_ref, km_ref, route_ref, doc_ref, k_ref, sems
 ):
-    pairs = (
-        (route_hbm, route_ref),
-        (doc_hbm, doc_ref),
-        (k_hbm, k_ref),
-        (v_hbm, v_ref),
-        (km_hbm, km_ref),
-        (qm_hbm, qm_ref),
-        (q_hbm, q_ref),
-    )
+    pairs = ((route_hbm, route_ref), (doc_hbm, doc_ref), (k_hbm, k_ref), (km_hbm, km_ref))
     copies = [pltpu.make_async_copy(a, b, sems.at[n]) for n, (a, b) in enumerate(pairs)]
     for copy in copies:
         copy.start()
     copies[0].wait()
     copies[1].wait()
-    col = lax.broadcasted_iota(jnp.int32, (BLOCK, BLOCK), 1)
-    row = lax.broadcasted_iota(jnp.int32, (BLOCK, BLOCK), 0)
-    causal = row <= col
-    near = causal & ((col < WINDOW) == (row < WINDOW))
-    first_half = col < WINDOW
     z, y, c = lax.axis_index("z"), lax.axis_index("y"), lax.axis_index("c")
-    here = shard_index()
+    here = (z * 4 + y) * 2 + c
     place = iota((2 * CHUNKS, 64), 0)
     block = iota((2 * CHUNKS, 64), 1)
     from_y = lax.shift_right_logical(place, 1) & 3
@@ -119,15 +81,48 @@
     rows = (lax.shift_right_logical(iota((BLOCK, 64), 0), 1) == iota((BLOCK, 64), 1)).astype(BF16)
     tokens = (iota((64, BLOCK), 0) == lax.shift_right_logical(iota((64, BLOCK), 1), 1)).astype(BF16)
     placed = dot(dot(rows, pieces).astype(BF16), tokens)
-    dest_ref[...] = jnp.where((row & 1) == (col & 1), placed, 0.0).astype(BF16)
-    for copy in copies[2:5]:
-        copy.wait()
+    parity = (iota((BLOCK, BLOCK), 0) & 1) == (iota((BLOCK, BLOCK), 1) & 1)
+    dest_ref[...] = jnp.where(parity, placed, 0.0).astype(BF16)
+    copies[2].wait()
+    copies[3].wait()
+    psi = two_softmax(dot(km_ref[...], k_ref[...], NT).reshape(HEADS, FEATURES, BLOCK))
+    psi_ref[...] = psi.reshape(ROWS, BLOCK).astype(BF16)
+
+
+def place_call(k, km, routes, documents):
+    vmem = pl.BlockSpec(memory_space=pltpu.VMEM)
+    return pl.pallas_call(
+        place_kernel,
+        out_shape=(
+            jax.ShapeDtypeStruct((ROWS, BLOCK), BF16),
+            jax.ShapeDtypeStruct((BLOCK, BLOCK), BF16),
+            jax.ShapeDtypeStruct((2 * CHUNKS, BLOCK), F32),
+        ),
+        in_specs=[pl.BlockSpec(memory_space=pltpu.HBM)] * 4,
+        out_specs=(vmem,) * 3,
+        scratch_shapes=[
+            pltpu.VMEM((HEADS * FEATURES, HEAD_DIM), BF16),
+            pltpu.VMEM((64, 64), jnp.int32),
+            pltpu.VMEM((1, 64), jnp.int32),
+            pltpu.VMEM((BLOCK, HEAD_DIM), BF16),
+            pltpu.SemaphoreType.DMA((4,)),
+        ],
+        compiler_params=pltpu.CompilerParams(vmem_limit_bytes=8 * 1024 * 1024),
+        cost_estimate=pl.CostEstimate(
+            flops=100_000_000, bytes_accessed=1_000_000, transcendentals=200_000
+        ),
+        name="place",
+    )(*[in_hbm(each) for each in (km, routes, documents, k)])
+
+
+def local_kernel(q_ref, k_ref, v_ref, qm_ref, own_ref, near_ref, phi_ref, both_ref):
     keys = k_ref[...]
     values = jnp.concatenate([v_ref[...], jnp.ones((BLOCK, BLOCK), BF16)], axis=1)
-    psi = two_softmax(dot(km_ref[...], keys, NT).reshape(HEADS, FEATURES, BLOCK))
-    psi_ref[...] = psi.reshape(ROWS, BLOCK).astype(BF16)
-    copies[5].wait()
-    copies[6].wait()
+    col = iota((BLOCK, BLOCK), 1)
+    row = iota((BLOCK, BLOCK), 0)
+    causal = row <= col
+    near = causal & ((col < WINDOW) == (row < WINDOW))
+    first_half = col < WINDOW
     for h in range(HEADS):
         at = h * BLOCK
         query = q_ref[:, at : at + BLOCK]
@@ -145,7 +140,7 @@
         both_ref[at : at + BLOCK, :] = both.T.astype(BF16)
 
 
-def local_call(q, k, v, qm, km, routes, documents):
+def local_call(q, k, v, qm):
     vmem = pl.BlockSpec(memory_space=pltpu.VMEM)
     return pl.pallas_call(
         local_kernel,
@@ -154,37 +149,23 @@
             jax.ShapeDtypeStruct((ROWS, CHUNK), F32),
             jax.ShapeDtypeStruct((ROWS, BLOCK), F32),
             jax.ShapeDtypeStruct((ROWS, CHUNK), BF16),
-            jax.ShapeDtypeStruct((ROWS, BLOCK), BF16),
-            jax.ShapeDtypeStruct((BLOCK, BLOCK), BF16),
-            jax.ShapeDtypeStruct((2 * CHUNKS, BLOCK), F32),
-        ),
-        in_specs=[pl.BlockSpec(memory_space=pltpu.HBM)] * 7,
-        out_specs=(vmem,) * 7,
-        scratch_shapes=[
-            pltpu.VMEM((BLOCK, ROWS), BF16),
-            pltpu.VMEM((HEADS * FEATURES, HEAD_DIM), BF16),
-            pltpu.VMEM((HEADS * FEATURES, HEAD_DIM), BF16),
-            pltpu.VMEM((64, 64), jnp.int32),
-            pltpu.VMEM((1, 64), jnp.int32),
-            pltpu.VMEM((BLOCK, HEAD_DIM), BF16),
-            pltpu.VMEM((BLOCK, HEAD_DIM), BF16),
-            pltpu.SemaphoreType.DMA((7,)),
-        ],
+        ),
+        in_specs=[vmem] * 4,
+        out_specs=(vmem,) * 4,
         compiler_params=pltpu.CompilerParams(vmem_limit_bytes=16 * 1024 * 1024),
         cost_estimate=pl.CostEstimate(
             flops=400_000_000, bytes_accessed=4_000_000, transcendentals=500_000
         ),
         name="local_block",
-    )(*[in_hbm(each) for each in (q, qm, km, routes, documents, k, v)])
-
-
-def slot_kernel(k0_ref, v0_ref, k1_ref, v1_ref, k2_ref, v2_ref, out_ref):
+    )(q, k, v, qm)
+
+
+def slot_kernel(now_ref, back1_ref, back2_ref, out_ref):
     y, c = lax.axis_index("y"), lax.axis_index("c")
-    planes = ((k0_ref, v0_ref), (k1_ref, v1_ref), (k2_ref, v2_ref))
+    planes = (now_ref, back1_ref, back2_ref)
 
     def put(d, k, plane):
-        for n in range(2):
-            out_ref[d, k, n] = planes[plane][n][...]
+        out_ref[d, k] = planes[plane][...]
 
     for d in range(4):
 
@@ -214,7 +195,7 @@
     return pl.pallas_call(
         slot_kernel,
         out_shape=jax.ShapeDtypeStruct((4, 2, 2, BLOCK, HEAD_DIM), BF16),
-        in_specs=[vmem] * 6,
+        in_specs=[vmem] * 3,
         out_specs=vmem,
         compiler_params=pltpu.CompilerParams(vmem_limit_bytes=8 * 1024 * 1024),
         name="fill_slots",
@@ -416,33 +397,34 @@
     key_rows = jnp.swapaxes(key_map, 1, 2).reshape(HEADS * FEATURES, HEAD_DIM)
     shift1 = [(i, (i + 1) % 8) for i in range(8)]
     shift2 = [(i, (i + 2) % 8) for i in range(8)]
-    plane0 = (keys[0], values[0])
-    plane2 = tuple(lax.ppermute(each, "z", shift2) for each in plane0)
-    plane1 = tuple(lax.ppermute(each, "z", shift1) for each in plane0)
-    local = local_call(
-        queries[0], keys[0], values[0], query_rows, key_rows, assignment[0], documents
-    )
-    plane1, plane2, local = lax.optimization_barrier((plane1, plane2, local))
-
-    slots = slot_call(*plane0, *plane1, *plane2)
+    plane0 = jnp.stack([keys[0], values[0]])
+    plane2 = lax.ppermute(plane0, "z", shift2)
+    plane1 = lax.ppermute(plane0, "z", shift1)
+    placed = place_call(keys[0], key_rows, assignment[0], documents)
+    plane1, plane2, placed = lax.optimization_barrier((plane1, plane2, placed))
+    slots = slot_call(plane0, plane1, plane2)
     mine = lax.all_to_all(slots, "y", 0, 0, tiled=True)
     other = lax.ppermute(mine, "c", [(0, 1), (1, 0)])
+    query, _ = lax.optimization_barrier((queries[0], mine))
+    local = local_call(query, keys[0], values[0], query_rows) + tuple(placed)
     loss_scale = HEAD_DIM / math.sqrt(4 * 64 * BLOCK)
     difference, outgoing = main_call(
-        loss_scale, queries[0], keys[0], values[0], mine, other, key_rows, local
+        loss_scale, query, keys[0], values[0], mine, other, key_rows, local
     )
     got = lax.all_to_all(outgoing, ("y", "c"), 0, 0, tiled=True)
     relay = got[:, :, :1024].reshape(8, 8, 2, 1024).transpose(1, 0, 2, 3).reshape(8, 16, 1024)
     part = jnp.sum(got[:, :, 1024:].astype(F32), axis=0).astype(BF16)
     part = jnp.broadcast_to(part[None], (8, 16, 512))
     got = lax.all_to_all(jnp.concatenate([relay, part], axis=2), "z", 0, 0, tiled=True)
-    relaid = got[:, :, :1024].reshape(1, BLOCK, 1024)
+    relay = got
     part = jnp.sum(got[:, :, 1024:].astype(F32), axis=0).astype(BF16)
     part = part.reshape(16, 4, HEAD_DIM).transpose(1, 0, 2).reshape(FEATURES, HEAD_DIM)
     part = jnp.broadcast_to(part[None], (16, FEATURES, HEAD_DIM))
     got = lax.all_to_all(part, ("x", "y"), 0, 0, tiled=True)
     part = jnp.sum(got.reshape(4, 4, FEATURES, HEAD_DIM).astype(F32), axis=0).astype(BF16)
+    relay, part = lax.optimization_barrier((relay, part))
     far = lax.ppermute(part, "c", [(0, 1), (1, 0)])
+    relaid = relay[:, :, :1024].reshape(1, BLOCK, 1024)
     mine_first = lax.broadcasted_iota(jnp.int32, (4, 2, FEATURES, HEAD_DIM), 1) == c
     grad = jnp.where(mine_first, part[:, None], far[:, None]).astype(F32)
     grad = grad.reshape(HEADS, FEATURES, HEAD_DIM)

time: 84.4 us -> 85.1 us (level)
  starting transfers between devices: 22 us -> 17.4 us
  blocking collectives: 38 us -> 40.3 us
  waiting for transfers between devices: 9.36 us -> 11.6 us
    ppermute x4 -> x2, starting transfers between devices: 9.58 us -> 5.53 us  [the longest x1 2.99 us: on_device(): plane2 = lax.ppermute(plane0, 'z', shift2)]
    ppermute x4 -> x2, waiting for transfers between devices: 0.28 us -> 4.04 us  [the longest x1 2.83 us: on_device(): plane2 = lax.ppermute(plane0, 'z', shift2)]
    all_to_all x1, blocking collectives: 16.2 us -> 18.8 us  [on_device(): lax.all_to_all(jnp.concatenate([relay, part], axis=2), 'z', 0, 0, tiled=T...]
    ppermute x1, waiting for transfers between devices: 1.54 us -> 0.01 us  [on_device(): other = lax.ppermute(mine, 'c', [(0, 1), (1, 0)])]
    pallas_call x1, Pallas kernels: 3.57 us -> 2.14 us  [local_call(): pl.pallas_call(local_kernel, out_shape=(jax.ShapeDtypeStruct((BLOCK, ROWS...]
    pallas_call x0 -> x1, Pallas kernels: none -> 1.39 us  [place_call(): pl.pallas_call(place_kernel, out_shape=(jax.ShapeDtypeStruct((ROWS, BLOCK...]
  transfers between devices with their start and end apart: 7 -> 5, of which waited for: 4 -> 4; matrix products, arithmetic and copies ran while one was open for 1% -> 1% of each run, Pallas kernels for 4% -> 4%
where the time goes in v5:
time: 85.1 us; the launch traced here: 84.7 us
  blocking collectives  40.3 us (47%)
  starting transfers between devices  17.4 us (20%)
  waiting for transfers between devices  11.6 us (14%)
  Pallas kernels  11.1 us (13%)
  local copies, waits for them, and re-layouts  2.71 us (3%)
  other arithmetic  0.91 us (1%)
    all_to_all x1, blocking collectives, on_device(): lax.all_to_all(jnp.concatenate([relay, part], axis=2), 'z', 0, 0, tiled=T...  18.8 us
    all_to_all x1, blocking collectives, on_device(): mine = lax.all_to_all(slots, 'y', 0, 0, tiled=True)  11.1 us
    all_to_all x1, blocking collectives, on_device(): got = lax.all_to_all(outgoing, ('y', 'c'), 0, 0, tiled=True)  10.5 us
    all_to_all x1, waiting for transfers between devices, on_device(): got = lax.all_to_all(part, ('x', 'y'), 0, 0, tiled=True)  7.47 us
    pallas_call x1, Pallas kernels, main_call(): pl.pallas_call(functools.partial(main_kernel, loss_scale), out_shape=(jax...  7.45 us
    all_to_all x1, starting transfers between devices, on_device(): got = lax.all_to_all(part, ('x', 'y'), 0, 0, tiled=True)  4.72 us
    ppermute x1, starting transfers between devices, on_device(): far = lax.ppermute(part, 'c', [(0, 1), (1, 0)])  3.59 us
    ppermute x1, starting transfers between devices, on_device(): other = lax.ppermute(mine, 'c', [(0, 1), (1, 0)])  3.52 us
  transfers between devices with their start and end apart: 5, of which 4 were waited for; matrix products, arithmetic and copies ran while one was open for 1% of the time, Pallas kernels for 4%

profile of v5, /device:TPU:1, one launch (start us, length us, event | category | flops | bytes accessed | tf_op | source)
XLA Modules:
  0.0 84.7 jit_solution(3005828176505251203)
XLA Ops:
  0.6 0.0 copy-start.1
  0.6 0.8 constant_dynamic-update-slice_fusion.1
  1.4 0.0 copy-done.1
  1.4 2.5 %collective-permute-start = (bf16[2,128,128]{2,1,0:T(8,128)(2,1)S(1)}, bf16[2,128,128]{2,1,0:T(8,128)(2,1)S(1)}, u32[]{:S(2)}, u32[]{:S(2)}) collective-permute-start(bf16[2,128,128]{2,1,0:T(8,128)(2,1)S(1)} %constant_dynamic-update-slice_fusion.now_ref), channel_id=1, source_target_pairs={{0,8},{8,16},{16,24},{24,32},{32,40},{40,48},{48,56},{56,0},{1,9},... | collective-permute-start | bytes 196616 | tf_op jit(solution)/shard_map/ppermute | solution.py:402
  4.0 3.0 %collective-permute-start.1 = (bf16[2,128,128]{2,1,0:T(8,128)(2,1)S(1)}, bf16[2,128,128]{2,1,0:T(8,128)(2,1)S(1)}, u32[]{:S(2)}, u32[]{:S(2)}) collective-permute-start(bf16[2,128,128]{2,1,0:T(8,128)(2,1)S(1)} %constant_dynamic-update-slice_fusion.now_ref), channel_id=1, source_target_pairs={{0,16},{8,24},{16,32},{24,40},{32,48},{40,56},{48,0},{56,8},{1,17}... | collective-permute-start | bytes 196616 | tf_op jit(solution)/shard_map/ppermute | solution.py:401
  7.0 1.4 %place.1 = (bf16[1024,128]{1,0:T(8,128)(2,1)S(1)}, bf16[128,128]{1,0:T(8,128)(2,1)S(1)}, f32[16,128]{1,0:T(8,128)S(1)}) custom-call(bf16[512,128]{1,0:T(8,128)(2,1)} %bitcast.34, s32[64,64]{1,0:T(8,128)} %bitcast.41, s32[1,64]{1,0:T(1,128)} %doc_hbm.1, bf16[128,128]{1,0:T(8,128)(2,1)} %bitcast.26), custom_call_target="tpu_custom_call" | custom-call | flops 100000000 | bytes 1000000 | tf_op jit(solution)/shard_map/place/pallas_call | solution.py:94
  8.4 1.2 %collective-permute-done.back1_ref = bf16[2,128,128]{2,1,0:T(8,128)(2,1)S(1)} collective-permute-done((bf16[2,128,128]{2,1,0:T(8,128)(2,1)S(1)}, bf16[2,128,128]{2,1,0:T(8,128)(2,1)S(1)}, u32[]{:S(2)}, u32[]{:S(2)}) %collective-permute-start) | collective-permute-done | bytes 65568 | tf_op jit(solution)/shard_map/ppermute | solution.py:402
  9.6 2.8 %collective-permute-done.1.back2_ref = bf16[2,128,128]{2,1,0:T(8,128)(2,1)S(1)} collective-permute-done((bf16[2,128,128]{2,1,0:T(8,128)(2,1)S(1)}, bf16[2,128,128]{2,1,0:T(8,128)(2,1)S(1)}, u32[]{:S(2)}, u32[]{:S(2)}) %collective-permute-start.1) | collective-permute-done | bytes 65568 | tf_op jit(solution)/shard_map/ppermute | solution.py:401
  12.4 0.1 fill_slots.1
  12.5 0.0 copy-start
  12.5 0.0 copy-start.2
  12.5 0.0 copy-start.3
  12.5 11.1 %all_to_all.20.a_ref = bf16[4,2,2,128,128]{4,3,2,1,0:T(8,128)(2,1)S(1)} all-to-all(bf16[4,2,2,128,128]{4,3,2,1,0:T(8,128)(2,1)S(1)} %fill_slots.1), channel_id=1, replica_groups=mesh['x'=4,'z'=8,'y'=4,'c'=2] {'y'}, dimensions={0} | all-to-all | bytes 1048576 | tf_op jit(solution)/shard_map/all_to_all | solution.py:406
  23.6 3.5 %collective-permute-start.2 = (bf16[4,2,2,128,128]{4,3,2,1,0:T(8,128)(2,1)S(1)}, bf16[4,2,2,128,128]{4,3,2,1,0:T(8,128)(2,1)S(1)}, u32[]{:S(2)}, u32[]{:S(2)}) collective-permute-start(bf16[4,2,2,128,128]{4,3,2,1,0:T(8,128)(2,1)S(1)} %all_to_all.20.a_ref), channel_id=1, source_target_pairs={{0,1},{1,0},{2,3},{3,2},{4,5},{5,4},{6,7},{7,6},{8,9},{9,8},{10,11... | collective-permute-start | bytes 1572872 | tf_op jit(solution)/shard_map/ppermute | solution.py:407
  27.1 0.0 copy-done
  27.1 0.0 copy-done.2
  27.1 0.0 copy-done.3
  27.1 0.0 copy-start.4
  27.1 2.1 %local_block.1 = (f32[128,1024]{1,0:T(8,128)S(1)}, f32[1024,256]{1,0:T(8,128)S(1)}, f32[1024,128]{1,0:T(8,128)S(1)}, bf16[1024,256]{1,0:T(8,128)(2,1)S(1)}) custom-call(bf16[128,1024]{1,0:T(8,128)(2,1)S(1)} %bitcast.31, bf16[128,128]{1,0:T(8,128)(2,1)S(1)} %bitcast.27, bf16[128,128]{1,0:T(8,128)(2,1)S(1)} %bitcast.29, bf16[512,128]{1,0:T(8,128)(2,1)S(1)} %bitcast.33), custom_call_target="tpu_custom_call" | custom-call | flops 400000000 | bytes 4000000 | tf_op jit(solution)/shard_map/local_block/pallas_call | solution.py:145
  29.3 0.0 collective-permute-done.2.b_ref
  29.3 0.0 copy-done.4
  29.3 7.5 %transfer.1 = (f32[128,1024]{1,0:T(8,128)}, bf16[8,16,1536]{2,1,0:T(8,128)(2,1)S(1)}) custom-call(bf16[128,1024]{1,0:T(8,128)(2,1)S(1)} %bitcast.32, bf16[128,128]{1,0:T(8,128)(2,1)S(1)} %bitcast.28, bf16[128,128]{1,0:T(8,128)(2,1)S(1)} %bitcast.30, bf16[4,2,2,128,128]{4,3,2,1,0:T(8,128)(2,1)S(1)} %all_to_all.20.a_ref, ...), custom_call_target="tpu_custom_call" | custom-call | flops 3000000000 | bytes 3000000 | tf_op jit(solution)/shard_map/transfer/pallas_call | solution.py:370
  36.8 10.5 %all_to_all.21 = bf16[8,16,1536]{2,1,0:T(8,128)(2,1)S(1)} all-to-all(bf16[8,16,1536]{2,1,0:T(8,128)(2,1)S(1)} %get-tuple-element.33), channel_id=1, replica_groups=mesh['x'=4,'z'=8,'y'=4,'c'=2] {'y','c'}, dimensions={0} | all-to-all | bytes 786432 | tf_op jit(solution)/shard_map/all_to_all | solution.py:414
  47.2 0.1 reshape.37
  47.4 0.1 copy.17
  47.5 0.1 copy.18
  47.6 18.8 %all_to_all.22 = bf16[8,16,1536]{2,1,0:T(8,128)(2,1)S(1)} all-to-all(bf16[8,16,1536]{2,1,0:T(8,128)(2,1)S(1)} %copy.18), channel_id=1, replica_groups=mesh['x'=4,'z'=8,'y'=4,'c'=2] {'z'}, dimensions={0} | all-to-all | bytes 786432 | tf_op jit(solution)/shard_map/all_to_all | solution.py:418
  66.5 0.8 broadcast_in_dim.40
  67.2 4.7 %all-to-all-start.3 = ((bf16[16,64,128]{2,1,0:T(8,128)(2,1)}), bf16[16,64,128]{2,1,0:T(8,128)(2,1)S(1)}, u32[]{:S(2)}, u32[]{:S(2)}) async-start(bf16[16,64,128]{2,1,0:T(8,128)(2,1)} %broadcast_in_dim.40), calls=%async_computation.3 | async-start | bytes 524288 | tf_op jit(solution)/shard_map/all_to_all | solution.py:423
  71.9 7.5 %all-to-all-done.3 = bf16[16,64,128]{2,1,0:T(8,128)(2,1)S(1)} async-done(((bf16[16,64,128]{2,1,0:T(8,128)(2,1)}), bf16[16,64,128]{2,1,0:T(8,128)(2,1)S(1)}, u32[]{:S(2)}, u32[]{:S(2)}) %all-to-all-start.3) | async-done | bytes 262176 | tf_op jit(solution)/shard_map/all_to_all | solution.py:423
  79.5 3.6 %collective-permute-start.3 = (bf16[4,64,128]{2,1,0:T(8,128)(2,1)S(1)}, bf16[4,64,128]{2,1,0:T(8,128)(2,1)S(1)}, u32[]{:S(2)}, u32[]{:S(2)}) collective-permute-start(bf16[4,64,128]{2,1,0:T(8,128)(2,1)S(1)} %reduce_sum.38), channel_id=1, source_target_pairs={{0,1},{1,0},{2,3},{3,2},{4,5},{5,4},{6,7},{7,6},{8,9},{9,8},{10,11... | collective-permute-start | bytes 196616 | tf_op jit(solution)/shard_map/ppermute | solution.py:426
  83.1 0.1 iota.12
  83.2 0.7 slice.15
  83.9 0.1 collective-permute-done.3
  84.0 0.8 convert_bitcast_fusion
  (11 shorter events, 0.2 us)
Async XLA Ops:
  0.6 0.8 copy-start.1
  1.4 8.1 %collective-permute-start = (bf16[2,128,128]{2,1,0:T(8,128)(2,1)S(1)}, bf16[2,128,128]{2,1,0:T(8,128)(2,1)S(1)}, u32[]{:S(2)}, u32[]{:S(2)}) collective-permute-start(bf16[2,128,128]{2,1,0:T(8,128)(2,1)S(1)} %constant_dynamic-update-slice_fusion.now_ref), channel_id=1, source_target_pairs={{0,8},{8,16},{16,24},{24,32},{32,40},{40,48},{48,56},{56,0},{1,9},... | collective-permute-start | bytes 196616 | tf_op jit(solution)/shard_map/ppermute | solution.py:402
  4.0 8.4 %collective-permute-start.1 = (bf16[2,128,128]{2,1,0:T(8,128)(2,1)S(1)}, bf16[2,128,128]{2,1,0:T(8,128)(2,1)S(1)}, u32[]{:S(2)}, u32[]{:S(2)}) collective-permute-start(bf16[2,128,128]{2,1,0:T(8,128)(2,1)S(1)} %constant_dynamic-update-slice_fusion.now_ref), channel_id=1, source_target_pairs={{0,16},{8,24},{16,32},{24,40},{32,48},{40,56},{48,0},{56,8},{1,17}... | collective-permute-start | bytes 196616 | tf_op jit(solution)/shard_map/ppermute | solution.py:401
  12.5 14.6 %copy-start = (bf16[1,128,128]{2,1,0:T(8,128)(2,1)S(1)}, bf16[1,128,128]{2,1,0:T(8,128)(2,1)}, u32[]{:S(2)}) copy-start(bf16[1,128,128]{2,1,0:T(8,128)(2,1)} %param.8) | copy-start | bytes 98308
  12.5 14.6 %copy-start.2 = (bf16[1,128,1024]{2,1,0:T(8,128)(2,1)S(1)}, bf16[1,128,1024]{2,1,0:T(8,128)(2,1)}, u32[]{:S(2)}) copy-start(bf16[1,128,1024]{2,1,0:T(8,128)(2,1)} %param.7) | copy-start | bytes 786436
  12.5 14.6 %copy-start.3 = (bf16[8,128,64]{1,2,0:T(8,128)(2,1)S(1)}, bf16[8,128,64]{1,2,0:T(8,128)(2,1)}, u32[]{:S(2)}) copy-start(bf16[8,128,64]{1,2,0:T(8,128)(2,1)} %param.10) | copy-start | bytes 393220
  23.6 5.7 %collective-permute-start.2 = (bf16[4,2,2,128,128]{4,3,2,1,0:T(8,128)(2,1)S(1)}, bf16[4,2,2,128,128]{4,3,2,1,0:T(8,128)(2,1)S(1)}, u32[]{:S(2)}, u32[]{:S(2)}) collective-permute-start(bf16[4,2,2,128,128]{4,3,2,1,0:T(8,128)(2,1)S(1)} %all_to_all.20.a_ref), channel_id=1, source_target_pairs={{0,1},{1,0},{2,3},{3,2},{4,5},{5,4},{6,7},{7,6},{8,9},{9,8},{10,11... | collective-permute-start | bytes 1572872 | tf_op jit(solution)/shard_map/ppermute | solution.py:407
  27.1 2.2 %copy-start.4 = (bf16[8,128,64]{1,2,0:T(8,128)(2,1)S(1)}, bf16[8,128,64]{1,2,0:T(8,128)(2,1)}, u32[]{:S(2)}) copy-start(bf16[8,128,64]{1,2,0:T(8,128)(2,1)} %param.11) | copy-start | bytes 393220
  67.2 12.2 %all-to-all-start.3 = ((bf16[16,64,128]{2,1,0:T(8,128)(2,1)}), bf16[16,64,128]{2,1,0:T(8,128)(2,1)S(1)}, u32[]{:S(2)}, u32[]{:S(2)}) async-start(bf16[16,64,128]{2,1,0:T(8,128)(2,1)} %broadcast_in_dim.40), calls=%async_computation.3 | async-start | bytes 524288 | tf_op jit(solution)/shard_map/all_to_all | solution.py:423
  79.5 4.5 %collective-permute-start.3 = (bf16[4,64,128]{2,1,0:T(8,128)(2,1)S(1)}, bf16[4,64,128]{2,1,0:T(8,128)(2,1)S(1)}, u32[]{:S(2)}, u32[]{:S(2)}) collective-permute-start(bf16[4,64,128]{2,1,0:T(8,128)(2,1)S(1)} %reduce_sum.38), channel_id=1, source_target_pairs={{0,1},{1,0},{2,3},{3,2},{4,5},{5,4},{6,7},{7,6},{8,9},{9,8},{10,11... | collective-permute-start | bytes 196616 | tf_op jit(solution)/shard_map/ppermute | solution.py:426

commit v6 on v5

--- a/solution.py
+++ b/solution.py
@@ -50,6 +50,29 @@
 
 def iota(shape, axis):
     return lax.broadcasted_iota(jnp.int32, shape, axis)
+
+
+def pack_kernel(k_hbm, v_hbm, out_ref, sems):
+    copies = [
+        pltpu.make_async_copy(k_hbm, out_ref.at[0], sems.at[0]),
+        pltpu.make_async_copy(v_hbm, out_ref.at[1], sems.at[1]),
+    ]
+    for copy in copies:
+        copy.start()
+    for copy in copies:
+        copy.wait()
+
+
+def pack_call(k, v):
+    return pl.pallas_call(
+        pack_kernel,
+        out_shape=jax.ShapeDtypeStruct((2, BLOCK, HEAD_DIM), BF16),
+        in_specs=[pl.BlockSpec(memory_space=pltpu.HBM)] * 2,
+        out_specs=pl.BlockSpec(memory_space=pltpu.VMEM),
+        scratch_shapes=[pltpu.SemaphoreType.DMA((2,))],
+        compiler_params=pltpu.CompilerParams(vmem_limit_bytes=8 * 1024 * 1024),
+        name="pack_block",
+    )(in_hbm(k), in_hbm(v))
 
 
 def place_kernel(
@@ -348,7 +371,7 @@
         running = []
         for stage, length, late_by in (
             (scores, 9, 0),
-            (features, 8, 0),
+            (features, 8, 1),
             (weights, 9, 1),
             (mixes, 3, 2),
             (outputs, 8, 3),
@@ -391,13 +414,41 @@
     )(q, k, v, a, b, km, *local)
 
 
+def finish_kernel(part_ref, far_ref, out_ref):
+    c = lax.axis_index("c")
+
+    def put(first_ref, second_ref):
+        for y in range(4):
+            out_ref[2 * y] = first_ref[y].astype(F32)
+            out_ref[2 * y + 1] = second_ref[y].astype(F32)
+
+    @pl.when(c == 0)
+    def _():
+        put(part_ref, far_ref)
+
+    @pl.when(c == 1)
+    def _():
+        put(far_ref, part_ref)
+
+
+def finish_call(part, far):
+    vmem = pl.BlockSpec(memory_space=pltpu.VMEM)
+    return pl.pallas_call(
+        finish_kernel,
+        out_shape=jax.ShapeDtypeStruct((HEADS, FEATURES, HEAD_DIM), F32),
+        in_specs=[vmem] * 2,
+        out_specs=vmem,
+        compiler_params=pltpu.CompilerParams(vmem_limit_bytes=8 * 1024 * 1024),
+        name="finish",
+    )(part, far)
+
+
 def on_device(queries, keys, values, query_map, key_map, documents, assignment):
-    c = lax.axis_index("c")
     query_rows = jnp.swapaxes(query_map, 1, 2).reshape(HEADS * FEATURES, HEAD_DIM)
     key_rows = jnp.swapaxes(key_map, 1, 2).reshape(HEADS * FEATURES, HEAD_DIM)
     shift1 = [(i, (i + 1) % 8) for i in range(8)]
     shift2 = [(i, (i + 2) % 8) for i in range(8)]
-    plane0 = jnp.stack([keys[0], values[0]])
+    plane0 = pack_call(keys[0], values[0])
     plane2 = lax.ppermute(plane0, "z", shift2)
     plane1 = lax.ppermute(plane0, "z", shift1)
     placed = place_call(keys[0], key_rows, assignment[0], documents)
@@ -425,9 +476,7 @@
     relay, part = lax.optimization_barrier((relay, part))
     far = lax.ppermute(part, "c", [(0, 1), (1, 0)])
     relaid = relay[:, :, :1024].reshape(1, BLOCK, 1024)
-    mine_first = lax.broadcasted_iota(jnp.int32, (4, 2, FEATURES, HEAD_DIM), 1) == c
-    grad = jnp.where(mine_first, part[:, None], far[:, None]).astype(F32)
-    grad = grad.reshape(HEADS, FEATURES, HEAD_DIM)
+    grad = finish_call(part, far)
     return relaid, difference[None], jnp.swapaxes(grad, 1, 2)
 
 

time: 85.1 us -> 83.9 us (0.986)
  blocking collectives: 40.3 us -> 53.2 us
  waiting for transfers between devices: 11.6 us -> 4.66 us
  starting transfers between devices: 17.4 us -> 11.2 us
  local copies, waits for them, and re-layouts: 2.71 us -> 1.13 us
  Pallas kernels: 11.1 us -> 12.4 us
    all_to_all x0 -> x1, blocking collectives: none -> 12 us  [on_device(): got = lax.all_to_all(part, ('x', 'y'), 0, 0, tiled=True)]
    all_to_all x1 -> x0, waiting for transfers between devices: 7.47 us -> none  [on_device(): got = lax.all_to_all(part, ('x', 'y'), 0, 0, tiled=True)]
    all_to_all x1 -> x0, starting transfers between devices: 4.72 us -> none  [on_device(): got = lax.all_to_all(part, ('x', 'y'), 0, 0, tiled=True)]
    ppermute x1, waiting for transfers between devices: 1.2 us -> 2.74 us  [on_device(): plane1 = lax.ppermute(plane0, 'z', shift1)]
    pallas_call x0 -> x2, Pallas kernels: none -> 1.52 us  [the longest x1 0.79 us: pack_call(): pl.pallas_call(pack_kernel, out_shape=jax.ShapeDtypeStruct((2, BLOCK, HEA...]
    ppermute x1, starting transfers between devices: 3.52 us -> 2.12 us  [on_device(): other = lax.ppermute(mine, 'c', [(0, 1), (1, 0)])]
    all_to_all x1, blocking collectives: 11.1 us -> 12.4 us  [on_device(): mine = lax.all_to_all(slots, 'y', 0, 0, tiled=True)]
    ppermute x1, waiting for transfers between devices: 2.83 us -> 1.74 us  [on_device(): plane2 = lax.ppermute(plane0, 'z', shift2)]
  transfers between devices with their start and end apart: 5 -> 4, of which waited for: 4 -> 3; matrix products, arithmetic and copies ran while one was open for 1% -> 1% of each run, Pallas kernels for 4% -> 4%
where the time goes in v6:
time: 83.9 us; the launch traced here: 83.5 us
  blocking collectives  53.2 us (63%)
  Pallas kernels  12.4 us (15%)
  starting transfers between devices  11.2 us (13%)
  waiting for transfers between devices  4.66 us (6%)
  local copies, waits for them, and re-layouts  1.13 us (1%)
    all_to_all x1, blocking collectives, on_device(): lax.all_to_all(jnp.concatenate([relay, part], axis=2), 'z', 0, 0, tiled=T...  18.3 us
    all_to_all x1, blocking collectives, on_device(): mine = lax.all_to_all(slots, 'y', 0, 0, tiled=True)  12.4 us
    all_to_all x1, blocking collectives, on_device(): got = lax.all_to_all(part, ('x', 'y'), 0, 0, tiled=True)  12 us
    all_to_all x1, blocking collectives, on_device(): got = lax.all_to_all(outgoing, ('y', 'c'), 0, 0, tiled=True)  10.5 us
    pallas_call x1, Pallas kernels, main_call(): pl.pallas_call(functools.partial(main_kernel, loss_scale), out_shape=(jax...  7.31 us
    ppermute x1, starting transfers between devices, on_device(): plane2 = lax.ppermute(plane0, 'z', shift2)  3.9 us
    ppermute x1, starting transfers between devices, on_device(): far = lax.ppermute(part, 'c', [(0, 1), (1, 0)])  3.59 us
    ppermute x1, waiting for transfers between devices, on_device(): plane1 = lax.ppermute(plane0, 'z', shift1)  2.74 us
  transfers between devices with their start and end apart: 4, of which 3 were waited for; matrix products, arithmetic and copies ran while one was open for 1% of the time, Pallas kernels for 4%

profile of v6, /device:TPU:1, one launch (start us, length us, event | category | flops | bytes accessed | tf_op | source)
XLA Modules:
  0.0 83.5 jit_solution(9044418955298959741)
XLA Ops:
  0.6 0.8 pack_block.1.now_ref
  1.4 3.9 %collective-permute-start.1 = (bf16[2,128,128]{2,1,0:T(8,128)(2,1)S(1)}, bf16[2,128,128]{2,1,0:T(8,128)(2,1)S(1)}, u32[]{:S(2)}, u32[]{:S(2)}) collective-permute-start(bf16[2,128,128]{2,1,0:T(8,128)(2,1)S(1)} %pack_block.1.now_ref), channel_id=1, source_target_pairs={{0,16},{8,24},{16,32},{24,40},{32,48},{40,56},{48,0},{56,8},{1,17}... | collective-permute-start | bytes 196616 | tf_op jit(solution)/shard_map/ppermute | solution.py:452
  5.3 1.6 %collective-permute-start = (bf16[2,128,128]{2,1,0:T(8,128)(2,1)S(1)}, bf16[2,128,128]{2,1,0:T(8,128)(2,1)S(1)}, u32[]{:S(2)}, u32[]{:S(2)}) collective-permute-start(bf16[2,128,128]{2,1,0:T(8,128)(2,1)S(1)} %pack_block.1.now_ref), channel_id=1, source_target_pairs={{0,8},{8,16},{16,24},{24,32},{32,40},{40,48},{48,56},{56,0},{1,9},... | collective-permute-start | bytes 196616 | tf_op jit(solution)/shard_map/ppermute | solution.py:453
  7.0 1.4 %place.1 = (bf16[1024,128]{1,0:T(8,128)(2,1)S(1)}, bf16[128,128]{1,0:T(8,128)(2,1)S(1)}, f32[16,128]{1,0:T(8,128)S(1)}) custom-call(bf16[512,128]{1,0:T(8,128)(2,1)} %bitcast.29, s32[64,64]{1,0:T(8,128)} %bitcast.37, s32[1,64]{1,0:T(1,128)} %doc_hbm.1, bf16[128,128]{1,0:T(8,128)(2,1)} %bitcast.20), custom_call_target="tpu_custom_call" | custom-call | flops 100000000 | bytes 1000000 | tf_op jit(solution)/shard_map/place/pallas_call | solution.py:117
  8.4 1.7 %collective-permute-done.1.back2_ref = bf16[2,128,128]{2,1,0:T(8,128)(2,1)S(1)} collective-permute-done((bf16[2,128,128]{2,1,0:T(8,128)(2,1)S(1)}, bf16[2,128,128]{2,1,0:T(8,128)(2,1)S(1)}, u32[]{:S(2)}, u32[]{:S(2)}) %collective-permute-start.1) | collective-permute-done | bytes 65568 | tf_op jit(solution)/shard_map/ppermute | solution.py:452
  10.1 2.7 %collective-permute-done.back1_ref = bf16[2,128,128]{2,1,0:T(8,128)(2,1)S(1)} collective-permute-done((bf16[2,128,128]{2,1,0:T(8,128)(2,1)S(1)}, bf16[2,128,128]{2,1,0:T(8,128)(2,1)S(1)}, u32[]{:S(2)}, u32[]{:S(2)}) %collective-permute-start) | collective-permute-done | bytes 65568 | tf_op jit(solution)/shard_map/ppermute | solution.py:453
  12.9 0.1 fill_slots.1
  12.9 0.0 copy-start
  12.9 0.0 copy-start.1
  13.0 0.0 copy-start.2
  13.0 0.0 copy-start.3
  13.0 12.4 %all_to_all.20.a_ref = bf16[4,2,2,128,128]{4,3,2,1,0:T(8,128)(2,1)S(1)} all-to-all(bf16[4,2,2,128,128]{4,3,2,1,0:T(8,128)(2,1)S(1)} %fill_slots.1), channel_id=1, replica_groups=mesh['x'=4,'z'=8,'y'=4,'c'=2] {'y'}, dimensions={0} | all-to-all | bytes 1048576 | tf_op jit(solution)/shard_map/all_to_all | solution.py:457
  25.4 2.1 %collective-permute-start.2 = (bf16[4,2,2,128,128]{4,3,2,1,0:T(8,128)(2,1)S(1)}, bf16[4,2,2,128,128]{4,3,2,1,0:T(8,128)(2,1)S(1)}, u32[]{:S(2)}, u32[]{:S(2)}) collective-permute-start(bf16[4,2,2,128,128]{4,3,2,1,0:T(8,128)(2,1)S(1)} %all_to_all.20.a_ref), channel_id=1, source_target_pairs={{0,1},{1,0},{2,3},{3,2},{4,5},{5,4},{6,7},{7,6},{8,9},{9,8},{10,11... | collective-permute-start | bytes 1572872 | tf_op jit(solution)/shard_map/ppermute | solution.py:458
  27.5 0.0 copy-done
  27.5 0.0 copy-done.1
  27.5 0.0 copy-done.2
  27.5 0.0 copy-done.3
  27.6 0.0 copy-start.4
  27.6 2.1 %local_block.1 = (f32[128,1024]{1,0:T(8,128)S(1)}, f32[1024,256]{1,0:T(8,128)S(1)}, f32[1024,128]{1,0:T(8,128)S(1)}, bf16[1024,256]{1,0:T(8,128)(2,1)S(1)}) custom-call(bf16[128,1024]{1,0:T(8,128)(2,1)S(1)} %bitcast.26, bf16[128,128]{1,0:T(8,128)(2,1)S(1)} %bitcast.21, bf16[128,128]{1,0:T(8,128)(2,1)S(1)} %bitcast.24, bf16[512,128]{1,0:T(8,128)(2,1)S(1)} %bitcast.28), custom_call_target="tpu_custom_call" | custom-call | flops 400000000 | bytes 4000000 | tf_op jit(solution)/shard_map/local_block/pallas_call | solution.py:168
  29.7 0.0 collective-permute-done.2.b_ref
  29.7 0.0 copy-done.4
  29.7 7.3 %transfer.1 = (f32[128,1024]{1,0:T(8,128)}, bf16[8,16,1536]{2,1,0:T(8,128)(2,1)S(1)}) custom-call(bf16[128,1024]{1,0:T(8,128)(2,1)S(1)} %bitcast.27, bf16[128,128]{1,0:T(8,128)(2,1)S(1)} %bitcast.22, bf16[128,128]{1,0:T(8,128)(2,1)S(1)} %bitcast.25, bf16[4,2,2,128,128]{4,3,2,1,0:T(8,128)(2,1)S(1)} %all_to_all.20.a_ref, ...), custom_call_target="tpu_custom_call" | custom-call | flops 3000000000 | bytes 3000000 | tf_op jit(solution)/shard_map/transfer/pallas_call | solution.py:393
  37.0 10.5 %all_to_all.21 = bf16[8,16,1536]{2,1,0:T(8,128)(2,1)S(1)} all-to-all(bf16[8,16,1536]{2,1,0:T(8,128)(2,1)S(1)} %get-tuple-element.33), channel_id=1, replica_groups=mesh['x'=4,'z'=8,'y'=4,'c'=2] {'y','c'}, dimensions={0} | all-to-all | bytes 786432 | tf_op jit(solution)/shard_map/all_to_all | solution.py:465
  47.5 0.1 reshape.31
  47.6 0.1 copy.17
  47.8 0.1 copy.18
  47.9 18.3 %all_to_all.22 = bf16[8,16,1536]{2,1,0:T(8,128)(2,1)S(1)} all-to-all(bf16[8,16,1536]{2,1,0:T(8,128)(2,1)S(1)} %copy.18), channel_id=1, replica_groups=mesh['x'=4,'z'=8,'y'=4,'c'=2] {'z'}, dimensions={0} | all-to-all | bytes 786432 | tf_op jit(solution)/shard_map/all_to_all | solution.py:469
  66.3 12.0 %all_to_all.23 = bf16[16,64,128]{2,1,0:T(8,128)(2,1)S(1)} all-to-all(bf16[16,64,128]{2,1,0:T(8,128)(2,1)S(1)} %broadcast_in_dim.18), channel_id=1, replica_groups=mesh['x'=4,'z'=8,'y'=4,'c'=2] {'x','y'}, dimensions={0} | all-to-all | bytes 524288 | tf_op jit(solution)/shard_map/all_to_all | solution.py:474
  78.3 3.6 %collective-permute-start.3 = (bf16[4,64,128]{2,1,0:T(8,128)(2,1)S(1)}, bf16[4,64,128]{2,1,0:T(8,128)(2,1)S(1)}, u32[]{:S(2)}, u32[]{:S(2)}) collective-permute-start(bf16[4,64,128]{2,1,0:T(8,128)(2,1)S(1)} %reduce_sum.38.part_ref), channel_id=1, source_target_pairs={{0,1},{1,0},{2,3},{3,2},{4,5},{5,4},{6,7},{7,6},{8,9},{9,8},{10,11... | collective-permute-start | bytes 196616 | tf_op jit(solution)/shard_map/ppermute | solution.py:477
  81.9 0.7 slice.15
  82.6 0.2 collective-permute-done.3.far_ref
  82.8 0.7 finish.1
  (9 shorter events, 0.2 us)
Async XLA Ops:
  1.4 8.7 %collective-permute-start.1 = (bf16[2,128,128]{2,1,0:T(8,128)(2,1)S(1)}, bf16[2,128,128]{2,1,0:T(8,128)(2,1)S(1)}, u32[]{:S(2)}, u32[]{:S(2)}) collective-permute-start(bf16[2,128,128]{2,1,0:T(8,128)(2,1)S(1)} %pack_block.1.now_ref), channel_id=1, source_target_pairs={{0,16},{8,24},{16,32},{24,40},{32,48},{40,56},{48,0},{56,8},{1,17}... | collective-permute-start | bytes 196616 | tf_op jit(solution)/shard_map/ppermute | solution.py:452
  5.3 7.5 %collective-permute-start = (bf16[2,128,128]{2,1,0:T(8,128)(2,1)S(1)}, bf16[2,128,128]{2,1,0:T(8,128)(2,1)S(1)}, u32[]{:S(2)}, u32[]{:S(2)}) collective-permute-start(bf16[2,128,128]{2,1,0:T(8,128)(2,1)S(1)} %pack_block.1.now_ref), channel_id=1, source_target_pairs={{0,8},{8,16},{16,24},{24,32},{32,40},{40,48},{48,56},{56,0},{1,9},... | collective-permute-start | bytes 196616 | tf_op jit(solution)/shard_map/ppermute | solution.py:453
  12.9 14.6 %copy-start = (bf16[1,128,128]{2,1,0:T(8,128)(2,1)S(1)}, bf16[1,128,128]{2,1,0:T(8,128)(2,1)}, u32[]{:S(2)}) copy-start(bf16[1,128,128]{2,1,0:T(8,128)(2,1)} %param.8) | copy-start | bytes 98308
  12.9 14.6 %copy-start.1 = (bf16[1,128,128]{2,1,0:T(8,128)(2,1)S(1)}, bf16[1,128,128]{2,1,0:T(8,128)(2,1)}, u32[]{:S(2)}) copy-start(bf16[1,128,128]{2,1,0:T(8,128)(2,1)} %param.9) | copy-start | bytes 98308
  13.0 14.6 %copy-start.2 = (bf16[1,128,1024]{2,1,0:T(8,128)(2,1)S(1)}, bf16[1,128,1024]{2,1,0:T(8,128)(2,1)}, u32[]{:S(2)}) copy-start(bf16[1,128,1024]{2,1,0:T(8,128)(2,1)} %param.7) | copy-start | bytes 786436
  13.0 14.6 %copy-start.3 = (bf16[8,128,64]{1,2,0:T(8,128)(2,1)S(1)}, bf16[8,128,64]{1,2,0:T(8,128)(2,1)}, u32[]{:S(2)}) copy-start(bf16[8,128,64]{1,2,0:T(8,128)(2,1)} %param.10) | copy-start | bytes 393220
  25.4 4.3 %collective-permute-start.2 = (bf16[4,2,2,128,128]{4,3,2,1,0:T(8,128)(2,1)S(1)}, bf16[4,2,2,128,128]{4,3,2,1,0:T(8,128)(2,1)S(1)}, u32[]{:S(2)}, u32[]{:S(2)}) collective-permute-start(bf16[4,2,2,128,128]{4,3,2,1,0:T(8,128)(2,1)S(1)} %all_to_all.20.a_ref), channel_id=1, source_target_pairs={{0,1},{1,0},{2,3},{3,2},{4,5},{5,4},{6,7},{7,6},{8,9},{9,8},{10,11... | collective-permute-start | bytes 1572872 | tf_op jit(solution)/shard_map/ppermute | solution.py:458
  27.6 2.2 %copy-start.4 = (bf16[8,128,64]{1,2,0:T(8,128)(2,1)S(1)}, bf16[8,128,64]{1,2,0:T(8,128)(2,1)}, u32[]{:S(2)}) copy-start(bf16[8,128,64]{1,2,0:T(8,128)(2,1)} %param.11) | copy-start | bytes 393220
  78.3 4.5 %collective-permute-start.3 = (bf16[4,64,128]{2,1,0:T(8,128)(2,1)S(1)}, bf16[4,64,128]{2,1,0:T(8,128)(2,1)S(1)}, u32[]{:S(2)}, u32[]{:S(2)}) collective-permute-start(bf16[4,64,128]{2,1,0:T(8,128)(2,1)S(1)} %reduce_sum.38.part_ref), channel_id=1, source_target_pairs={{0,1},{1,0},{2,3},{3,2},{4,5},{5,4},{6,7},{7,6},{8,9},{9,8},{10,11... | collective-permute-start | bytes 196616 | tf_op jit(solution)/shard_map/ppermute | solution.py:477

commit v7 on v4

--- a/solution.py
+++ b/solution.py
@@ -48,12 +48,31 @@
     return pltpu.with_memory_space_constraint(x, pltpu.HBM)
 
 
-def shard_index():
-    return (lax.axis_index("z") * 4 + lax.axis_index("y")) * 2 + lax.axis_index("c")
-
-
 def iota(shape, axis):
     return lax.broadcasted_iota(jnp.int32, shape, axis)
+
+
+def pack_kernel(k_hbm, v_hbm, out_ref, sems):
+    copies = [
+        pltpu.make_async_copy(k_hbm, out_ref.at[0], sems.at[0]),
+        pltpu.make_async_copy(v_hbm, out_ref.at[1], sems.at[1]),
+    ]
+    for copy in copies:
+        copy.start()
+    for copy in copies:
+        copy.wait()
+
+
+def pack_call(k, v):
+    return pl.pallas_call(
+        pack_kernel,
+        out_shape=jax.ShapeDtypeStruct((2, BLOCK, HEAD_DIM), BF16),
+        in_specs=[pl.BlockSpec(memory_space=pltpu.HBM)] * 2,
+        out_specs=pl.BlockSpec(memory_space=pltpu.VMEM),
+        scratch_shapes=[pltpu.SemaphoreType.DMA((2,))],
+        compiler_params=pltpu.CompilerParams(vmem_limit_bytes=8 * 1024 * 1024),
+        name="pack_block",
+    )(in_hbm(k), in_hbm(v))
 
 
 def local_kernel(
@@ -72,12 +91,12 @@
     dest_ref,
     ok_ref,
     q_ref,
+    k_ref,
+    v_ref,
+    km_ref,
     qm_ref,
-    km_ref,
     route_ref,
     doc_ref,
-    k_ref,
-    v_ref,
     sems,
 ):
     pairs = (
@@ -100,7 +119,7 @@
     near = causal & ((col < WINDOW) == (row < WINDOW))
     first_half = col < WINDOW
     z, y, c = lax.axis_index("z"), lax.axis_index("y"), lax.axis_index("c")
-    here = shard_index()
+    here = (z * 4 + y) * 2 + c
     place = iota((2 * CHUNKS, 64), 0)
     block = iota((2 * CHUNKS, 64), 1)
     from_y = lax.shift_right_logical(place, 1) & 3
@@ -157,17 +176,17 @@
             jax.ShapeDtypeStruct((ROWS, BLOCK), BF16),
             jax.ShapeDtypeStruct((BLOCK, BLOCK), BF16),
             jax.ShapeDtypeStruct((2 * CHUNKS, BLOCK), F32),
+            jax.ShapeDtypeStruct((BLOCK, ROWS), BF16),
+            jax.ShapeDtypeStruct((BLOCK, HEAD_DIM), BF16),
+            jax.ShapeDtypeStruct((BLOCK, HEAD_DIM), BF16),
+            jax.ShapeDtypeStruct((HEADS * FEATURES, HEAD_DIM), BF16),
         ),
         in_specs=[pl.BlockSpec(memory_space=pltpu.HBM)] * 7,
-        out_specs=(vmem,) * 7,
+        out_specs=(vmem,) * 11,
         scratch_shapes=[
-            pltpu.VMEM((BLOCK, ROWS), BF16),
-            pltpu.VMEM((HEADS * FEATURES, HEAD_DIM), BF16),
             pltpu.VMEM((HEADS * FEATURES, HEAD_DIM), BF16),
             pltpu.VMEM((64, 64), jnp.int32),
             pltpu.VMEM((1, 64), jnp.int32),
-            pltpu.VMEM((BLOCK, HEAD_DIM), BF16),
-            pltpu.VMEM((BLOCK, HEAD_DIM), BF16),
             pltpu.SemaphoreType.DMA((7,)),
         ],
         compiler_params=pltpu.CompilerParams(vmem_limit_bytes=16 * 1024 * 1024),
@@ -178,13 +197,65 @@
     )(*[in_hbm(each) for each in (q, qm, km, routes, documents, k, v)])
 
 
-def slot_kernel(k0_ref, v0_ref, k1_ref, v1_ref, k2_ref, v2_ref, out_ref):
+def half_kernel(q_ref, k_ref, a_ref, km_ref, ok_ref, s_ref, psi_ref, top_ref, key_scr):
+    fill_keys(key_scr, a_ref, k_ref, ok_ref, 0)
+    for g in range(HEADS // 2):
+        query = two_heads(q_ref, g)
+        top = None
+        for i in range(CHUNKS // 2):
+            keys = key_scr[i * CHUNK : (i + 1) * CHUNK, :]
+            s = dot(keys, query, NT)
+            s_ref[i * CHUNK : (i + 1) * CHUNK, g * CHUNK : (g + 1) * CHUNK] = s
+            now = jnp.max(s.reshape(CHUNK // 8, 8, CHUNK), axis=0)
+            top = now if top is None else jnp.maximum(top, now)
+            u = dot(km_ref[g * BLOCK : (g + 1) * BLOCK, :], keys, NT)
+            psi = two_softmax(u.reshape(2, FEATURES, CHUNK)).reshape(CHUNK, CHUNK)
+            psi_ref[g * CHUNK : (g + 1) * CHUNK, i * CHUNK : (i + 1) * CHUNK] = psi.astype(BF16)
+        top_ref[:, g * CHUNK : (g + 1) * CHUNK] = top
+
+
+def two_heads(q_ref, g):
+    return jnp.concatenate(
+        [q_ref[:, (2 * g + k) * BLOCK : (2 * g + k + 1) * BLOCK] for k in range(2)], axis=0
+    )
+
+
+def fill_keys(key_scr, src, k_ref, ok_ref, first):
+    first_key = k_ref[0:1, :]
+    for i in range(CHUNKS // 2):
+        for k in range(2):
+            at = i * CHUNK + k * BLOCK
+            one = ok_ref[2 * (first + i) + k : 2 * (first + i) + k + 1, :]
+            other = (1.0 - one).astype(BF16)
+            key_scr[at : at + BLOCK, :] = src[i, k, 0] * one.astype(BF16) + first_key * other
+
+
+def half_call(q, k, a, km, ok):
+    vmem = pl.BlockSpec(memory_space=pltpu.VMEM)
+    return pl.pallas_call(
+        half_kernel,
+        out_shape=(
+            jax.ShapeDtypeStruct((FAR // 2, ROWS), F32),
+            jax.ShapeDtypeStruct((ROWS, FAR // 2), BF16),
+            jax.ShapeDtypeStruct((8, ROWS), F32),
+        ),
+        in_specs=[vmem] * 5,
+        out_specs=(vmem,) * 3,
+        scratch_shapes=[pltpu.VMEM((FAR // 2, BLOCK), BF16)],
+        compiler_params=pltpu.CompilerParams(vmem_limit_bytes=16 * 1024 * 1024),
+        cost_estimate=pl.CostEstimate(
+            flops=400_000_000, bytes_accessed=4_000_000, transcendentals=1_000_000
+        ),
+        name="first_half",
+    )(q, k, a, km, ok)
+
+
+def slot_kernel(now_ref, back1_ref, back2_ref, out_ref):
     y, c = lax.axis_index("y"), lax.axis_index("c")
-    planes = ((k0_ref, v0_ref), (k1_ref, v1_ref), (k2_ref, v2_ref))
+    planes = (now_ref, back1_ref, back2_ref)
 
     def put(d, k, plane):
-        for n in range(2):
-            out_ref[d, k, n] = planes[plane][n][...]
+        out_ref[d, k] = planes[plane][...]
 
     for d in range(4):
 
@@ -214,7 +285,7 @@
     return pl.pallas_call(
         slot_kernel,
         out_shape=jax.ShapeDtypeStruct((4, 2, 2, BLOCK, HEAD_DIM), BF16),
-        in_specs=[vmem] * 6,
+        in_specs=[vmem] * 3,
         out_specs=vmem,
         compiler_params=pltpu.CompilerParams(vmem_limit_bytes=8 * 1024 * 1024),
         name="fill_slots",
@@ -229,6 +300,9 @@
     a_ref,
     b_ref,
     km_ref,
+    s_half,
+    psi_half,
+    top_half,
     own_ref,
     near_ref,
     phi_ref,
@@ -245,18 +319,15 @@
     vp_scr,
     wide_scr,
 ):
-    first_key = k_ref[0:1, :]
     all_ones = jnp.ones((BLOCK, BLOCK), BF16)
     ones = jnp.ones((TALL - HEAD_DIM, BLOCK), BF16)
+    fill_keys(key_scr, b_ref, k_ref, ok_ref, CHUNKS // 2)
     for i in range(CHUNKS):
         src = a_ref if i < 4 else b_ref
         for k in range(2):
             at = i * CHUNK + k * BLOCK
-            one = ok_ref[2 * i + k : 2 * i + k + 1, :]
-            other = (1.0 - one).astype(BF16)
-            one = one.astype(BF16)
+            one = ok_ref[2 * i + k : 2 * i + k + 1, :].astype(BF16)
             value = src[i % 4, k, 1] * one
-            key_scr[at : at + BLOCK, :] = src[i % 4, k, 0] * one + first_key * other
             vp_scr[:HEAD_DIM, at : at + BLOCK] = value.T
             vp_scr[HEAD_DIM:, at : at + BLOCK] = ones * one
             wide_scr[at : at + BLOCK, :BLOCK] = value
@@ -270,16 +341,16 @@
     dest = dest_ref[...]
 
     groups = HEADS // 2
+    half = CHUNKS // 2
     tops, sums = [None] * groups, [None] * groups
 
     def scores(g):
-        query = jnp.concatenate(
-            [q_ref[:, (2 * g + k) * BLOCK : (2 * g + k + 1) * BLOCK] for k in range(2)], axis=0
-        )
+        query = two_heads(q_ref, g)
         top = jnp.max(
             own_ref[:, g * CHUNK : (g + 1) * CHUNK].reshape(BLOCK // 8, 8, CHUNK), axis=0
         )
-        for i in range(CHUNKS):
+        top = jnp.maximum(top, top_half[:, g * CHUNK : (g + 1) * CHUNK])
+        for i in range(half):
             s = dot(key_scr[i * CHUNK : (i + 1) * CHUNK, :], query, NT)
             s_scr[g % 2, i * CHUNK : (i + 1) * CHUNK, :] = s
             top = jnp.maximum(top, jnp.max(s.reshape(CHUNK // 8, 8, CHUNK), axis=0))
@@ -287,7 +358,7 @@
         tops[g] = jnp.max(top, axis=0, keepdims=True) * SCALE
 
     def features(g):
-        for i in range(CHUNKS):
+        for i in range(half):
             keys = key_scr[i * CHUNK : (i + 1) * CHUNK, :]
             u = dot(km_ref[g * BLOCK : (g + 1) * BLOCK, :], keys, NT)
             psi = two_softmax(u.reshape(2, FEATURES, CHUNK)).reshape(CHUNK, CHUNK)
@@ -296,7 +367,10 @@
 
     def weights(g):
         for i in range(CHUNKS):
-            s = s_scr[g % 2, i * CHUNK : (i + 1) * CHUNK, :]
+            if i < half:
+                s = s_half[i * CHUNK : (i + 1) * CHUNK, g * CHUNK : (g + 1) * CHUNK]
+            else:
+                s = s_scr[g % 2, (i - half) * CHUNK : (i - half + 1) * CHUNK, :]
             w = jnp.exp2(s * SCALE - tops[g])
             p_scr[g % 2, i * CHUNK : (i + 1) * CHUNK, :] = w.astype(BF16)
             yield
@@ -307,7 +381,8 @@
     def mixes(g):
         mixed = dot(vp_scr[...], p_scr[g % 2])
         yield
-        state = dot(psi_scr[g % 3], wide_scr[...])
+        state = dot(psi_half[g * CHUNK : (g + 1) * CHUNK, :], wide_scr[: FAR // 2, :])
+        state = state + dot(psi_scr[g % 3], wide_scr[FAR // 2 :, :])
         yield
         late = state + dot(psi_own_ref[g * CHUNK : (g + 1) * CHUNK, :], value_early)
         sums[g] = (mixed, state.astype(BF16), late.astype(BF16))
@@ -366,8 +441,8 @@
     for step in range(groups + 3):
         running = []
         for stage, length, late_by in (
-            (scores, 9, 0),
-            (features, 8, 0),
+            (scores, 5, 0),
+            (features, 4, 1),
             (weights, 9, 1),
             (mixes, 3, 2),
             (outputs, 8, 3),
@@ -384,7 +459,7 @@
                 pass
 
 
-def main_call(loss_scale, q, k, v, a, b, km, local):
+def main_call(loss_scale, q, k, v, a, b, km, half, local):
     vmem = pl.BlockSpec(memory_space=pltpu.VMEM)
     return pl.pallas_call(
         functools.partial(main_kernel, loss_scale),
@@ -392,60 +467,89 @@
             jax.ShapeDtypeStruct((BLOCK, HEADS * HEAD_DIM), F32),
             jax.ShapeDtypeStruct((8, 16, 1536), BF16),
         ),
-        in_specs=[vmem] * 13,
+        in_specs=[vmem] * 16,
         out_specs=(vmem, vmem),
         scratch_shapes=[
-            pltpu.VMEM((2, FAR, CHUNK), F32),
+            pltpu.VMEM((2, FAR // 2, CHUNK), F32),
             pltpu.VMEM((2, FAR + BLOCK, CHUNK), BF16),
-            pltpu.VMEM((3, CHUNK, FAR), BF16),
-            pltpu.VMEM((FAR, BLOCK), BF16),
+            pltpu.VMEM((3, CHUNK, FAR // 2), BF16),
+            pltpu.VMEM((FAR // 2, BLOCK), BF16),
             pltpu.VMEM((TALL, FAR + BLOCK), BF16),
             pltpu.VMEM((FAR, CHUNK), BF16),
         ],
-        compiler_params=pltpu.CompilerParams(vmem_limit_bytes=32 * 1024 * 1024),
+        compiler_params=pltpu.CompilerParams(vmem_limit_bytes=24 * 1024 * 1024),
         cost_estimate=pl.CostEstimate(
             flops=3_000_000_000, bytes_accessed=3_000_000, transcendentals=4_000_000
         ),
         name="transfer",
-    )(q, k, v, a, b, km, *local)
+    )(q, k, v, a, b, km, *half, *local)
+
+
+def finish_kernel(part_ref, far_ref, out_ref):
+    c = lax.axis_index("c")
+
+    def put(first_ref, second_ref):
+        for y in range(4):
+            out_ref[2 * y] = first_ref[y].astype(F32)
+            out_ref[2 * y + 1] = second_ref[y].astype(F32)
+
+    @pl.when(c == 0)
+    def _():
+        put(part_ref, far_ref)
+
+    @pl.when(c == 1)
+    def _():
+        put(far_ref, part_ref)
+
+
+def finish_call(part, far):
+    vmem = pl.BlockSpec(memory_space=pltpu.VMEM)
+    return pl.pallas_call(
+        finish_kernel,
+        out_shape=jax.ShapeDtypeStruct((HEADS, FEATURES, HEAD_DIM), F32),
+        in_specs=[vmem] * 2,
+        out_specs=vmem,
+        compiler_params=pltpu.CompilerParams(vmem_limit_bytes=8 * 1024 * 1024),
+        name="finish",
+    )(part, far)
 
 
 def on_device(queries, keys, values, query_map, key_map, documents, assignment):
-    c = lax.axis_index("c")
     query_rows = jnp.swapaxes(query_map, 1, 2).reshape(HEADS * FEATURES, HEAD_DIM)
     key_rows = jnp.swapaxes(key_map, 1, 2).reshape(HEADS * FEATURES, HEAD_DIM)
     shift1 = [(i, (i + 1) % 8) for i in range(8)]
     shift2 = [(i, (i + 2) % 8) for i in range(8)]
-    plane0 = (keys[0], values[0])
-    plane2 = tuple(lax.ppermute(each, "z", shift2) for each in plane0)
-    plane1 = tuple(lax.ppermute(each, "z", shift1) for each in plane0)
+    plane0 = pack_call(keys[0], values[0])
+    plane2 = lax.ppermute(plane0, "z", shift2)
+    plane1 = lax.ppermute(plane0, "z", shift1)
     local = local_call(
         queries[0], keys[0], values[0], query_rows, key_rows, assignment[0], documents
     )
     plane1, plane2, local = lax.optimization_barrier((plane1, plane2, local))
-
-    slots = slot_call(*plane0, *plane1, *plane2)
+    slots = slot_call(plane0, plane1, plane2)
     mine = lax.all_to_all(slots, "y", 0, 0, tiled=True)
     other = lax.ppermute(mine, "c", [(0, 1), (1, 0)])
+    local, (q, k, v, km) = local[:7], local[7:]
+    half = half_call(q, k, mine, km, local[-1])
     loss_scale = HEAD_DIM / math.sqrt(4 * 64 * BLOCK)
     difference, outgoing = main_call(
-        loss_scale, queries[0], keys[0], values[0], mine, other, key_rows, local
+        loss_scale, q, k, v, mine, other, km, half, local
     )
     got = lax.all_to_all(outgoing, ("y", "c"), 0, 0, tiled=True)
     relay = got[:, :, :1024].reshape(8, 8, 2, 1024).transpose(1, 0, 2, 3).reshape(8, 16, 1024)
     part = jnp.sum(got[:, :, 1024:].astype(F32), axis=0).astype(BF16)
     part = jnp.broadcast_to(part[None], (8, 16, 512))
     got = lax.all_to_all(jnp.concatenate([relay, part], axis=2), "z", 0, 0, tiled=True)
-    relaid = got[:, :, :1024].reshape(1, BLOCK, 1024)
+    relay = got
     part = jnp.sum(got[:, :, 1024:].astype(F32), axis=0).astype(BF16)
     part = part.reshape(16, 4, HEAD_DIM).transpose(1, 0, 2).reshape(FEATURES, HEAD_DIM)
     part = jnp.broadcast_to(part[None], (16, FEATURES, HEAD_DIM))
     got = lax.all_to_all(part, ("x", "y"), 0, 0, tiled=True)
     part = jnp.sum(got.reshape(4, 4, FEATURES, HEAD_DIM).astype(F32), axis=0).astype(BF16)
+    relay, part = lax.optimization_barrier((relay, part))
     far = lax.ppermute(part, "c", [(0, 1), (1, 0)])
-    mine_first = lax.broadcasted_iota(jnp.int32, (4, 2, FEATURES, HEAD_DIM), 1) == c
-    grad = jnp.where(mine_first, part[:, None], far[:, None]).astype(F32)
-    grad = grad.reshape(HEADS, FEATURES, HEAD_DIM)
+    relaid = relay[:, :, :1024].reshape(1, BLOCK, 1024)
+    grad = finish_call(part, far)
     return relaid, difference[None], jnp.swapaxes(grad, 1, 2)
 
 

time: 84.4 us -> 82.4 us (0.976)
  blocking collectives: 38 us -> 53.2 us
  starting transfers between devices: 22 us -> 11.2 us
  waiting for transfers between devices: 9.36 us -> 2.47 us
  Pallas kernels: 11.1 us -> 13.3 us
    all_to_all x0 -> x1, blocking collectives: none -> 12 us  [on_device(): got = lax.all_to_all(part, ('x', 'y'), 0, 0, tiled=True)]
    all_to_all x1 -> x0, waiting for transfers between devices: 7.47 us -> none  [on_device(): got = lax.all_to_all(part, ('x', 'y'), 0, 0, tiled=True)]
    all_to_all x1 -> x0, starting transfers between devices: 4.73 us -> none  [on_device(): got = lax.all_to_all(part, ('x', 'y'), 0, 0, tiled=True)]
    ppermute x4 -> x2, starting transfers between devices: 9.58 us -> 5.53 us  [the longest x1 3.9 us: on_device(): plane2 = lax.ppermute(plane0, 'z', shift2)]
    pallas_call x0 -> x3, Pallas kernels: none -> 3.26 us  [the longest x1 1.74 us: half_call(): pl.pallas_call(half_kernel, out_shape=(jax.ShapeDtypeStruct((FAR // 2, RO...]
    all_to_all x1, blocking collectives: 16.2 us -> 18.3 us  [on_device(): lax.all_to_all(jnp.concatenate([relay, part], axis=2), 'z', 0, 0, tiled=T...]
    ppermute x4 -> x2, waiting for transfers between devices: 0.28 us -> 2.3 us  [the longest x1 2.29 us: on_device(): plane1 = lax.ppermute(plane0, 'z', shift1)]
    ppermute x1, starting transfers between devices: 4.09 us -> 2.12 us  [on_device(): other = lax.ppermute(mine, 'c', [(0, 1), (1, 0)])]
  transfers between devices with their start and end apart: 7 -> 4, of which waited for: 4 -> 2; matrix products, arithmetic and copies ran while one was open for 1% -> 1% of each run, Pallas kernels for 4% -> 6%
where the time goes in v7:
time: 82.4 us; the launch traced here: 82.1 us
  blocking collectives  53.2 us (65%)
  Pallas kernels  13.3 us (16%)
  starting transfers between devices  11.2 us (14%)
  waiting for transfers between devices  2.47 us (3%)
  local copies, waits for them, and re-layouts  1.1 us (1%)
    all_to_all x1, blocking collectives, on_device(): lax.all_to_all(jnp.concatenate([relay, part], axis=2), 'z', 0, 0, tiled=T...  18.3 us
    all_to_all x1, blocking collectives, on_device(): mine = lax.all_to_all(slots, 'y', 0, 0, tiled=True)  12.3 us
    all_to_all x1, blocking collectives, on_device(): got = lax.all_to_all(part, ('x', 'y'), 0, 0, tiled=True)  12 us
    all_to_all x1, blocking collectives, on_device(): got = lax.all_to_all(outgoing, ('y', 'c'), 0, 0, tiled=True)  10.6 us
    pallas_call x1, Pallas kernels, main_call(): pl.pallas_call(functools.partial(main_kernel, loss_scale), out_shape=(jax...  6.36 us
    ppermute x1, starting transfers between devices, on_device(): plane2 = lax.ppermute(plane0, 'z', shift2)  3.9 us
    ppermute x1, starting transfers between devices, on_device(): far = lax.ppermute(part, 'c', [(0, 1), (1, 0)])  3.59 us
    pallas_call x1, Pallas kernels, local_call(): pl.pallas_call(local_kernel, out_shape=(jax.ShapeDtypeStruct((BLOCK, ROWS...  3.58 us
  transfers between devices with their start and end apart: 4, of which 2 were waited for; matrix products, arithmetic and copies ran while one was open for 1% of the time, Pallas kernels for 6%

profile of v7, /device:TPU:1, one launch (start us, length us, event | category | flops | bytes accessed | tf_op | source)
XLA Modules:
  0.0 82.1 jit_solution(2967641877732085012)
XLA Ops:
  0.6 0.8 pack_block.1.now_ref
  1.4 3.9 %collective-permute-start.1 = (bf16[2,128,128]{2,1,0:T(8,128)(2,1)S(1)}, bf16[2,128,128]{2,1,0:T(8,128)(2,1)S(1)}, u32[]{:S(2)}, u32[]{:S(2)}) collective-permute-start(bf16[2,128,128]{2,1,0:T(8,128)(2,1)S(1)} %pack_block.1.now_ref), channel_id=1, source_target_pairs={{0,16},{8,24},{16,32},{24,40},{32,48},{40,56},{48,0},{56,8},{1,17}... | collective-permute-start | bytes 196616 | tf_op jit(solution)/shard_map/ppermute | solution.py:523
  5.3 1.6 %collective-permute-start = (bf16[2,128,128]{2,1,0:T(8,128)(2,1)S(1)}, bf16[2,128,128]{2,1,0:T(8,128)(2,1)S(1)}, u32[]{:S(2)}, u32[]{:S(2)}) collective-permute-start(bf16[2,128,128]{2,1,0:T(8,128)(2,1)S(1)} %pack_block.1.now_ref), channel_id=1, source_target_pairs={{0,8},{8,16},{16,24},{24,32},{32,40},{40,48},{48,56},{56,0},{1,9},... | collective-permute-start | bytes 196616 | tf_op jit(solution)/shard_map/ppermute | solution.py:524
  7.0 3.6 %local_block.1 = (f32[128,1024]{1,0:T(8,128)S(1)}, f32[1024,256]{1,0:T(8,128)S(1)}, f32[1024,128]{1,0:T(8,128)S(1)}, bf16[1024,256]{1,0:T(8,128)(2,1)S(1)}, bf16...) custom-call(bf16[128,1024]{1,0:T(8,128)(2,1)} %bitcast.29, ...), custom_call_target="tpu_custom_call" | custom-call | flops 400000000 | bytes 4000000 | tf_op jit(solution)/shard_map/local_block/pallas_call | solution.py:169
  10.6 0.0 collective-permute-done.1.back2_ref
  10.6 2.3 %collective-permute-done.back1_ref = bf16[2,128,128]{2,1,0:T(8,128)(2,1)S(1)} collective-permute-done((bf16[2,128,128]{2,1,0:T(8,128)(2,1)S(1)}, bf16[2,128,128]{2,1,0:T(8,128)(2,1)S(1)}, u32[]{:S(2)}, u32[]{:S(2)}) %collective-permute-start) | collective-permute-done | bytes 65568 | tf_op jit(solution)/shard_map/ppermute | solution.py:524
  12.9 0.1 fill_slots.1
  12.9 12.3 %all_to_all.20.a_ref = bf16[4,2,2,128,128]{4,3,2,1,0:T(8,128)(2,1)S(1)} all-to-all(bf16[4,2,2,128,128]{4,3,2,1,0:T(8,128)(2,1)S(1)} %fill_slots.1), channel_id=1, replica_groups=mesh['x'=4,'z'=8,'y'=4,'c'=2] {'y'}, dimensions={0} | all-to-all | bytes 1048576 | tf_op jit(solution)/shard_map/all_to_all | solution.py:530
  25.2 2.1 %collective-permute-start.2 = (bf16[4,2,2,128,128]{4,3,2,1,0:T(8,128)(2,1)S(1)}, bf16[4,2,2,128,128]{4,3,2,1,0:T(8,128)(2,1)S(1)}, u32[]{:S(2)}, u32[]{:S(2)}) collective-permute-start(bf16[4,2,2,128,128]{4,3,2,1,0:T(8,128)(2,1)S(1)} %all_to_all.20.a_ref), channel_id=1, source_target_pairs={{0,1},{1,0},{2,3},{3,2},{4,5},{5,4},{6,7},{7,6},{8,9},{9,8},{10,11... | collective-permute-start | bytes 1572872 | tf_op jit(solution)/shard_map/ppermute | solution.py:531
  27.4 1.7 %first_half.1 = (f32[1024,1024]{1,0:T(8,128)S(1)}, bf16[1024,1024]{1,0:T(8,128)(2,1)S(1)}, f32[8,1024]{1,0:T(8,128)S(1)}) custom-call(bf16[128,1024]{1,0:T(8,128)(2,1)S(1)} %get-tuple-element.45.q_ref, bf16[128,128]{1,0:T(8,128)(2,1)S(1)} %get-tuple-element.46.k_ref, bf16[4,2,2,128,128]{4,3,2,1,0:T(8,128)(2,1)S(1)} %all_to_all.20.a_ref, ...), custom_call_target="tpu_custom_call" | custom-call | flops 400000000 | bytes 4000000 | tf_op jit(solution)/shard_map/first_half/pallas_call | solution.py:235
  29.1 0.0 collective-permute-done.2.b_ref
  29.1 6.4 %transfer.1 = (f32[128,1024]{1,0:T(8,128)}, bf16[8,16,1536]{2,1,0:T(8,128)(2,1)S(1)}) custom-call(bf16[128,1024]{1,0:T(8,128)(2,1)S(1)} %get-tuple-element.45.q_ref, bf16[128,128]{1,0:T(8,128)(2,1)S(1)} %get-tuple-element.46.k_ref, bf16[128,128]{1,0:T(8,128)(2,1)S(1)} %get-tuple-element.47.v_ref, bf16[4,2,2,128,128]{4,3,2,1,0:T(8,128)(2,1)S(1)} %all_to_all.20.a_ref, ...), custom_call_target="tpu_custom_call" | custom-call | flops 3000000000 | bytes 3000000 | tf_op jit(solution)/shard_map/transfer/pallas_call | solution.py:464
  35.5 10.6 %all_to_all.21 = bf16[8,16,1536]{2,1,0:T(8,128)(2,1)S(1)} all-to-all(bf16[8,16,1536]{2,1,0:T(8,128)(2,1)S(1)} %get-tuple-element.61), channel_id=1, replica_groups=mesh['x'=4,'z'=8,'y'=4,'c'=2] {'y','c'}, dimensions={0} | all-to-all | bytes 786432 | tf_op jit(solution)/shard_map/all_to_all | solution.py:538
  46.1 0.1 reshape.31
  46.2 0.1 copy.17
  46.4 0.1 copy.18
  46.5 18.3 %all_to_all.22 = bf16[8,16,1536]{2,1,0:T(8,128)(2,1)S(1)} all-to-all(bf16[8,16,1536]{2,1,0:T(8,128)(2,1)S(1)} %copy.18), channel_id=1, replica_groups=mesh['x'=4,'z'=8,'y'=4,'c'=2] {'z'}, dimensions={0} | all-to-all | bytes 786432 | tf_op jit(solution)/shard_map/all_to_all | solution.py:542
  64.8 12.0 %all_to_all.23 = bf16[16,64,128]{2,1,0:T(8,128)(2,1)S(1)} all-to-all(bf16[16,64,128]{2,1,0:T(8,128)(2,1)S(1)} %broadcast_in_dim.18), channel_id=1, replica_groups=mesh['x'=4,'z'=8,'y'=4,'c'=2] {'x','y'}, dimensions={0} | all-to-all | bytes 524288 | tf_op jit(solution)/shard_map/all_to_all | solution.py:547
  76.9 3.6 %collective-permute-start.3 = (bf16[4,64,128]{2,1,0:T(8,128)(2,1)S(1)}, bf16[4,64,128]{2,1,0:T(8,128)(2,1)S(1)}, u32[]{:S(2)}, u32[]{:S(2)}) collective-permute-start(bf16[4,64,128]{2,1,0:T(8,128)(2,1)S(1)} %reduce_sum.38.part_ref), channel_id=1, source_target_pairs={{0,1},{1,0},{2,3},{3,2},{4,5},{5,4},{6,7},{7,6},{8,9},{9,8},{10,11... | collective-permute-start | bytes 196616 | tf_op jit(solution)/shard_map/ppermute | solution.py:550
  80.5 0.7 slice.15
  81.2 0.2 collective-permute-done.3.far_ref
  81.4 0.7 finish.1
  (9 shorter events, 0.2 us)
Async XLA Ops:
  1.4 9.1 %collective-permute-start.1 = (bf16[2,128,128]{2,1,0:T(8,128)(2,1)S(1)}, bf16[2,128,128]{2,1,0:T(8,128)(2,1)S(1)}, u32[]{:S(2)}, u32[]{:S(2)}) collective-permute-start(bf16[2,128,128]{2,1,0:T(8,128)(2,1)S(1)} %pack_block.1.now_ref), channel_id=1, source_target_pairs={{0,16},{8,24},{16,32},{24,40},{32,48},{40,56},{48,0},{56,8},{1,17}... | collective-permute-start | bytes 196616 | tf_op jit(solution)/shard_map/ppermute | solution.py:523
  5.3 7.5 %collective-permute-start = (bf16[2,128,128]{2,1,0:T(8,128)(2,1)S(1)}, bf16[2,128,128]{2,1,0:T(8,128)(2,1)S(1)}, u32[]{:S(2)}, u32[]{:S(2)}) collective-permute-start(bf16[2,128,128]{2,1,0:T(8,128)(2,1)S(1)} %pack_block.1.now_ref), channel_id=1, source_target_pairs={{0,8},{8,16},{16,24},{24,32},{32,40},{40,48},{48,56},{56,0},{1,9},... | collective-permute-start | bytes 196616 | tf_op jit(solution)/shard_map/ppermute | solution.py:524
  25.2 3.9 %collective-permute-start.2 = (bf16[4,2,2,128,128]{4,3,2,1,0:T(8,128)(2,1)S(1)}, bf16[4,2,2,128,128]{4,3,2,1,0:T(8,128)(2,1)S(1)}, u32[]{:S(2)}, u32[]{:S(2)}) collective-permute-start(bf16[4,2,2,128,128]{4,3,2,1,0:T(8,128)(2,1)S(1)} %all_to_all.20.a_ref), channel_id=1, source_target_pairs={{0,1},{1,0},{2,3},{3,2},{4,5},{5,4},{6,7},{7,6},{8,9},{9,8},{10,11... | collective-permute-start | bytes 1572872 | tf_op jit(solution)/shard_map/ppermute | solution.py:531
  76.9 4.5 %collective-permute-start.3 = (bf16[4,64,128]{2,1,0:T(8,128)(2,1)S(1)}, bf16[4,64,128]{2,1,0:T(8,128)(2,1)S(1)}, u32[]{:S(2)}, u32[]{:S(2)}) collective-permute-start(bf16[4,64,128]{2,1,0:T(8,128)(2,1)S(1)} %reduce_sum.38.part_ref), channel_id=1, source_target_pairs={{0,1},{1,0},{2,3},{3,2},{4,5},{5,4},{6,7},{7,6},{8,9},{9,8},{10,11... | collective-permute-start | bytes 196616 | tf_op jit(solution)/shard_map/ppermute | solution.py:550

commit v8 on v7

--- a/solution.py
+++ b/solution.py
@@ -87,7 +87,7 @@
     near_ref,
     phi_ref,
     both_ref,
-    psi_ref,
+    early_ref,
     dest_ref,
     ok_ref,
     q_ref,
@@ -144,7 +144,8 @@
     keys = k_ref[...]
     values = jnp.concatenate([v_ref[...], jnp.ones((BLOCK, BLOCK), BF16)], axis=1)
     psi = two_softmax(dot(km_ref[...], keys, NT).reshape(HEADS, FEATURES, BLOCK))
-    psi_ref[...] = psi.reshape(ROWS, BLOCK).astype(BF16)
+    early = jnp.where(iota((BLOCK, CHUNK), 0) < WINDOW, values.astype(F32), 0.0).astype(BF16)
+    early_ref[...] = dot(psi.reshape(ROWS, BLOCK).astype(BF16), early)
     copies[5].wait()
     copies[6].wait()
     for h in range(HEADS):
@@ -173,7 +174,7 @@
             jax.ShapeDtypeStruct((ROWS, CHUNK), F32),
             jax.ShapeDtypeStruct((ROWS, BLOCK), F32),
             jax.ShapeDtypeStruct((ROWS, CHUNK), BF16),
-            jax.ShapeDtypeStruct((ROWS, BLOCK), BF16),
+            jax.ShapeDtypeStruct((ROWS, CHUNK), F32),
             jax.ShapeDtypeStruct((BLOCK, BLOCK), BF16),
             jax.ShapeDtypeStruct((2 * CHUNKS, BLOCK), F32),
             jax.ShapeDtypeStruct((BLOCK, ROWS), BF16),
@@ -197,8 +198,16 @@
     )(*[in_hbm(each) for each in (q, qm, km, routes, documents, k, v)])
 
 
-def half_kernel(q_ref, k_ref, a_ref, km_ref, ok_ref, s_ref, psi_ref, top_ref, key_scr):
+def half_kernel(
+    q_ref, k_ref, a_ref, km_ref, ok_ref, s_ref, state_ref, top_ref, key_scr, psi_scr, wide_scr
+):
     fill_keys(key_scr, a_ref, k_ref, ok_ref, 0)
+    for i in range(CHUNKS // 2):
+        for k in range(2):
+            at = i * CHUNK + k * BLOCK
+            one = ok_ref[2 * i + k : 2 * i + k + 1, :].astype(BF16)
+            wide_scr[at : at + BLOCK, :BLOCK] = a_ref[i, k, 1] * one
+            wide_scr[at : at + BLOCK, BLOCK:] = jnp.ones((BLOCK, BLOCK), BF16) * one
     for g in range(HEADS // 2):
         query = two_heads(q_ref, g)
         top = None
@@ -210,7 +219,10 @@
             top = now if top is None else jnp.maximum(top, now)
             u = dot(km_ref[g * BLOCK : (g + 1) * BLOCK, :], keys, NT)
             psi = two_softmax(u.reshape(2, FEATURES, CHUNK)).reshape(CHUNK, CHUNK)
-            psi_ref[g * CHUNK : (g + 1) * CHUNK, i * CHUNK : (i + 1) * CHUNK] = psi.astype(BF16)
+            psi_scr[g * CHUNK : (g + 1) * CHUNK, i * CHUNK : (i + 1) * CHUNK] = psi.astype(BF16)
+        state_ref[g * CHUNK : (g + 1) * CHUNK, :] = dot(
+            psi_scr[g * CHUNK : (g + 1) * CHUNK, :], wide_scr[...]
+        )
         top_ref[:, g * CHUNK : (g + 1) * CHUNK] = top
 
 
@@ -236,12 +248,16 @@
         half_kernel,
         out_shape=(
             jax.ShapeDtypeStruct((FAR // 2, ROWS), F32),
-            jax.ShapeDtypeStruct((ROWS, FAR // 2), BF16),
+            jax.ShapeDtypeStruct((ROWS, CHUNK), F32),
             jax.ShapeDtypeStruct((8, ROWS), F32),
         ),
         in_specs=[vmem] * 5,
         out_specs=(vmem,) * 3,
-        scratch_shapes=[pltpu.VMEM((FAR // 2, BLOCK), BF16)],
+        scratch_shapes=[
+            pltpu.VMEM((FAR // 2, BLOCK), BF16),
+            pltpu.VMEM((ROWS, FAR // 2), BF16),
+            pltpu.VMEM((FAR // 2, CHUNK), BF16),
+        ],
         compiler_params=pltpu.CompilerParams(vmem_limit_bytes=16 * 1024 * 1024),
         cost_estimate=pl.CostEstimate(
             flops=400_000_000, bytes_accessed=4_000_000, transcendentals=1_000_000
@@ -301,13 +317,13 @@
     b_ref,
     km_ref,
     s_half,
-    psi_half,
+    state_half,
     top_half,
     own_ref,
     near_ref,
     phi_ref,
     both_ref,
-    psi_own_ref,
+    early_ref,
     dest_ref,
     ok_ref,
     diff_ref,
@@ -330,13 +346,11 @@
             value = src[i % 4, k, 1] * one
             vp_scr[:HEAD_DIM, at : at + BLOCK] = value.T
             vp_scr[HEAD_DIM:, at : at + BLOCK] = ones * one
-            wide_scr[at : at + BLOCK, :BLOCK] = value
-            wide_scr[at : at + BLOCK, BLOCK:] = all_ones * one
+            if i >= 4:
+                wide_scr[at - FAR // 2 : at - FAR // 2 + BLOCK, :BLOCK] = value
+                wide_scr[at - FAR // 2 : at - FAR // 2 + BLOCK, BLOCK:] = all_ones * one
     vp_scr[:HEAD_DIM, FAR:] = v_ref[...].T
     vp_scr[HEAD_DIM:, FAR:] = ones
-    early = lax.broadcasted_iota(jnp.int32, (BLOCK, CHUNK), 0) < WINDOW
-    value_early = jnp.concatenate([v_ref[...], all_ones], axis=1)
-    value_early = jnp.where(early, value_early.astype(F32), 0.0).astype(BF16)
     first_half = lax.broadcasted_iota(jnp.int32, (BLOCK, BLOCK), 1) < WINDOW
     dest = dest_ref[...]
 
@@ -381,10 +395,9 @@
     def mixes(g):
         mixed = dot(vp_scr[...], p_scr[g % 2])
         yield
-        state = dot(psi_half[g * CHUNK : (g + 1) * CHUNK, :], wide_scr[: FAR // 2, :])
-        state = state + dot(psi_scr[g % 3], wide_scr[FAR // 2 :, :])
-        yield
-        late = state + dot(psi_own_ref[g * CHUNK : (g + 1) * CHUNK, :], value_early)
+        state = state_half[g * CHUNK : (g + 1) * CHUNK, :] + dot(psi_scr[g % 3], wide_scr[...])
+        yield
+        late = state + early_ref[g * CHUNK : (g + 1) * CHUNK, :]
         sums[g] = (mixed, state.astype(BF16), late.astype(BF16))
         yield
 
@@ -441,11 +454,11 @@
     for step in range(groups + 3):
         running = []
         for stage, length, late_by in (
+            (outputs, 8, 3),
+            (mixes, 3, 2),
+            (weights, 9, 1),
+            (features, 4, 1),
             (scores, 5, 0),
-            (features, 4, 1),
-            (weights, 9, 1),
-            (mixes, 3, 2),
-            (outputs, 8, 3),
         ):
             if 0 <= step - late_by < groups:
                 running.append((stage(step - late_by), length))
@@ -475,7 +488,7 @@
             pltpu.VMEM((3, CHUNK, FAR // 2), BF16),
             pltpu.VMEM((FAR // 2, BLOCK), BF16),
             pltpu.VMEM((TALL, FAR + BLOCK), BF16),
-            pltpu.VMEM((FAR, CHUNK), BF16),
+            pltpu.VMEM((FAR // 2, CHUNK), BF16),
         ],
         compiler_params=pltpu.CompilerParams(vmem_limit_bytes=24 * 1024 * 1024),
         cost_estimate=pl.CostEstimate(

time: 82.4 us -> 82 us (level)
  transfers between devices with their start and end apart: 4 -> 4, of which waited for: 2 -> 2; matrix products, arithmetic and copies ran while one was open for 1% -> 1% of each run, Pallas kernels for 6% -> 7%
where the time goes in v8:
time: 82 us; the launch traced here: 81.6 us
  blocking collectives  53 us (65%)
  Pallas kernels  13.1 us (16%)
  starting transfers between devices  11.2 us (14%)
  waiting for transfers between devices  2.28 us (3%)
  local copies, waits for them, and re-layouts  1.1 us (1%)
    all_to_all x1, blocking collectives, on_device(): lax.all_to_all(jnp.concatenate([relay, part], axis=2), 'z', 0, 0, tiled=T...  18.2 us
    all_to_all x1, blocking collectives, on_device(): mine = lax.all_to_all(slots, 'y', 0, 0, tiled=True)  12.3 us
    all_to_all x1, blocking collectives, on_device(): got = lax.all_to_all(part, ('x', 'y'), 0, 0, tiled=True)  12 us
    all_to_all x1, blocking collectives, on_device(): got = lax.all_to_all(outgoing, ('y', 'c'), 0, 0, tiled=True)  10.5 us
    pallas_call x1, Pallas kernels, main_call(): pl.pallas_call(functools.partial(main_kernel, loss_scale), out_shape=(jax...  5.6 us
    ppermute x1, starting transfers between devices, on_device(): plane2 = lax.ppermute(plane0, 'z', shift2)  3.9 us
    pallas_call x1, Pallas kernels, local_call(): pl.pallas_call(local_kernel, out_shape=(jax.ShapeDtypeStruct((BLOCK, ROWS...  3.76 us
    ppermute x1, starting transfers between devices, on_device(): far = lax.ppermute(part, 'c', [(0, 1), (1, 0)])  3.59 us
  transfers between devices with their start and end apart: 4, of which 2 were waited for; matrix products, arithmetic and copies ran while one was open for 1% of the time, Pallas kernels for 7%

profile of v8, /device:TPU:1, one launch (start us, length us, event | category | flops | bytes accessed | tf_op | source)
XLA Modules:
  0.0 81.6 jit_solution(8391969817950186377)
XLA Ops:
  0.6 0.8 pack_block.1.now_ref
  1.4 3.9 %collective-permute-start.1 = (bf16[2,128,128]{2,1,0:T(8,128)(2,1)S(1)}, bf16[2,128,128]{2,1,0:T(8,128)(2,1)S(1)}, u32[]{:S(2)}, u32[]{:S(2)}) collective-permute-start(bf16[2,128,128]{2,1,0:T(8,128)(2,1)S(1)} %pack_block.1.now_ref), channel_id=1, source_target_pairs={{0,16},{8,24},{16,32},{24,40},{32,48},{40,56},{48,0},{56,8},{1,17}... | collective-permute-start | bytes 196616 | tf_op jit(solution)/shard_map/ppermute | solution.py:536
  5.3 1.6 %collective-permute-start = (bf16[2,128,128]{2,1,0:T(8,128)(2,1)S(1)}, bf16[2,128,128]{2,1,0:T(8,128)(2,1)S(1)}, u32[]{:S(2)}, u32[]{:S(2)}) collective-permute-start(bf16[2,128,128]{2,1,0:T(8,128)(2,1)S(1)} %pack_block.1.now_ref), channel_id=1, source_target_pairs={{0,8},{8,16},{16,24},{24,32},{32,40},{40,48},{48,56},{56,0},{1,9},... | collective-permute-start | bytes 196616 | tf_op jit(solution)/shard_map/ppermute | solution.py:537
  7.0 3.8 %local_block.1 = (f32[128,1024]{1,0:T(8,128)S(1)}, f32[1024,256]{1,0:T(8,128)S(1)}, f32[1024,128]{1,0:T(8,128)S(1)}, bf16[1024,256]{1,0:T(8,128)(2,1)S(1)}, f32[...) custom-call(bf16[128,1024]{1,0:T(8,128)(2,1)} %bitcast.29, ...), custom_call_target="tpu_custom_call" | custom-call | flops 400000000 | bytes 4000000 | tf_op jit(solution)/shard_map/local_block/pallas_call | solution.py:170
  10.7 0.0 collective-permute-done.1.back2_ref
  10.7 2.1 %collective-permute-done.back1_ref = bf16[2,128,128]{2,1,0:T(8,128)(2,1)S(1)} collective-permute-done((bf16[2,128,128]{2,1,0:T(8,128)(2,1)S(1)}, bf16[2,128,128]{2,1,0:T(8,128)(2,1)S(1)}, u32[]{:S(2)}, u32[]{:S(2)}) %collective-permute-start) | collective-permute-done | bytes 65568 | tf_op jit(solution)/shard_map/ppermute | solution.py:537
  12.9 0.1 fill_slots.1
  12.9 12.3 %all_to_all.20.a_ref = bf16[4,2,2,128,128]{4,3,2,1,0:T(8,128)(2,1)S(1)} all-to-all(bf16[4,2,2,128,128]{4,3,2,1,0:T(8,128)(2,1)S(1)} %fill_slots.1), channel_id=1, replica_groups=mesh['x'=4,'z'=8,'y'=4,'c'=2] {'y'}, dimensions={0} | all-to-all | bytes 1048576 | tf_op jit(solution)/shard_map/all_to_all | solution.py:543
  25.2 2.1 %collective-permute-start.2 = (bf16[4,2,2,128,128]{4,3,2,1,0:T(8,128)(2,1)S(1)}, bf16[4,2,2,128,128]{4,3,2,1,0:T(8,128)(2,1)S(1)}, u32[]{:S(2)}, u32[]{:S(2)}) collective-permute-start(bf16[4,2,2,128,128]{4,3,2,1,0:T(8,128)(2,1)S(1)} %all_to_all.20.a_ref), channel_id=1, source_target_pairs={{0,1},{1,0},{2,3},{3,2},{4,5},{5,4},{6,7},{7,6},{8,9},{9,8},{10,11... | collective-permute-start | bytes 1572872 | tf_op jit(solution)/shard_map/ppermute | solution.py:544
  27.4 2.2 %first_half.1 = (f32[1024,1024]{1,0:T(8,128)S(1)}, f32[1024,256]{1,0:T(8,128)S(1)}, f32[8,1024]{1,0:T(8,128)S(1)}) custom-call(bf16[128,1024]{1,0:T(8,128)(2,1)S(1)} %get-tuple-element.45.q_ref, bf16[128,128]{1,0:T(8,128)(2,1)S(1)} %get-tuple-element.46.k_ref, bf16[4,2,2,128,128]{4,3,2,1,0:T(8,128)(2,1)S(1)} %all_to_all.20.a_ref, ...), custom_call_target="tpu_custom_call" | custom-call | flops 400000000 | bytes 4000000 | tf_op jit(solution)/shard_map/first_half/pallas_call | solution.py:247
  29.5 0.0 collective-permute-done.2.b_ref
  29.5 5.6 %transfer.1 = (f32[128,1024]{1,0:T(8,128)}, bf16[8,16,1536]{2,1,0:T(8,128)(2,1)S(1)}) custom-call(bf16[128,1024]{1,0:T(8,128)(2,1)S(1)} %get-tuple-element.45.q_ref, bf16[128,128]{1,0:T(8,128)(2,1)S(1)} %get-tuple-element.46.k_ref, bf16[128,128]{1,0:T(8,128)(2,1)S(1)} %get-tuple-element.47.v_ref, bf16[4,2,2,128,128]{4,3,2,1,0:T(8,128)(2,1)S(1)} %all_to_all.20.a_ref, ...), custom_call_target="tpu_custom_call" | custom-call | flops 3000000000 | bytes 3000000 | tf_op jit(solution)/shard_map/transfer/pallas_call | solution.py:477
  35.1 10.5 %all_to_all.21 = bf16[8,16,1536]{2,1,0:T(8,128)(2,1)S(1)} all-to-all(bf16[8,16,1536]{2,1,0:T(8,128)(2,1)S(1)} %get-tuple-element.61), channel_id=1, replica_groups=mesh['x'=4,'z'=8,'y'=4,'c'=2] {'y','c'}, dimensions={0} | all-to-all | bytes 786432 | tf_op jit(solution)/shard_map/all_to_all | solution.py:551
  45.6 0.1 reshape.31
  45.7 0.1 copy.17
  45.9 0.1 copy.18
  46.0 18.2 %all_to_all.22 = bf16[8,16,1536]{2,1,0:T(8,128)(2,1)S(1)} all-to-all(bf16[8,16,1536]{2,1,0:T(8,128)(2,1)S(1)} %copy.18), channel_id=1, replica_groups=mesh['x'=4,'z'=8,'y'=4,'c'=2] {'z'}, dimensions={0} | all-to-all | bytes 786432 | tf_op jit(solution)/shard_map/all_to_all | solution.py:555
  64.4 12.0 %all_to_all.23 = bf16[16,64,128]{2,1,0:T(8,128)(2,1)S(1)} all-to-all(bf16[16,64,128]{2,1,0:T(8,128)(2,1)S(1)} %broadcast_in_dim.18), channel_id=1, replica_groups=mesh['x'=4,'z'=8,'y'=4,'c'=2] {'x','y'}, dimensions={0} | all-to-all | bytes 524288 | tf_op jit(solution)/shard_map/all_to_all | solution.py:560
  76.4 3.6 %collective-permute-start.3 = (bf16[4,64,128]{2,1,0:T(8,128)(2,1)S(1)}, bf16[4,64,128]{2,1,0:T(8,128)(2,1)S(1)}, u32[]{:S(2)}, u32[]{:S(2)}) collective-permute-start(bf16[4,64,128]{2,1,0:T(8,128)(2,1)S(1)} %reduce_sum.38.part_ref), channel_id=1, source_target_pairs={{0,1},{1,0},{2,3},{3,2},{4,5},{5,4},{6,7},{7,6},{8,9},{9,8},{10,11... | collective-permute-start | bytes 196616 | tf_op jit(solution)/shard_map/ppermute | solution.py:563
  80.0 0.7 slice.15
  80.7 0.2 collective-permute-done.3.far_ref
  80.9 0.7 finish.1
  (9 shorter events, 0.2 us)
Async XLA Ops:
  1.4 9.3 %collective-permute-start.1 = (bf16[2,128,128]{2,1,0:T(8,128)(2,1)S(1)}, bf16[2,128,128]{2,1,0:T(8,128)(2,1)S(1)}, u32[]{:S(2)}, u32[]{:S(2)}) collective-permute-start(bf16[2,128,128]{2,1,0:T(8,128)(2,1)S(1)} %pack_block.1.now_ref), channel_id=1, source_target_pairs={{0,16},{8,24},{16,32},{24,40},{32,48},{40,56},{48,0},{56,8},{1,17}... | collective-permute-start | bytes 196616 | tf_op jit(solution)/shard_map/ppermute | solution.py:536
  5.3 7.5 %collective-permute-start = (bf16[2,128,128]{2,1,0:T(8,128)(2,1)S(1)}, bf16[2,128,128]{2,1,0:T(8,128)(2,1)S(1)}, u32[]{:S(2)}, u32[]{:S(2)}) collective-permute-start(bf16[2,128,128]{2,1,0:T(8,128)(2,1)S(1)} %pack_block.1.now_ref), channel_id=1, source_target_pairs={{0,8},{8,16},{16,24},{24,32},{32,40},{40,48},{48,56},{56,0},{1,9},... | collective-permute-start | bytes 196616 | tf_op jit(solution)/shard_map/ppermute | solution.py:537
  25.2 4.3 %collective-permute-start.2 = (bf16[4,2,2,128,128]{4,3,2,1,0:T(8,128)(2,1)S(1)}, bf16[4,2,2,128,128]{4,3,2,1,0:T(8,128)(2,1)S(1)}, u32[]{:S(2)}, u32[]{:S(2)}) collective-permute-start(bf16[4,2,2,128,128]{4,3,2,1,0:T(8,128)(2,1)S(1)} %all_to_all.20.a_ref), channel_id=1, source_target_pairs={{0,1},{1,0},{2,3},{3,2},{4,5},{5,4},{6,7},{7,6},{8,9},{9,8},{10,11... | collective-permute-start | bytes 1572872 | tf_op jit(solution)/shard_map/ppermute | solution.py:544
  76.4 4.5 %collective-permute-start.3 = (bf16[4,64,128]{2,1,0:T(8,128)(2,1)S(1)}, bf16[4,64,128]{2,1,0:T(8,128)(2,1)S(1)}, u32[]{:S(2)}, u32[]{:S(2)}) collective-permute-start(bf16[4,64,128]{2,1,0:T(8,128)(2,1)S(1)} %reduce_sum.38.part_ref), channel_id=1, source_target_pairs={{0,1},{1,0},{2,3},{3,2},{4,5},{5,4},{6,7},{7,6},{8,9},{9,8},{10,11... | collective-permute-start | bytes 196616 | tf_op jit(solution)/shard_map/ppermute | solution.py:563

commit v9 on v8

--- a/solution.py
+++ b/solution.py
@@ -233,13 +233,13 @@
 
 
 def fill_keys(key_scr, src, k_ref, ok_ref, first):
-    first_key = k_ref[0:1, :]
+    first_key = k_ref[0:16, :].astype(F32)[0:1, :]
     for i in range(CHUNKS // 2):
         for k in range(2):
             at = i * CHUNK + k * BLOCK
             one = ok_ref[2 * (first + i) + k : 2 * (first + i) + k + 1, :]
-            other = (1.0 - one).astype(BF16)
-            key_scr[at : at + BLOCK, :] = src[i, k, 0] * one.astype(BF16) + first_key * other
+            other = (first_key * (1.0 - one)).astype(BF16)
+            key_scr[at : at + BLOCK, :] = src[i, k, 0] * one.astype(BF16) + other
 
 
 def half_call(q, k, a, km, ok):

time: 82 us -> 81.9 us (level)
  no operation moved by 1% of the time
where the time goes in v9:
time: 81.9 us; the launch traced here: 81.6 us
  blocking collectives  53 us (65%)
  Pallas kernels  13.1 us (16%)
  starting transfers between devices  11.2 us (14%)
  waiting for transfers between devices  2.28 us (3%)
  local copies, waits for them, and re-layouts  1.1 us (1%)
    all_to_all x1, blocking collectives, on_device(): lax.all_to_all(jnp.concatenate([relay, part], axis=2), 'z', 0, 0, tiled=T...  18.3 us
    all_to_all x1, blocking collectives, on_device(): mine = lax.all_to_all(slots, 'y', 0, 0, tiled=True)  12.3 us
    all_to_all x1, blocking collectives, on_device(): got = lax.all_to_all(part, ('x', 'y'), 0, 0, tiled=True)  12 us
    all_to_all x1, blocking collectives, on_device(): got = lax.all_to_all(outgoing, ('y', 'c'), 0, 0, tiled=True)  10.5 us
    pallas_call x1, Pallas kernels, main_call(): pl.pallas_call(functools.partial(main_kernel, loss_scale), out_shape=(jax...  5.62 us
    ppermute x1, starting transfers between devices, on_device(): plane2 = lax.ppermute(plane0, 'z', shift2)  3.9 us
    pallas_call x1, Pallas kernels, local_call(): pl.pallas_call(local_kernel, out_shape=(jax.ShapeDtypeStruct((BLOCK, ROWS...  3.76 us
    ppermute x1, starting transfers between devices, on_device(): far = lax.ppermute(part, 'c', [(0, 1), (1, 0)])  3.59 us
  transfers between devices with their start and end apart: 4, of which 2 were waited for; matrix products, arithmetic and copies ran while one was open for 1% of the time, Pallas kernels for 7%

profile of v9, /device:TPU:1, one launch (start us, length us, event | category | flops | bytes accessed | tf_op | source)
XLA Modules:
  0.0 81.6 jit_solution(3354306286066864473)
XLA Ops:
  0.6 0.8 pack_block.1.now_ref
  1.4 3.9 %collective-permute-start.1 = (bf16[2,128,128]{2,1,0:T(8,128)(2,1)S(1)}, bf16[2,128,128]{2,1,0:T(8,128)(2,1)S(1)}, u32[]{:S(2)}, u32[]{:S(2)}) collective-permute-start(bf16[2,128,128]{2,1,0:T(8,128)(2,1)S(1)} %pack_block.1.now_ref), channel_id=1, source_target_pairs={{0,16},{8,24},{16,32},{24,40},{32,48},{40,56},{48,0},{56,8},{1,17}... | collective-permute-start | bytes 196616 | tf_op jit(solution)/shard_map/ppermute | solution.py:536
  5.3 1.6 %collective-permute-start = (bf16[2,128,128]{2,1,0:T(8,128)(2,1)S(1)}, bf16[2,128,128]{2,1,0:T(8,128)(2,1)S(1)}, u32[]{:S(2)}, u32[]{:S(2)}) collective-permute-start(bf16[2,128,128]{2,1,0:T(8,128)(2,1)S(1)} %pack_block.1.now_ref), channel_id=1, source_target_pairs={{0,8},{8,16},{16,24},{24,32},{32,40},{40,48},{48,56},{56,0},{1,9},... | collective-permute-start | bytes 196616 | tf_op jit(solution)/shard_map/ppermute | solution.py:537
  7.0 3.8 %local_block.1 = (f32[128,1024]{1,0:T(8,128)S(1)}, f32[1024,256]{1,0:T(8,128)S(1)}, f32[1024,128]{1,0:T(8,128)S(1)}, bf16[1024,256]{1,0:T(8,128)(2,1)S(1)}, f32[...) custom-call(bf16[128,1024]{1,0:T(8,128)(2,1)} %bitcast.29, ...), custom_call_target="tpu_custom_call" | custom-call | flops 400000000 | bytes 4000000 | tf_op jit(solution)/shard_map/local_block/pallas_call | solution.py:170
  10.7 0.0 collective-permute-done.1.back2_ref
  10.7 2.1 %collective-permute-done.back1_ref = bf16[2,128,128]{2,1,0:T(8,128)(2,1)S(1)} collective-permute-done((bf16[2,128,128]{2,1,0:T(8,128)(2,1)S(1)}, bf16[2,128,128]{2,1,0:T(8,128)(2,1)S(1)}, u32[]{:S(2)}, u32[]{:S(2)}) %collective-permute-start) | collective-permute-done | bytes 65568 | tf_op jit(solution)/shard_map/ppermute | solution.py:537
  12.9 0.1 fill_slots.1
  12.9 12.3 %all_to_all.20.a_ref = bf16[4,2,2,128,128]{4,3,2,1,0:T(8,128)(2,1)S(1)} all-to-all(bf16[4,2,2,128,128]{4,3,2,1,0:T(8,128)(2,1)S(1)} %fill_slots.1), channel_id=1, replica_groups=mesh['x'=4,'z'=8,'y'=4,'c'=2] {'y'}, dimensions={0} | all-to-all | bytes 1048576 | tf_op jit(solution)/shard_map/all_to_all | solution.py:543
  25.2 2.1 %collective-permute-start.2 = (bf16[4,2,2,128,128]{4,3,2,1,0:T(8,128)(2,1)S(1)}, bf16[4,2,2,128,128]{4,3,2,1,0:T(8,128)(2,1)S(1)}, u32[]{:S(2)}, u32[]{:S(2)}) collective-permute-start(bf16[4,2,2,128,128]{4,3,2,1,0:T(8,128)(2,1)S(1)} %all_to_all.20.a_ref), channel_id=1, source_target_pairs={{0,1},{1,0},{2,3},{3,2},{4,5},{5,4},{6,7},{7,6},{8,9},{9,8},{10,11... | collective-permute-start | bytes 1572872 | tf_op jit(solution)/shard_map/ppermute | solution.py:544
  27.4 2.2 %first_half.1 = (f32[1024,1024]{1,0:T(8,128)S(1)}, f32[1024,256]{1,0:T(8,128)S(1)}, f32[8,1024]{1,0:T(8,128)S(1)}) custom-call(bf16[128,1024]{1,0:T(8,128)(2,1)S(1)} %get-tuple-element.45.q_ref, bf16[128,128]{1,0:T(8,128)(2,1)S(1)} %get-tuple-element.46.k_ref, bf16[4,2,2,128,128]{4,3,2,1,0:T(8,128)(2,1)S(1)} %all_to_all.20.a_ref, ...), custom_call_target="tpu_custom_call" | custom-call | flops 400000000 | bytes 4000000 | tf_op jit(solution)/shard_map/first_half/pallas_call | solution.py:247
  29.5 0.0 collective-permute-done.2.b_ref
  29.5 5.6 %transfer.1 = (f32[128,1024]{1,0:T(8,128)}, bf16[8,16,1536]{2,1,0:T(8,128)(2,1)S(1)}) custom-call(bf16[128,1024]{1,0:T(8,128)(2,1)S(1)} %get-tuple-element.45.q_ref, bf16[128,128]{1,0:T(8,128)(2,1)S(1)} %get-tuple-element.46.k_ref, bf16[128,128]{1,0:T(8,128)(2,1)S(1)} %get-tuple-element.47.v_ref, bf16[4,2,2,128,128]{4,3,2,1,0:T(8,128)(2,1)S(1)} %all_to_all.20.a_ref, ...), custom_call_target="tpu_custom_call" | custom-call | flops 3000000000 | bytes 3000000 | tf_op jit(solution)/shard_map/transfer/pallas_call | solution.py:477
  35.1 10.5 %all_to_all.21 = bf16[8,16,1536]{2,1,0:T(8,128)(2,1)S(1)} all-to-all(bf16[8,16,1536]{2,1,0:T(8,128)(2,1)S(1)} %get-tuple-element.61), channel_id=1, replica_groups=mesh['x'=4,'z'=8,'y'=4,'c'=2] {'y','c'}, dimensions={0} | all-to-all | bytes 786432 | tf_op jit(solution)/shard_map/all_to_all | solution.py:551
  45.6 0.1 reshape.31
  45.7 0.1 copy.17
  45.9 0.1 copy.18
  46.0 18.3 %all_to_all.22 = bf16[8,16,1536]{2,1,0:T(8,128)(2,1)S(1)} all-to-all(bf16[8,16,1536]{2,1,0:T(8,128)(2,1)S(1)} %copy.18), channel_id=1, replica_groups=mesh['x'=4,'z'=8,'y'=4,'c'=2] {'z'}, dimensions={0} | all-to-all | bytes 786432 | tf_op jit(solution)/shard_map/all_to_all | solution.py:555
  64.4 12.0 %all_to_all.23 = bf16[16,64,128]{2,1,0:T(8,128)(2,1)S(1)} all-to-all(bf16[16,64,128]{2,1,0:T(8,128)(2,1)S(1)} %broadcast_in_dim.18), channel_id=1, replica_groups=mesh['x'=4,'z'=8,'y'=4,'c'=2] {'x','y'}, dimensions={0} | all-to-all | bytes 524288 | tf_op jit(solution)/shard_map/all_to_all | solution.py:560
  76.4 3.6 %collective-permute-start.3 = (bf16[4,64,128]{2,1,0:T(8,128)(2,1)S(1)}, bf16[4,64,128]{2,1,0:T(8,128)(2,1)S(1)}, u32[]{:S(2)}, u32[]{:S(2)}) collective-permute-start(bf16[4,64,128]{2,1,0:T(8,128)(2,1)S(1)} %reduce_sum.38.part_ref), channel_id=1, source_target_pairs={{0,1},{1,0},{2,3},{3,2},{4,5},{5,4},{6,7},{7,6},{8,9},{9,8},{10,11... | collective-permute-start | bytes 196616 | tf_op jit(solution)/shard_map/ppermute | solution.py:563
  80.0 0.7 slice.15
  80.7 0.2 collective-permute-done.3.far_ref
  80.9 0.7 finish.1
  (9 shorter events, 0.2 us)
Async XLA Ops:
  1.4 9.3 %collective-permute-start.1 = (bf16[2,128,128]{2,1,0:T(8,128)(2,1)S(1)}, bf16[2,128,128]{2,1,0:T(8,128)(2,1)S(1)}, u32[]{:S(2)}, u32[]{:S(2)}) collective-permute-start(bf16[2,128,128]{2,1,0:T(8,128)(2,1)S(1)} %pack_block.1.now_ref), channel_id=1, source_target_pairs={{0,16},{8,24},{16,32},{24,40},{32,48},{40,56},{48,0},{56,8},{1,17}... | collective-permute-start | bytes 196616 | tf_op jit(solution)/shard_map/ppermute | solution.py:536
  5.3 7.5 %collective-permute-start = (bf16[2,128,128]{2,1,0:T(8,128)(2,1)S(1)}, bf16[2,128,128]{2,1,0:T(8,128)(2,1)S(1)}, u32[]{:S(2)}, u32[]{:S(2)}) collective-permute-start(bf16[2,128,128]{2,1,0:T(8,128)(2,1)S(1)} %pack_block.1.now_ref), channel_id=1, source_target_pairs={{0,8},{8,16},{16,24},{24,32},{32,40},{40,48},{48,56},{56,0},{1,9},... | collective-permute-start | bytes 196616 | tf_op jit(solution)/shard_map/ppermute | solution.py:537
  25.2 4.3 %collective-permute-start.2 = (bf16[4,2,2,128,128]{4,3,2,1,0:T(8,128)(2,1)S(1)}, bf16[4,2,2,128,128]{4,3,2,1,0:T(8,128)(2,1)S(1)}, u32[]{:S(2)}, u32[]{:S(2)}) collective-permute-start(bf16[4,2,2,128,128]{4,3,2,1,0:T(8,128)(2,1)S(1)} %all_to_all.20.a_ref), channel_id=1, source_target_pairs={{0,1},{1,0},{2,3},{3,2},{4,5},{5,4},{6,7},{7,6},{8,9},{9,8},{10,11... | collective-permute-start | bytes 1572872 | tf_op jit(solution)/shard_map/ppermute | solution.py:544
  76.4 4.5 %collective-permute-start.3 = (bf16[4,64,128]{2,1,0:T(8,128)(2,1)S(1)}, bf16[4,64,128]{2,1,0:T(8,128)(2,1)S(1)}, u32[]{:S(2)}, u32[]{:S(2)}) collective-permute-start(bf16[4,64,128]{2,1,0:T(8,128)(2,1)S(1)} %reduce_sum.38.part_ref), channel_id=1, source_target_pairs={{0,1},{1,0},{2,3},{3,2},{4,5},{5,4},{6,7},{7,6},{8,9},{9,8},{10,11... | collective-permute-start | bytes 196616 | tf_op jit(solution)/shard_map/ppermute | solution.py:563
